TPU v7x, 32 devices: a whole 2x2x4 slice. The times are simulated.
32 devices in a mesh: space: 4 (over z), ens: 8 (over y, x, core).
Axes of the slice: x: 2, y: 2, z: 4, core: 2. Of those that a mesh axis runs over, the one named last changes fastest.
Arguments:
- log_perm: float32 [64, 8, 64, 512], P('ens', 'space'), may hold values from -4 to 4
- storage: float32 [8, 64, 512], P('space'), may hold values from 0.5 to 2
- head_init: float32 [8, 64, 512], P('space'), may hold values from -6 to 6
- well_cells: int32 [16], replicated, may hold values from 0 to 262143
- well_rates: float32 [16], replicated, may hold values from -12 to 12
- obs_cells: int32 [32], replicated, may hold values from 0 to 262143
- obs_values: float32 [32], replicated, may hold values from -6 to 6
- noise_var: float32 [32], replicated, may hold values from 0.05 to 0.5
- step_size: float32 [1], replicated, may hold values from 0.5 to 2
- perturb: float32 [64, 32], P('ens'), may hold values from -2 to 2
Outputs:
- head_field: float32 [64, 8, 64, 512], P('ens', 'space')
- updated: float32 [64, 8, 64, 512], P('ens', 'space')
All inputs are finite; a program needn't handle non-finite values.
Results may differ from a plain program's by a relative error of at most 0.00025.
Values sent between devices are 32-bit elements; how exact they have to be, the bound alone decides.
No kernel may reach another device: no remote copies, remote signals or barrier semaphores. Data moves between devices by JAX's collectives and lax.ppermute only.
A program may use at most 192 MiB of HBM per device.

v0:
```python
import jax
import jax.numpy as jnp
from jax import lax
from jax.sharding import PartitionSpec as P

SWEEPS = 3


OMEGA = 0.8
HIGHEST = lax.Precision.HIGHEST
DIRECTIONS = [
    (a, b, c) for a in (-1, 0, 1) for b in (-1, 0, 1) for c in (-1, 0, 1) if (a, b, c) != (0, 0, 0)
]


def padded_2(block, sides, width):
    for axis, dim in sides:
        count = lax.axis_size(axis)
        forward = [(i, i + 1) for i in range(count - 1)]
        backward = [(target, source) for source, target in forward]
        low = lax.ppermute(
            lax.slice_in_dim(block, block.shape[dim] - width, None, axis=dim), axis, forward
        )
        high = lax.ppermute(lax.slice_in_dim(block, 0, width, axis=dim), axis, backward)
        block = jnp.concatenate([low, block, high], axis=dim)
    return block


def shifted(padded, a, b, c, planes, depth, across):
    return padded[..., 1 + a : 1 + a + planes, 1 + b : 1 + b + depth, 1 + c : 1 + c + across]


def solve_pair(factor, residual):
    first = lax.linalg.triangular_solve(factor, residual.T, left_side=True, lower=True)
    second = lax.linalg.triangular_solve(
        factor, first, left_side=True, lower=True, transpose_a=True
    )
    return second.T


def shards(
    log_perm,
    storage,
    head_init,
    well_cells,
    well_rates,
    obs_cells,
    obs_values,
    noise_var,
    step_size,
    perturb,
):
    members, planes, depth, across = log_perm.shape
    cell_count = planes * depth * across
    total_members = members * lax.axis_size("ens")
    offset = lax.axis_index("space") * cell_count
    cell_ids = lax.broadcasted_iota(jnp.int32, (1, cell_count), 1)
    hits = (cell_ids == (well_cells - offset)[:, None]).astype(jnp.float32)
    source = jnp.dot(well_rates, hits, precision=HIGHEST).reshape(planes, depth, across)
    permeability = jnp.exp(log_perm)
    rimmed = padded_2(permeability, (("space", 1),), 1)
    padded = jnp.pad(rimmed, ((0, 0), (0, 0), (1, 1), (1, 1)))
    transmit = []
    for a, b, c in DIRECTIONS:
        factor = 2.0 ** (1 - abs(a) - abs(b) - abs(c))
        neighbour = shifted(padded, a, b, c, planes, depth, across)
        transmit.append(factor * 2.0 * permeability * neighbour / (permeability + neighbour))
    diagonal = storage + sum(transmit)
    forcing = storage * head_init + source
    head_field = jnp.broadcast_to(head_init, log_perm.shape)
    for sweep_index in range(SWEEPS):
        rimmed_head = padded_2(head_field, (("space", 1),), 1)
        padded_head = jnp.pad(rimmed_head, ((0, 0), (0, 0), (1, 1), (1, 1)))
        gathered = sum(
            (
                transmit[i] * shifted(padded_head, a, b, c, planes, depth, across)
                for i, (a, b, c) in enumerate(DIRECTIONS)
            )
        )
        head_field = (1.0 - OMEGA) * head_field + OMEGA * (forcing + gathered) / diagonal
    local_obs = obs_cells - offset
    inside = ((local_obs >= 0) & (local_obs < cell_count)).astype(jnp.float32)
    picked = (
        jnp.take(
            head_field.reshape(members, cell_count), jnp.clip(local_obs, 0, cell_count - 1), axis=1
        )
        * inside
    )
    observed = lax.psum(picked, "space")
    every_obs = lax.all_gather(observed, "ens", axis=0, tiled=True)
    mean_obs = jnp.mean(every_obs, axis=0)
    spread = every_obs - mean_obs
    covariance = jnp.dot(spread.T, spread, precision=HIGHEST) / (total_members - 1)
    deviation = observed - mean_obs
    system = covariance + jnp.diag(noise_var / step_size[0])
    factor_lower = jnp.linalg.cholesky(system)
    gain_rows = solve_pair(factor_lower, obs_values[None, :] + perturb - observed)
    flat = log_perm.reshape(members, cell_count)
    piece_field = lax.all_gather(flat, "ens", axis=0, tiled=True)
    piece_dev = lax.all_gather(deviation, "ens", axis=0, tiled=True)
    mixing = jnp.dot(piece_dev, gain_rows.T, precision=HIGHEST)
    change = lax.dot_general(mixing, piece_field, (((0,), (0,)), ((), ())), precision=HIGHEST)
    updated = (flat + change / (total_members - 1)).reshape(log_perm.shape)
    return (head_field, updated)


def solution(mesh):
    return jax.shard_map(
        shards,
        mesh=mesh,
        in_specs=(
            P("ens", "space", None, None),
            P("space", None, None),
            P("space", None, None),
            P(),
            P(),
            P(),
            P(),
            P(),
            P(),
            P("ens", None),
        ),
        out_specs=(P("ens", "space", None, None), P("ens", "space", None, None)),
        check_vma=False,
    )
```

profile of v0, /device:TPU:0, one launch (start us, length us, event | category | flops | bytes accessed | tf_op | source)
XLA Modules:
  0.0 291.6 jit_solution(8946189057640788096)
XLA Ops:
  10.8 5.1 %collective-permute-start = (f32[8,1,64,512]{3,2,1,0:T(8,128)}, f32[8,1,64,512]{3,2,1,0:T(8,128)S(1)}, u32[]{:S(2)}, u32[]{:S(2)}) collective-permute-start(f32[8,1,64,512]{3,2,1,0:T(8,128)} %get-tuple-element.14), channel_id=1, source_target_pairs={{0,8},{8,16},{16,24},{1,9},{9,17},{17,25},{2,10},{10,18},{18,26},{... | collective-permute-start | bytes 3145736 | tf_op jit(solution)/shard_map/ppermute | solution.py:21
  18.3 5.5 %collective-permute-start.2 = (f32[8,1,64,512]{3,2,1,0:T(8,128)}, f32[8,1,64,512]{3,2,1,0:T(8,128)}, u32[]{:S(2)}, u32[]{:S(2)}) collective-permute-start(f32[8,1,64,512]{3,2,1,0:T(8,128)} %broadcast_in_dim.53), channel_id=1, source_target_pairs={{0,8},{8,16},{16,24},{1,9},{9,17},{17,25},{2,10},{10,18},{18,26},{... | collective-permute-start | bytes 3145736 | tf_op jit(solution)/shard_map/ppermute | solution.py:21
  35.0 4.7 %collective-permute-done = f32[8,1,64,512]{3,2,1,0:T(8,128)S(1)} collective-permute-done((f32[8,1,64,512]{3,2,1,0:T(8,128)}, f32[8,1,64,512]{3,2,1,0:T(8,128)S(1)}, u32[]{:S(2)}, u32[]{:S(2)}) %collective-permute-start) | collective-permute-done | bytes 1048608 | tf_op jit(solution)/shard_map/ppermute | solution.py:21
  39.7 4.5 %collective-permute-done.1 = f32[8,1,64,512]{3,2,1,0:T(8,128)} collective-permute-done((f32[8,1,64,512]{3,2,1,0:T(8,128)}, f32[8,1,64,512]{3,2,1,0:T(8,128)}, u32[]{:S(2)}, u32[]{:S(2)}) %collective-permute-start.1) | collective-permute-done | bytes 1048608 | tf_op jit(solution)/shard_map/ppermute | solution.py:24
  44.2 3.7 %select_maximum_fusion.6 = f32[8,4,66,514]{3,2,1,0:T(8,128)S(1)} fusion(f32[8,1,64,512]{3,2,1,0:T(8,128)} %collective-permute-done.1, f32[8,2,64,512]{3,2,1,0:T(8,128)S(1)} %exp.3, f32[8,1,64,512]{3,2,1,0:T(8,128)S(1)} %collective-permute-done), kind=kLoop, calls=%fused_computation.13 | loop fusion | flops 16283520 | bytes 8536576 | tf_op jit(solution)/shard_map/concatenate | solution.py:25
  47.9 13.1 %collective-permute-done.2 = f32[8,1,64,512]{3,2,1,0:T(8,128)} collective-permute-done((f32[8,1,64,512]{3,2,1,0:T(8,128)}, f32[8,1,64,512]{3,2,1,0:T(8,128)}, u32[]{:S(2)}, u32[]{:S(2)}) %collective-permute-start.2) | collective-permute-done | bytes 1048608 | tf_op jit(solution)/shard_map/ppermute | solution.py:21
  61.0 4.2 %collective-permute-done.3 = f32[8,1,64,512]{3,2,1,0:T(8,128)} collective-permute-done((f32[8,1,64,512]{3,2,1,0:T(8,128)}, f32[8,1,64,512]{3,2,1,0:T(8,128)}, u32[]{:S(2)}, u32[]{:S(2)}) %collective-permute-start.3) | collective-permute-done | bytes 1048608 | tf_op jit(solution)/shard_map/ppermute | solution.py:24
  65.5 4.7 %select_maximum_fusion.4 = f32[8,4,66,514]{3,2,1,0:T(8,128)S(1)} fusion(f32[8,1,64,512]{3,2,1,0:T(8,128)} %collective-permute-done.3, f32[8,2,64,512]{3,2,1,0:T(8,128)S(1)} %broadcast_in_dim.54, f32[8,1,64,512]{3,2,1,0:T(8,128)} %collective-permute-done.2), kind=kLoop, calls=%fused_computation.11 | loop fusion | flops 16283520 | bytes 8536576 | tf_op jit(solution)/shard_map/concatenate | solution.py:25
  70.2 23.9 %fusion.71 = f32[8,2,64,512]{3,2,1,0:T(8,128)} fusion(f32[8,4,66,514]{3,2,1,0:T(8,128)S(1)} %select_maximum_fusion.4, f32[8,1,64,512]{3,2,1,0:T(8,128)} %collective-permute-done.3, f32[8,2,64,512]{3,2,1,0:T(8,128)} %copy-done.6, f32[8,1,64,512]{3,2,1,0:T(8,128)} %collective-permute-done.2, f32[2,64,512]{2,1,0:T(8,128)S(1)} %copy-done.8, ...), kind=kLoop, calls=%fused_computation.139 | loop fusion | flops 87031808 | bytes 114032640 | tf_op jit(solution)/shard_map/add | solution.py:80
  96.0 3.5 %collective-permute-start.4 = (f32[8,1,64,512]{3,2,1,0:T(8,128)S(1)}, f32[8,1,64,512]{3,2,1,0:T(8,128)S(1)}, u32[]{:S(2)}, u32[]{:S(2)}) collective-permute-start(f32[8,1,64,512]{3,2,1,0:T(8,128)S(1)} %get-tuple-element.12), channel_id=1, source_target_pairs={{0,8},{8,16},{16,24},{1,9},{9,17},{17,25},{2,10},{10,18},{18,26},{... | collective-permute-start | bytes 3145736 | tf_op jit(solution)/shard_map/ppermute | solution.py:21
  101.0 19.7 %collective-permute-done.4 = f32[8,1,64,512]{3,2,1,0:T(8,128)S(1)} collective-permute-done((f32[8,1,64,512]{3,2,1,0:T(8,128)S(1)}, f32[8,1,64,512]{3,2,1,0:T(8,128)S(1)}, u32[]{:S(2)}, u32[]{:S(2)}) %collective-permute-start.4) | collective-permute-done | bytes 1048608 | tf_op jit(solution)/shard_map/ppermute | solution.py:21
  120.7 4.2 %collective-permute-done.5 = f32[8,1,64,512]{3,2,1,0:T(8,128)S(1)} collective-permute-done((f32[8,1,64,512]{3,2,1,0:T(8,128)S(1)}, f32[8,1,64,512]{3,2,1,0:T(8,128)S(1)}, u32[]{:S(2)}, u32[]{:S(2)}) %collective-permute-start.5) | collective-permute-done | bytes 1048608 | tf_op jit(solution)/shard_map/ppermute | solution.py:24
  128.5 22.8 %fusion.40 = f32[8,2,64,512]{3,2,1,0:T(8,128)} fusion(f32[8,4,66,514]{3,2,1,0:T(8,128)S(1)} %select_maximum_fusion.2, f32[8,1,64,512]{3,2,1,0:T(8,128)} %copy-done.10, f32[8,2,64,512]{3,2,1,0:T(8,128)} %fusion.71, f32[8,1,64,512]{3,2,1,0:T(8,128)S(1)} %collective-permute-done.4, f32[2,64,512]{2,1,0:T(8,128)S(1)} %copy-done.8, ...), kind=kLoop, calls=%fused_computation.82 | loop fusion | flops 87556096 | bytes 113770496 | tf_op jit(solution)/shard_map/add | solution.py:80
  153.2 3.5 %collective-permute-start.6 = (f32[8,1,64,512]{3,2,1,0:T(8,128)S(1)}, f32[8,1,64,512]{3,2,1,0:T(8,128)S(1)}, u32[]{:S(2)}, u32[]{:S(2)}) collective-permute-start(f32[8,1,64,512]{3,2,1,0:T(8,128)S(1)} %get-tuple-element.10), channel_id=1, source_target_pairs={{0,8},{8,16},{16,24},{1,9},{9,17},{17,25},{2,10},{10,18},{18,26},{... | collective-permute-start | bytes 3145736 | tf_op jit(solution)/shard_map/ppermute | solution.py:21
  158.7 17.9 %collective-permute-done.6 = f32[8,1,64,512]{3,2,1,0:T(8,128)S(1)} collective-permute-done((f32[8,1,64,512]{3,2,1,0:T(8,128)S(1)}, f32[8,1,64,512]{3,2,1,0:T(8,128)S(1)}, u32[]{:S(2)}, u32[]{:S(2)}) %collective-permute-start.6) | collective-permute-done | bytes 1048608 | tf_op jit(solution)/shard_map/ppermute | solution.py:21
  176.6 4.2 %collective-permute-done.7 = f32[8,1,64,512]{3,2,1,0:T(8,128)S(1)} collective-permute-done((f32[8,1,64,512]{3,2,1,0:T(8,128)S(1)}, f32[8,1,64,512]{3,2,1,0:T(8,128)S(1)}, u32[]{:S(2)}, u32[]{:S(2)}) %collective-permute-start.7) | collective-permute-done | bytes 1048608 | tf_op jit(solution)/shard_map/ppermute | solution.py:24
  184.4 22.8 %fusion.9 = f32[8,2,64,512]{3,2,1,0:T(8,128)} fusion(f32[8,4,66,514]{3,2,1,0:T(8,128)S(1)} %select_maximum_fusion, f32[8,1,64,512]{3,2,1,0:T(8,128)} %copy-done.9, f32[8,2,64,512]{3,2,1,0:T(8,128)} %fusion.40, f32[8,1,64,512]{3,2,1,0:T(8,128)S(1)} %collective-permute-done.6, f32[2,64,512]{2,1,0:T(8,128)S(1)} %copy-done.8, ...), kind=kLoop, calls=%fused_computation.25 | loop fusion | flops 87556096 | bytes 113770496 | tf_op jit(solution)/shard_map/add | solution.py:80
  207.2 18.0 %copy.24 = f32[8,2,64,512]{0,3,2,1:T(8,128)} copy(f32[8,2,64,512]{3,2,1,0:T(8,128)} %fusion.9) | data formatting | bytes 4194304 | tf_op jit(solution)/shard_map/add | solution.py:80
  225.2 11.1 %gather_fusion = f32[32,8]{1,0:T(8,128)S(1)} fusion(f32[8,65536]{0,1:T(8,128)} %bitcast.36, s32[1024]{0:T(1024)S(1)} %pad_clamp_fusion), kind=kCustom, calls=%fused_computation | custom fusion | bytes 2176 | tf_op jit(solution)/shard_map/jit(_take)/gather | solution.py:84
  236.4 8.9 %psum.7 = f32[8,32]{1,0:T(8,128)S(1)} all-reduce(f32[8,32]{1,0:T(8,128)S(1)} %multiply_bitcast_fusion), channel_id=1, replica_groups=mesh['space'=4,'ens'=8] {'space'}, use_global_device_ids=true, to_apply=%region_0.1 | all-reduce | flops 256 | bytes 2048 | tf_op jit(solution)/shard_map/psum | solution.py:89
  245.3 9.1 %all_gather.9 = f32[64,32]{1,0:T(8,128)S(1)} all-gather(f32[8,32]{1,0:T(8,128)S(1)} %psum.7), channel_id=1, replica_groups=mesh['space'=4,'ens'=8] {'ens'}, dimensions={0}, use_global_device_ids=true | all-gather | bytes 9216 | tf_op jit(solution)/shard_map/all_gather | solution.py:90
  254.8 2.9 %cholesky.16 = f32[32,32]{1,0:T(8,128)S(1)} custom-call(f32[32,32]{1,0:T(8,128)S(1)} %fusion.112), custom_call_target="Cholesky" | custom-call | tf_op jit(solution)/shard_map/jit(cholesky)/cholesky | solution.py:96
  261.5 9.3 %all_gather.10 = f32[64,32]{1,0:T(8,128)S(1)} all-gather(f32[8,32]{1,0:T(8,128)S(1)} %broadcast_subtract_fusion), channel_id=1, replica_groups=mesh['space'=4,'ens'=8] {'ens'}, dimensions={0}, use_global_device_ids=true | all-gather | bytes 9216 | tf_op jit(solution)/shard_map/all_gather | solution.py:100
  271.2 11.0 %fusion = f32[8,65536]{1,0:T(8,128)S(1)} fusion(f32[8,65536]{1,0:T(8,128)S(1)} %bitcast.38, f32[64,8]{0,1:T(8,128)S(1)} %fusion.121, f32[64,65536]{1,0:T(8,128)} %all-gather.2.cloned.1.call-done), kind=kOutput, calls=%fused_computation.2 | convolution fusion | flops 403701760 | bytes 20973568 | tf_op jit(solution)/shard_map/dot_general | solution.py:102
  (77 shorter events, 38.5 us)
Async XLA Ops:
  7.2 22.3 %copy-start = (f32[16]{0:T(128)S(1)}, f32[16]{0:T(128)}, u32[]{:S(2)}) copy-start(f32[16]{0:T(128)} %param.14) | copy-start | bytes 196
  7.2 264.1 %all-gather.2.cloned.1.call-start = ((), (), s32[]{:S(2)}) async-start(), calls=%async_computation | async-start | bytes 18874368 | tf_op jit(solution)/shard_map/all_gather | solution.py:99
  9.2 8.0 %copy-start.11 = (f32[2,64,512]{2,1,0:T(8,128)S(1)}, f32[2,64,512]{2,1,0:T(8,128)}, u32[]{:S(2)}) copy-start(f32[2,64,512]{2,1,0:T(8,128)} %param.12) | copy-start | bytes 786436
  10.8 15.5 %copy-start.2 = (f32[8,2,64,512]{3,2,1,0:T(8,128)S(1)}, f32[8,2,64,512]{3,2,1,0:T(8,128)}, u32[]{:S(2)}) copy-start(f32[8,2,64,512]{3,2,1,0:T(8,128)} %param.10) | copy-start | bytes 6291460
  10.8 28.9 %collective-permute-start = (f32[8,1,64,512]{3,2,1,0:T(8,128)}, f32[8,1,64,512]{3,2,1,0:T(8,128)S(1)}, u32[]{:S(2)}, u32[]{:S(2)}) collective-permute-start(f32[8,1,64,512]{3,2,1,0:T(8,128)} %get-tuple-element.14), channel_id=1, source_target_pairs={{0,8},{8,16},{16,24},{1,9},{9,17},{17,25},{2,10},{10,18},{18,26},{... | collective-permute-start | bytes 3145736 | tf_op jit(solution)/shard_map/ppermute | solution.py:21
  15.9 28.3 %collective-permute-start.1 = (f32[8,1,64,512]{3,2,1,0:T(8,128)}, f32[8,1,64,512]{3,2,1,0:T(8,128)}, u32[]{:S(2)}, u32[]{:S(2)}) collective-permute-start(f32[8,1,64,512]{3,2,1,0:T(8,128)} %get-tuple-element.15), channel_id=1, source_target_pairs={{8,0},{16,8},{24,16},{9,1},{17,9},{25,17},{10,2},{18,10},{26,18},{... | collective-permute-start | bytes 3145736 | tf_op jit(solution)/shard_map/ppermute | solution.py:24
  18.3 42.7 %collective-permute-start.2 = (f32[8,1,64,512]{3,2,1,0:T(8,128)}, f32[8,1,64,512]{3,2,1,0:T(8,128)}, u32[]{:S(2)}, u32[]{:S(2)}) collective-permute-start(f32[8,1,64,512]{3,2,1,0:T(8,128)} %broadcast_in_dim.53), channel_id=1, source_target_pairs={{0,8},{8,16},{16,24},{1,9},{9,17},{17,25},{2,10},{10,18},{18,26},{... | collective-permute-start | bytes 3145736 | tf_op jit(solution)/shard_map/ppermute | solution.py:21
  25.0 40.2 %collective-permute-start.3 = (f32[8,1,64,512]{3,2,1,0:T(8,128)}, f32[8,1,64,512]{3,2,1,0:T(8,128)}, u32[]{:S(2)}, u32[]{:S(2)}) collective-permute-start(f32[8,1,64,512]{3,2,1,0:T(8,128)} %broadcast_in_dim.55), channel_id=1, source_target_pairs={{8,0},{16,8},{24,16},{9,1},{17,9},{25,17},{10,2},{18,10},{26,18},{... | collective-permute-start | bytes 3145736 | tf_op jit(solution)/shard_map/ppermute | solution.py:24
  28.8 4.5 %copy-start.8 = (f32[2,64,512]{2,1,0:T(8,128)S(1)}, f32[2,64,512]{2,1,0:T(8,128)}, u32[]{:S(2)}) copy-start(f32[2,64,512]{2,1,0:T(8,128)} %param.11) | copy-start | bytes 786436
  35.0 30.2 %copy-start.12 = (f32[2,64,512]{2,1,0:T(8,128)S(1)}, f32[2,64,512]{2,1,0:T(8,128)}, u32[]{:S(2)}) copy-start(f32[2,64,512]{2,1,0:T(8,128)} %param.12) | copy-start | bytes 786436
  65.5 4.7 %copy-start.6 = (f32[8,2,64,512]{3,2,1,0:T(8,128)}, f32[8,2,64,512]{3,2,1,0:T(8,128)S(1)}, u32[]{:S(2)}) copy-start(f32[8,2,64,512]{3,2,1,0:T(8,128)S(1)} %broadcast_in_dim.54) | copy-start | bytes 6291460
  65.5 4.7 %copy-start.3 = (f32[8,2,64,512]{3,2,1,0:T(8,128)S(1)}, f32[8,2,64,512]{3,2,1,0:T(8,128)}, u32[]{:S(2)}) copy-start(f32[8,2,64,512]{3,2,1,0:T(8,128)} %param.10) | copy-start | bytes 6291460
  94.1 31.7 %copy-start.5 = (f32[8,2,64,512]{3,2,1,0:T(8,128)S(1)}, f32[8,2,64,512]{3,2,1,0:T(8,128)}, u32[]{:S(2)}) copy-start(f32[8,2,64,512]{3,2,1,0:T(8,128)} %fusion.71) | copy-start | bytes 6291460
  96.0 24.6 %collective-permute-start.4 = (f32[8,1,64,512]{3,2,1,0:T(8,128)S(1)}, f32[8,1,64,512]{3,2,1,0:T(8,128)S(1)}, u32[]{:S(2)}, u32[]{:S(2)}) collective-permute-start(f32[8,1,64,512]{3,2,1,0:T(8,128)S(1)} %get-tuple-element.12), channel_id=1, source_target_pairs={{0,8},{8,16},{16,24},{1,9},{9,17},{17,25},{2,10},{10,18},{18,26},{... | collective-permute-start | bytes 3145736 | tf_op jit(solution)/shard_map/ppermute | solution.py:21
  99.5 25.3 %collective-permute-start.5 = (f32[8,1,64,512]{3,2,1,0:T(8,128)S(1)}, f32[8,1,64,512]{3,2,1,0:T(8,128)S(1)}, u32[]{:S(2)}, u32[]{:S(2)}) collective-permute-start(f32[8,1,64,512]{3,2,1,0:T(8,128)S(1)} %get-tuple-element.13), channel_id=1, source_target_pairs={{8,0},{16,8},{24,16},{9,1},{17,9},{25,17},{10,2},{18,10},{26,18},{... | collective-permute-start | bytes 3145736 | tf_op jit(solution)/shard_map/ppermute | solution.py:24
  151.3 7.4 %copy-start.15 = (s32[32]{0:T(128)S(1)}, s32[32]{0:T(128)}, u32[]{:S(2)}) copy-start(s32[32]{0:T(128)} %param.15) | copy-start | bytes 388
  151.3 7.4 %copy-start.17 = (f32[32]{0:T(128)S(1)}, f32[32]{0:T(128)}, u32[]{:S(2)}) copy-start(f32[32]{0:T(128)} %param.17) | copy-start | bytes 388
  151.3 30.5 %copy-start.4 = (f32[8,2,64,512]{3,2,1,0:T(8,128)S(1)}, f32[8,2,64,512]{3,2,1,0:T(8,128)}, u32[]{:S(2)}) copy-start(f32[8,2,64,512]{3,2,1,0:T(8,128)} %fusion.40) | copy-start | bytes 6291460
  153.2 23.4 %collective-permute-start.6 = (f32[8,1,64,512]{3,2,1,0:T(8,128)S(1)}, f32[8,1,64,512]{3,2,1,0:T(8,128)S(1)}, u32[]{:S(2)}, u32[]{:S(2)}) collective-permute-start(f32[8,1,64,512]{3,2,1,0:T(8,128)S(1)} %get-tuple-element.10), channel_id=1, source_target_pairs={{0,8},{8,16},{16,24},{1,9},{9,17},{17,25},{2,10},{10,18},{18,26},{... | collective-permute-start | bytes 3145736 | tf_op jit(solution)/shard_map/ppermute | solution.py:21
  156.7 24.1 %collective-permute-start.7 = (f32[8,1,64,512]{3,2,1,0:T(8,128)S(1)}, f32[8,1,64,512]{3,2,1,0:T(8,128)S(1)}, u32[]{:S(2)}, u32[]{:S(2)}) collective-permute-start(f32[8,1,64,512]{3,2,1,0:T(8,128)S(1)} %get-tuple-element.11), channel_id=1, source_target_pairs={{8,0},{16,8},{24,16},{9,1},{17,9},{25,17},{10,2},{18,10},{26,18},{... | collective-permute-start | bytes 3145736 | tf_op jit(solution)/shard_map/ppermute | solution.py:24
  207.2 63.6 %copy-start.13 = (f32[8,32]{1,0:T(8,128)S(1)}, f32[8,32]{1,0:T(8,128)}, u32[]{:S(2)}) copy-start(f32[8,32]{1,0:T(8,128)} %param.19) | copy-start | bytes 3076
  207.2 63.6 %copy-start.14 = (f32[32]{0:T(128)S(1)}, f32[32]{0:T(128)}, u32[]{:S(2)}) copy-start(f32[32]{0:T(128)} %param.16) | copy-start | bytes 388
  207.2 64.0 %copy-start.7 = (f32[1,8,128,512]{3,1,2,0:T(8,128)S(1)}, f32[1,8,128,512]{3,1,2,0:T(8,128)}, u32[]{:S(2)}) copy-start(f32[1,8,128,512]{3,1,2,0:T(8,128)} %copy.30) | copy-start | bytes 6291460
  282.2 2.6 copy-start.1
  (3 other events, 2.6 us)
Sparse Core Ops, SparseCore 0:
  28.9 93.0 all-gather.1
where the time goes:
time: 293 us; the launch traced here: 292 us
  other arithmetic  91.8 us (31%)
  waiting for transfers between devices  72.4 us (25%)
  local copies, waits for them, and re-layouts  48.4 us (17%)
  blocking collectives  27.2 us (9%)
  starting transfers between devices  23 us (8%)
  between operations  15 us (5%)
  matrix products  13.7 us (5%)
    add x3, other arithmetic, shards(): (1.0 - OMEGA) * head_field + OMEGA * (forcing + gathered) / diagonal  69.5 us
    ppermute x4, waiting for transfers between devices, padded_2(): lax.ppermute(lax.slice_in_dim(block, block.shape[dim] - width, None, axis...  55.4 us
    add x1, local copies, waits for them, and re-layouts, shards(): (1.0 - OMEGA) * head_field + OMEGA * (forcing + gathered) / diagonal  18 us
    ppermute x4, starting transfers between devices, padded_2(): lax.ppermute(lax.slice_in_dim(block, block.shape[dim] - width, None, axis...  17.6 us
    ppermute x4, waiting for transfers between devices, padded_2(): lax.ppermute(lax.slice_in_dim(block, 0, width, axis=dim), axis, backward)  17 us
    concatenate x4, other arithmetic, padded_2(): block = jnp.concatenate([low, block, high], axis=dim)  13.7 us
    gather x2, local copies, waits for them, and re-layouts, shards(): jnp.take(head_field.reshape(members, cell_count), jnp.clip(local_obs, 0,...  11.2 us
    dot_general x1, matrix products, shards(): lax.dot_general(mixing, piece_field, (((0,), (0,)), ((), ())), precision=...  11 us
  transfers between devices with their start and end apart: 9, of which 8 were waited for; matrix products, arithmetic and copies ran while one was open for 46% of the time, Pallas kernels for 0%

commit v1 on v0

v1 whole, which is shorter than its diff:
```python
import functools

import jax
import jax.numpy as jnp
from jax import lax
from jax.experimental import pallas as pl
from jax.experimental.pallas import tpu as pltpu
from jax.sharding import PartitionSpec as P

OMEGA = 0.8
HIGHEST = lax.Precision.HIGHEST
F32 = jnp.float32
MIB = 1 << 20
VMEM = pl.BlockSpec(memory_space=pltpu.VMEM)
SMEM = pl.BlockSpec(memory_space=pltpu.SMEM)
ANY = pl.BlockSpec(memory_space=pl.ANY)
REACH = 3
DEEP = 3
MICROSECOND = 3.0e6
EXPECTED = dict(planes=4, gather=5, sweep=13, local_heads=5, solve=5, mix=4, update=4)
SLOT = 8
SIDE = 2 * REACH + 1


def spot():
    slab = lax.axis_index("space")
    return lax.rem(slab, 2), lax.axis_index("ens"), slab


def recip(x):
    return pltpu.reciprocal(x, approx=True)


def call(kernel, name, out_shape, in_specs, out_specs, scratch=(), after=(), alias={}):
    tokens = len(after)

    def entry(*refs):
        kernel(*refs[tokens:])

    run = pl.pallas_call(
        entry,
        name=name,
        out_shape=out_shape,
        in_specs=[ANY] * tokens + list(in_specs),
        out_specs=out_specs,
        scratch_shapes=list(scratch),
        input_output_aliases={k + tokens: v for k, v in alias.items()},
        compiler_params=pltpu.CompilerParams(vmem_limit_bytes=64 * MIB),
        cost_estimate=pl.CostEstimate(
            flops=0, bytes_accessed=int(EXPECTED[name] * MICROSECOND), transcendentals=0
        ),
    )
    return functools.partial(run, *after)


def row_spans(depth, cut):
    return [(0, depth)] if cut is None else [(0, cut), (cut, depth)]


def planes_kernel(step, cut, lp, head, *refs):
    members, planes, depth, across = lp.shape
    spans = row_spans(depth, cut)
    parts = len(spans)
    sides = (refs[:parts], refs[parts : 2 * parts])
    own, raw, turned, perm, sem_in, sem_out = refs[2 * parts :]
    count = depth // step
    lines = depth // 8
    ins = []
    for b in range(count):
        rows = pl.ds(b * step, step)
        ins.append(
            pltpu.make_async_copy(lp.at[:, :, rows, :], raw.at[:, :, rows, :], sem_in.at[b])
        )
        ins[-1].start()
    odd, _, _ = spot()
    outs = []

    def send(src, dst):
        copy = pltpu.make_async_copy(src, dst, sem_out.at[len(outs)])
        copy.start()
        outs.append(copy)

    for i in range(planes):
        for k in range(lines):
            perm[i, depth + k] = head[i, pl.ds(8 * k, 8), :]
    plane = (1 - odd, odd)
    for s in range(2):
        send(
            perm.at[plane[s], pl.ds(depth, lines)],
            sides[s][0].at[pl.ds(spans[0][1], lines)],
        )
    sent = 0
    for b in range(count):
        ins[b].wait()

        def turn(k, carry):
            some = pl.ds(pl.multiple_of(b * step + 8 * k, 8), 8)
            for i in range(planes):
                x = jnp.swapaxes(raw[:, i, some, :], 0, 1)
                turned[i, some] = x
                perm[i, some] = jnp.exp(x)
            return carry

        lax.fori_loop(0, step // 8, turn, 0)
        rows = pl.ds(b * step, step)
        send(turned.at[:, rows], own.at[:, rows])
        while sent < parts and spans[sent][1] <= (b + 1) * step:
            lo, hi = spans[sent]
            for s in range(2):
                send(perm.at[plane[s], pl.ds(lo, hi - lo)], sides[s][sent].at[pl.ds(0, hi - lo)])
            sent += 1
    for copy in outs:
        copy.wait()


def planes_of(lp, head, cut, after=()):
    members, planes, depth, across = lp.shape
    step = 16
    lines = depth // 8
    spans = row_spans(depth, cut)
    sides = [
        jax.ShapeDtypeStruct((hi - lo + (lines if lo == 0 else 0), members, across), F32)
        for lo, hi in spans
    ]
    turned = (planes, depth, members, across)
    out = call(
        functools.partial(planes_kernel, step, cut),
        "planes",
        sides * 2 + [jax.ShapeDtypeStruct(turned, F32)],
        [ANY, VMEM],
        [ANY] * (2 * len(spans) + 1),
        [
            pltpu.VMEM(lp.shape, F32),
            pltpu.VMEM(turned, F32),
            pltpu.VMEM((planes, depth + lines, members, across), F32),
            pltpu.SemaphoreType.DMA((depth // step,)),
            pltpu.SemaphoreType.DMA((2 * len(spans) + depth // step + 2,)),
        ],
        after=after,
    )(lp, head)
    parts = len(spans)
    return out[:parts], out[parts : 2 * parts], out[2 * parts]


def sweep_kernel(cfg, *refs):
    first, last, za, zb, depth, members, across, pieces = cfg
    refs = list(refs)
    odd, _, _ = spot()
    lines = {"f": refs.pop(0)}
    if first:
        lines["s"] = refs.pop(0)
        lines["d"] = refs.pop(0)
    named = {}
    for key, spans in pieces:
        named[key] = [(refs.pop(0), lo, hi) for lo, hi in spans]
    if last:
        refs.pop(0)
        natural = refs.pop(0)
    else:
        outs = [refs.pop(0), refs.pop(0)]
        w_out = refs.pop(0) if first else None
    R, RP, H, HP, S, A, O, W, forcing = refs[:9]
    refs = refs[9:]
    dests = {"p": R, "h": H, "f": forcing}
    if first:
        DS, DA, HH, storage, head = refs[:5]
        refs = refs[5:]
        dests.update({"s": storage, "d": head})
    if last:
        NAT = refs.pop(0)
    sem_in, sem_out = refs
    zlo = max(za - 1, 0)
    zhi = min(zb, depth - 1)
    own = (1, 2)
    tiles = across // 128
    slots = {"a": 2 - odd, "b": 1 + odd, "ra": 3 - 3 * odd, "rb": 3 * odd}

    ends = []
    at = zlo
    for width in (4, 8, 12, 12, 12, 12, 12):
        if at >= zhi + 1:
            break
        ends.append(min(at + width, zhi + 1))
        at = ends[-1]
    if len(ends) > 1 and ends[-1] - ends[-2] < 4:
        ends.pop(-2)
    groups = []
    used = 0

    def copy_in(batch, src, dst):
        batch.append(pltpu.make_async_copy(src, dst, sem_in.at[len(batch) + used]))

    start = zlo
    for end in ends:
        batch = []
        for (kind, name), spans in named.items():
            low_row = za if kind == "w" else zlo
            high_row = zb if kind == "w" else zhi + 1
            for ref, lo, hi in spans:
                s, e = max(start, lo, low_row), min(end, hi, high_row)
                if s < e:
                    src, dst = pl.ds(s - lo, e - s), pl.ds(s - low_row, e - s)
                    if kind == "w":
                        copy_in(batch, ref.at[:, src], W.at[:, dst])
                    else:
                        copy_in(batch, ref.at[src], dests[kind].at[slots[name], dst])
        if start == zlo:
            for kind, ref in lines.items():
                copy_in(batch, ref, dests[kind])
            if first:
                for q, name in enumerate(("ra", "rb")):
                    ref, lo, hi = named["p", name][0]
                    some = pl.ds(hi - lo, depth // 8)
                    copy_in(batch, ref.at[some], HH.at[odd if q == 1 else 1 - odd])
        groups.append(batch)
        used += len(batch)
        start = end
    for batch in groups[:DEEP]:
        for copy in batch:
            copy.start()

    lane = lax.broadcasted_iota(jnp.int32, (members, 128), 1)
    final_lane = lane == 127
    first_lane = lane == 0

    def ahead(parts, beyond):
        turned = [pltpu.roll(x, 127, 1) for x in parts]
        out = [jnp.where(final_lane, turned[t + 1], turned[t]) for t in range(tiles - 1)]
        last_part = turned[-1]
        if beyond is not None:
            last_part = jnp.where(final_lane, beyond, last_part)
        return out + [last_part]

    def behind(parts):
        turned = [pltpu.roll(x, 1, 1) for x in parts]
        out = [jnp.where(first_lane, 0.0, turned[0])]
        return out + [jnp.where(first_lane, turned[t - 1], turned[t]) for t in range(1, tiles)]

    tile = [pl.ds(t * 128, 128) for t in range(tiles)]

    def load_row(z, chosen=range(4)):
        q = z - zlo
        for i in chosen:
            r = [recip(R[i, q, :, ys]) for ys in tile]
            rp = ahead(r, jnp.inf)
            for t, ys in enumerate(tile):
                R[i, q, :, ys] = r[t]
                RP[i, q, :, ys] = rp[t]
            if first:
                if i in own:
                    row = head[i - 1, pl.ds(z, 1), :]
                else:
                    row = HH[i // 3, z // 8, pl.ds(lax.rem(z, 8), 1), :]
                row = jnp.broadcast_to(row, (members, across))
                h = [row[:, t * 128 : (t + 1) * 128] for t in range(tiles)]
            else:
                h = [H[i, q, :, ys] for ys in tile]
            hp = ahead(h, None)
            for t, ys in enumerate(tile):
                if first:
                    H[i, q, :, ys] = h[t]
                HP[i, q, :, ys] = hp[t]

    def process(z, emit=True, inner=True, load=False):
        c = z - zlo
        both = (c, c + 1) if inner else (c,)
        done = {}
        for t, ys in enumerate(tile):

            def get(ref):
                return [[ref[i, q, :, ys] for q in both] for i in range(4)]

            r, rp, h, hp = get(R), get(RP), get(H), get(HP)
            total = {}
            for k, i in enumerate(own):
                total["s", i, 0] = S[k, :, ys]
                total["a", i, 0] = A[k, :, ys]
                if first:
                    total["ds", i, 0] = DS[k, :, ys]
                    total["da", i, 0] = DA[k, :, ys]

            def add(key, value):
                total[key] = total[key] + value if key in total else value

            def pair(scale, i, q, j, p, ahead):
                x = r[i][q] + (rp[j][p] if ahead else r[j][p])
                u = recip(x if scale == 1.0 else x * scale)
                if i in own:
                    add(("s", i, q), u * (hp[j][p] if ahead else h[j][p]))
                    if first:
                        add(("ds", i, q), u)
                if j in own:
                    add(("a" if ahead else "s", j, p), u * h[i][q])
                    if first:
                        add(("da" if ahead else "ds", j, p), u)

            w1, w2, w3 = 0.5, 1.0, 2.0
            sides = ((0, 1), (1, 2), (2, 3))
            for i in own:
                pair(w1, i, 0, i, 0, True)
            for i, j in sides:
                pair(w1, i, 0, j, 0, False)
                pair(w2, i, 0, j, 0, True)
                pair(w2, j, 0, i, 0, True)
            if inner:
                for i in own:
                    pair(w1, i, 0, i, 1, False)
                    pair(w2, i, 0, i, 1, True)
                    pair(w2, i, 1, i, 0, True)
                for i, j in sides:
                    pair(w2, i, 0, j, 1, False)
                    pair(w2, i, 1, j, 0, False)
                    pair(w3, i, 0, j, 1, True)
                    pair(w3, i, 1, j, 0, True)
                    pair(w3, j, 0, i, 1, True)
                    pair(w3, j, 1, i, 0, True)
                for k, i in enumerate(own):
                    S[k, :, ys] = total["s", i, 1]
                    A[k, :, ys] = total["a", i, 1]
                    if first:
                        DS[k, :, ys] = total["ds", i, 1]
                        DA[k, :, ys] = total["da", i, 1]
            for key, value in total.items():
                if key[2] == 0:
                    done.setdefault(key[:2], []).append(value)
            if load:
                load_row(z + 2, range(t * 4 // tiles, (t + 1) * 4 // tiles))
        if not emit:
            return
        o = z - za
        for k, i in enumerate(own):
            moved = behind(done["a", i])
            source = forcing[k, pl.ds(z, 1), :]
            if first:
                store = storage[k, pl.ds(z, 1), :]
            if first:
                da = behind(done["da", i])
            for t, ys in enumerate(tile):
                cut = slice(t * 128, (t + 1) * 128)
                gathered = done["s", i][t] + moved[t]
                if first:
                    diagonal = store[:, cut] + (done["ds", i][t] + da[t])
                    w = OMEGA * recip(diagonal)
                    W[k, o, :, ys] = w
                else:
                    w = W[k, o, :, ys]
                old = H[i, c, :, ys]
                O[k, o, :, ys] = (1.0 - OMEGA) * old + w * (source[:, cut] + gathered)

    results = []

    def start_out(src, dst):
        copy = pltpu.make_async_copy(src, dst, sem_out.at[len(results)])
        copy.start()
        results.append(copy)

    progress = [za]

    def flush(upto):
        if last:
            upto = upto // 8 * 8
        begin = progress[0]
        if upto <= begin:
            return
        progress[0] = upto
        rows = pl.ds(begin - za, upto - begin)
        if last:

            def turn(b, carry):
                some = pl.ds(pl.multiple_of(b * 8, 8), 8)
                for k in range(2):
                    NAT[:, k, some, :] = jnp.swapaxes(O[k, some], 0, 1)
                return carry

            lax.fori_loop((begin - za) // 8, (upto - za) // 8, turn, 0)
            start_out(
                NAT.at[:, :, rows, :], natural.at[:, :, pl.ds(begin, upto - begin), :]
            )
            return
        start_out(O.at[1 - odd, rows], outs[0].at[rows])
        start_out(O.at[odd, rows], outs[1].at[rows])
        if first:
            start_out(W.at[:, rows], w_out.at[:, rows])

    S[...] = jnp.zeros_like(S)
    A[...] = jnp.zeros_like(A)
    if first:
        DS[...] = jnp.zeros_like(DS)
        DA[...] = jnp.zeros_like(DA)
    at = zlo
    for g, end in enumerate(ends):
        for copy in groups[g]:
            copy.wait()
        if g + DEEP < len(groups):
            for copy in groups[g + DEEP]:
                copy.start()
        if g == 0:
            load_row(zlo)
            load_row(zlo + 1)
            if zlo < za:
                load_row(zlo + 2)
                process(zlo, emit=False)
                at = za

        def body(z, carry):
            process(z, load=True)
            return carry

        lax.fori_loop(at, end - 2, body, 0, unroll=2)
        at = end - 2
        flush(at)
    process(zhi - 1)
    if zb == depth:
        process(zhi, inner=False)
    flush(zb)
    for copy in results:
        copy.wait()


def sweep_of(first, last, za, zb, shape, lines, fields, into=None, after=()):
    members, planes, depth, across = shape
    zlo = max(za - 1, 0)
    zhi = min(zb, depth - 1)
    rows = zb - za
    pieces = tuple((key, tuple((lo, hi) for _, lo, hi in spans)) for key, spans in fields.items())
    operands = list(lines)
    for spans in fields.values():
        operands += [ref for ref, _, _ in spans]
    copies = sum(len(spans) for spans in fields.values()) * 7 + 8
    field = pltpu.VMEM((4, zhi + 1 - zlo, members, across), F32)
    line = pltpu.VMEM((2, members, across), F32)
    flat = pltpu.VMEM((2, depth, across), F32)
    both = pltpu.VMEM((2, rows, members, across), F32)
    scratch = [field] * 4 + [line] * 2 + [both] * 2 + [flat]
    if first:
        scratch += [line] * 2 + [pltpu.VMEM((2, depth // 8, 8, across), F32)] + [flat] * 2
    alias = {}
    if last:
        scratch += [pltpu.VMEM((members, 2, rows, across), F32)]
        out_shape = [jax.ShapeDtypeStruct(shape, F32)]
        operands.append(lines[0] if into is None else into)
        if into is not None:
            alias = {len(operands) - 1: 0}
    else:
        out_shape = [jax.ShapeDtypeStruct((rows, members, across), F32)] * 2
        if first:
            out_shape += [jax.ShapeDtypeStruct((2, rows, members, across), F32)]
    scratch += [pltpu.SemaphoreType.DMA((copies,)), pltpu.SemaphoreType.DMA((32,))]
    cfg = (first, last, za, zb, depth, members, across, pieces)
    cells = 2 * rows * members * across
    return call(
        functools.partial(sweep_kernel, cfg),
        "sweep",
        out_shape,
        [ANY] * len(operands),
        [ANY] * len(out_shape),
        scratch,
        alias=alias,
        after=after,
    )(*operands)


WAITS = {(1, 1): ("patches",), (2, 1): ("summed",)}
CUTS = (35, 34, 33, 32)
ORDER = (
    "planes",
    "gather",
    (1, 0),
    (1, 1),
    "local",
    (2, 0),
    (2, 1),
    "solve",
    (3, 0),
    (3, 1),
    "update",
)


def exact_pick(x, onehot):
    top = x.astype(jnp.bfloat16)
    rest = x - top.astype(F32)
    mid = rest.astype(jnp.bfloat16)
    low = (rest - mid.astype(F32)).astype(jnp.bfloat16)
    out = jnp.dot(low, onehot, preferred_element_type=F32)
    out = out + jnp.dot(mid, onehot, preferred_element_type=F32)
    return out + jnp.dot(top, onehot, preferred_element_type=F32)


def columns_of(cells, start, count, width, lanes, depth, across):
    lane = lax.broadcasted_iota(jnp.int32, (1, lanes), 1)
    at = lax.rem(lane, width)
    cell = jnp.zeros((1, lanes), jnp.int32)
    for o in range(count):
        cell = jnp.where((at >= o * SLOT) & (at < (o + 1) * SLOT), cells[start + o], cell)
    slot = lax.rem(lane, SLOT)
    y = lax.rem(cell, across) + slot - REACH
    y = jnp.where((slot < SIDE) & (at < count * SLOT), y, -1)
    line = lax.div(cell, across)
    return lax.div(line, depth), lax.rem(line, depth), y


def gather_kernel(spans, slabs, wells, rates, cells, head, storage, *refs):
    parts = len(spans)
    sides = (refs[:parts], refs[parts : 2 * parts])
    outs = refs[2 * parts : 2 * parts + slabs]
    forcing, field, picked, held_p, held_e, packed, sems, sem_out = refs[2 * parts + slabs :]
    out = held_p
    planes, depth, across = head.shape
    members, lanes = picked.shape[2:]
    odd, _, slab = spot()
    step = 16
    copies = {}
    for b in range(depth // step):
        for lo, hi in spans:
            s, e = max(lo, b * step), min(hi, (b + 1) * step)
            if s >= e:
                continue
            for side, plane in enumerate((1 - odd, odd)):
                ref = sides[side][spans.index((lo, hi))]
                batch = copies.setdefault(b, [])
                copy = pltpu.make_async_copy(
                    ref.at[pl.ds(s - lo, e - s)],
                    field.at[plane, pl.ds(s, e - s)],
                    sems.at[b, len(batch)],
                )
                copy.start()
                batch.append(copy)

    forcing[...] = storage[...] * head[...]
    lane = lax.broadcasted_iota(jnp.int32, (1, across), 1)

    def add_well(k, carry):
        cell = wells[k] - slab * (planes * depth * across)

        @pl.when((cell >= 0) & (cell < planes * depth * across))
        def _():
            line = lax.div(cell, across)
            x = lax.div(line, depth)
            z = lax.rem(line, depth)
            row = forcing[x, pl.ds(z, 1), :]
            here = lane == lax.rem(cell, across)
            forcing[x, pl.ds(z, 1), :] = row + jnp.where(here, rates[k], 0.0)

        return carry

    lax.fori_loop(0, wells.shape[0], add_well, 0)
    _, zcol, ycol = columns_of(cells, 0, lanes // SLOT, lanes, lanes, depth, across)
    across_ids = lax.broadcasted_iota(jnp.int32, (across, lanes), 0)
    onehot = jnp.where(across_ids == ycol, 1.0, 0.0).astype(jnp.bfloat16)
    held_p[...] = jnp.zeros_like(held_p)
    held_e[...] = jnp.zeros_like(held_e)
    depth_ids = lax.broadcasted_iota(jnp.int32, (depth, lanes), 0)
    for a, ref in enumerate((head, storage, forcing)):
        for i in range(planes):
            lines = exact_pick(ref[i], onehot)
            for d in range(SIDE):
                here = zcol + (d - REACH) == depth_ids
                line = jnp.sum(jnp.where(here, lines, 0.0), axis=0, keepdims=True)
                held_e[i, d, pl.ds(a, 1), :] = line
    for b in range(depth // step):
        for copy in copies[b]:
            copy.wait()
        some = pl.ds(step * b, step)
        for i in range(planes):
            rows = field[i, some].reshape(step * members, across)
            picked[i, some] = exact_pick(rows, onehot).reshape(step, members, lanes)

        def body(k, carry):
            for i in range(planes):
                held = [out[i, d, pl.ds(0, members), :] for d in range(SIDE)]
                for e in range(8):
                    z = b * step + k * 8 + e
                    value = picked[i, z]
                    for d in range(SIDE):
                        held[d] = jnp.where(zcol + (d - REACH) == z, value, held[d])
                for d in range(SIDE):
                    out[i, d, pl.ds(0, members), :] = held[d]
            return carry

        lax.fori_loop(0, step // 8, body, 0)

    width = lanes // slabs
    first = lax.broadcasted_iota(jnp.int32, (members, 128), 1) < 64
    for t in range(slabs):
        tile = pl.ds(width * t // 128 * 128, 128)
        shift = width * t % 128
        for i in range(planes):
            for d in range(SIDE):
                p = pltpu.roll(held_p[i, d, :, tile], (128 - shift) % 128, 1)
                e = pltpu.roll(held_e[i, d, :, tile], (192 - shift) % 128, 1)
                packed[t, i, d] = jnp.where(first, p, e)
    results = []
    for k in range(slabs):
        copy = pltpu.make_async_copy(packed.at[slab ^ k], outs[k], sem_out.at[k])
        copy.start()
        results.append(copy)
    for copy in results:
        copy.wait()


def gather_of(wells, rates, cells, head, storage, spans, slabs, side_a, side_b, after=()):
    planes, depth, across = head.shape
    members = side_a[0].shape[1]
    lanes = cells.shape[0] * SLOT
    held = (planes, SIDE, members, lanes)
    packed = (planes, SIDE, members, 128)
    return call(
        functools.partial(gather_kernel, spans, slabs),
        "gather",
        [jax.ShapeDtypeStruct(packed, F32)] * slabs + [jax.ShapeDtypeStruct(head.shape, F32)],
        [SMEM] * 3 + [VMEM] * 2 + [ANY] * (2 * len(spans)),
        [ANY] * slabs + [VMEM],
        [
            pltpu.VMEM((planes, depth, members, across), F32),
            pltpu.VMEM((planes, depth, members, lanes), F32),
            pltpu.VMEM(held, F32),
            pltpu.VMEM(held, F32),
            pltpu.VMEM((slabs,) + packed, F32),
            pltpu.SemaphoreType.DMA((depth // 16, 4)),
            pltpu.SemaphoreType.DMA((slabs,)),
        ],
        after=after,
    )(wells, rates, cells, head, storage, *side_a, *side_b)


def local_kernel(nz, ny, nobs, slabs, cells, perturb, *refs):
    blocks = refs[:slabs]
    out, R, RM, RP, H, HM, HP, ST, FO, W, NEW = refs[slabs:]
    members, lanes = R.shape[2:]
    _, _, slab = spot()
    share = nobs // slabs
    x0, zcol, ycol = columns_of(cells, slab * share, share, 64, lanes, nz, ny)

    def spread(ref, minus, plus, i, d, value):
        ref[i, d] = value
        minus[i, d] = pltpu.roll(value, 1, 1)
        plus[i, d] = pltpu.roll(value, lanes - 1, 1)

    def select(i, carry):
        x = x0 + (i - REACH)
        masks = [x == 2 * (slab ^ (g // 2)) + g % 2 for g in range(2 * slabs)]
        for d in range(SIDE):
            z = zcol + (d - REACH)
            inside = (x >= 0) & (x < 2 * slabs) & (z >= 0) & (z < nz)
            inside = inside & (ycol >= 0) & (ycol < ny)
            both = jnp.zeros((members, lanes), F32)
            for g in range(2 * slabs):
                both = jnp.where(masks[g], blocks[g // 2][g % 2, d], both)
            perm = both
            rest = pltpu.roll(both, 64, 1)
            r = jnp.where(inside, recip(perm), jnp.inf)
            spread(R, RM, RP, i, d, r)
            head = jnp.broadcast_to(jnp.where(inside, rest[0:1], 0.0), (members, lanes))
            spread(H, HM, HP, i, d, head)
            ST[i, d] = jnp.where(inside, rest[1:2], 1.0)
            FO[i, d] = jnp.where(inside, rest[2:3], 0.0)
        return carry

    lax.fori_loop(0, SIDE, select, 0)
    rs, hs = (RM, R, RP), (HM, H, HP)

    def update(i, d, first):
        mine = R[i, d]
        total = {}
        weight = {}
        for a in (-1, 0, 1):
            for b in (-1, 0, 1):
                for c in (-1, 0, 1):
                    n = abs(a) + abs(b) + abs(c)
                    if n == 0:
                        continue
                    u = recip(mine + rs[c + 1][i + a, d + b])
                    t = u * hs[c + 1][i + a, d + b]
                    total[n] = total[n] + t if n in total else t
                    if first:
                        weight[n] = weight[n] + u if n in weight else u
        gathered = 2.0 * total[1] + total[2] + 0.5 * total[3]
        if first:
            diagonal = ST[i, d] + (2.0 * weight[1] + weight[2] + 0.5 * weight[3])
            w = OMEGA * recip(diagonal)
            W[i, d] = w
        else:
            w = W[i, d]
        return (1.0 - OMEGA) * H[i, d] + w * (FO[i, d] + gathered)

    for sweep in range(1, REACH):
        width = SIDE - 2 * sweep

        def body(i, carry):
            for d in range(sweep, SIDE - sweep):
                NEW[i, d] = update(i, d, sweep == 1)
            return carry

        lax.fori_loop(sweep, SIDE - sweep, body, 0)
        for i in range(sweep, SIDE - sweep):
            for d in range(sweep, SIDE - sweep):
                spread(H, HM, HP, i, d, NEW[i, d])
    final = update(REACH, REACH, False)
    lane = lax.broadcasted_iota(jnp.int32, (lanes, 128), 0)
    target = lax.broadcasted_iota(jnp.int32, (lanes, 128), 1) - slab * share
    onehot = (lane == target * SLOT + REACH) & (target >= 0) & (target < share)
    observed = exact_pick(final, jnp.where(onehot, 1.0, 0.0).astype(jnp.bfloat16))
    rest = jnp.zeros((members, 128 - 2 * nobs), F32)
    part = perturb[...] * (1.0 / slabs)
    out[...] = jnp.concatenate([observed[:, :nobs], part, rest], 1)


def local_of(nz, ny, cells, perturb, blocks, after=()):
    nobs = cells.shape[0]
    lanes = 128
    members = perturb.shape[0]
    slabs = len(blocks)
    full = pltpu.VMEM((SIDE, SIDE, members, lanes), F32)
    line = pltpu.VMEM((SIDE, SIDE, 1, lanes), F32)
    return call(
        functools.partial(local_kernel, nz, ny, nobs, slabs),
        "local_heads",
        jax.ShapeDtypeStruct((members, 128), F32),
        [SMEM] + [VMEM] * (1 + slabs),
        VMEM,
        [full] * 6 + [line] * 2 + [full] * 2,
        after=after,
    )(cells, perturb, *blocks)


def solve_kernel(nobs, peers, values, noise, step, seen, out, aug):
    every = seen[...]
    total = every.shape[0]
    heads = every[:, :nobs]
    mean = jnp.sum(heads, axis=0, keepdims=True) * (1.0 / total)
    dev = heads - mean
    contract = (((0,), (0,)), ((), ()))
    cov = lax.dot_general(dev, dev, contract, precision=HIGHEST, preferred_element_type=F32)
    cov = cov * (1.0 / (total - 1))
    row = lax.broadcasted_iota(jnp.int32, (nobs, nobs), 0)
    col = lax.broadcasted_iota(jnp.int32, (nobs, nobs), 1)
    system = cov + jnp.where(row == col, noise[...] * (1.0 / step[0]), 0.0)
    identity = jnp.where(row == col, 1.0, 0.0)
    work = jnp.concatenate([system, identity], 1)
    line = lax.broadcasted_iota(jnp.int32, work.shape, 0)
    for k in range(nobs):
        pivot = work[k : k + 1, :] * (1.0 / work[k : k + 1, k : k + 1])
        work = jnp.where(line == k, pivot, work - work[:, k : k + 1] * pivot)
    aug[...] = work
    inverse = aug[:, pl.ds(nobs, nobs)]
    mine = every[: every.shape[0] // peers]
    residual = values[...] + mine[:, nobs : 2 * nobs] - mine[:, :nobs]
    gain = jnp.dot(residual, inverse, precision=HIGHEST, preferred_element_type=F32)
    nt = (((1,), (1,)), ((), ()))
    mixing = lax.dot_general(gain, dev, nt, precision=HIGHEST, preferred_element_type=F32)
    out[...] = mixing * (1.0 / (total - 1))


def solve_of(seen, peers, values, noise, step, after=()):
    nobs = values.shape[0]
    total = seen.shape[0]
    return call(
        functools.partial(solve_kernel, nobs, peers),
        "solve",
        jax.ShapeDtypeStruct((total // peers, total), F32),
        [VMEM, VMEM, SMEM, VMEM],
        VMEM,
        [pltpu.VMEM((nobs, 2 * nobs), F32)],
        after=after,
    )(values[None], noise[None], step, seen)


def update_kernel(step, mixing, lp, every, out, x, a, sem_lp, sem_in, sem_out):
    members, planes, depth, across = lp.shape
    peers = every.shape[0]
    _, me, _ = spot()
    blocks = [(b, i) for b in range(depth // step) for i in range(planes)]
    ahead = a.shape[0]
    ins, outs, fields = [], [], []
    for n, (b, i) in enumerate(blocks):
        rows = pl.ds(b * step, step)
        ins.append(
            pltpu.make_async_copy(every.at[:, i, rows], a.at[n % ahead], sem_in.at[n])
        )
        fields.append(
            pltpu.make_async_copy(lp.at[:, i, rows, :], x.at[:, i, rows, :], sem_lp.at[n])
        )
        outs.append(
            pltpu.make_async_copy(x.at[:, i, rows, :], out.at[:, i, rows, :], sem_out.at[n])
        )
    for n in range(ahead):
        ins[n].start()
        fields[n].start()
    m = mixing[...]
    m_top = m.astype(jnp.bfloat16)
    m_low = (m - m_top.astype(F32)).astype(jnp.bfloat16)
    left = jnp.concatenate([m_top, m_top], 1)
    right = jnp.concatenate([m_low, jnp.zeros_like(m_low)], 1)
    left = jnp.concatenate([left, right], 0)
    for n, (b, i) in enumerate(blocks):
        ins[n].wait()
        fields[n].wait()
        for g in range(step // 8):
            lines = []
            for z in range(8 * g, 8 * g + 8):
                f = jnp.concatenate([a[n % ahead, me ^ k, z] for k in range(peers)], 0)
                top = f.astype(jnp.bfloat16)
                low = (f - top.astype(F32)).astype(jnp.bfloat16)
                both = jnp.concatenate([top, low], 0)
                y = jnp.dot(left, both, preferred_element_type=F32)
                lines.append(y[:members] + y[members:])
            change = jnp.stack(lines, 0)
            some = pl.ds(b * step + 8 * g, 8)
            x[:, i, some, :] = x[:, i, some, :] + jnp.swapaxes(change, 0, 1)
        outs[n].start()
        if n + ahead < len(blocks):
            ins[n + ahead].start()
            fields[n + ahead].start()
    for copy in outs:
        copy.wait()


def update_of(mixing, lp, every, after=()):
    members, planes, depth, across = lp.shape
    peers = every.shape[0]
    step = 8
    ahead = 6
    count = planes * depth // step
    return call(
        functools.partial(update_kernel, step),
        "update",
        jax.ShapeDtypeStruct(lp.shape, F32),
        [VMEM, ANY, ANY],
        ANY,
        [
            pltpu.VMEM(lp.shape, F32),
            pltpu.VMEM((ahead, peers, step, members, across), F32),
            pltpu.SemaphoreType.DMA((count,)),
            pltpu.SemaphoreType.DMA((count,)),
            pltpu.SemaphoreType.DMA((count,)),
        ],
        after=after,
    )(mixing, lp, every)


def swap(x, axis, bit):
    return lax.ppermute(x, axis, [(i, i ^ bit) for i in range(lax.axis_size(axis))])


def swaps(parts, axis):
    return [parts[0]] + [swap(parts[k], axis, k) for k in range(1, lax.axis_size(axis))]


def gather_by_swaps(x, axis, token):
    x = lax.optimization_barrier((x, *token))[0]
    bit = 1
    while bit < lax.axis_size(axis):
        x = jnp.concatenate([x, swap(x, axis, bit)], 0)
        bit *= 2
    return x


def halo(x, side):
    pairs = [(i, i + 1) for i in range(side, lax.axis_size("space") - 1, 2)]
    return lax.ppermute(x, "space", pairs + [(b, a) for a, b in pairs])


def shards(
    log_perm,
    storage,
    head_init,
    well_cells,
    well_rates,
    obs_cells,
    obs_values,
    noise_var,
    step_size,
    perturb,
):
    shape = log_perm.shape
    members, planes, depth, across = shape
    slabs = lax.axis_size("space")
    peers = lax.axis_size("ens")
    spans = row_spans(depth, CUTS[0])
    names = ("a", "b", "ra", "rb")
    state = {"token": ()}

    def after(*refs):
        state["token"] = refs

    def span(parts, cut):
        return [(x, lo, hi) for x, (lo, hi) in zip(parts, row_spans(depth, cut))]

    def planes_step():
        side_a, side_b, own = planes_of(log_perm, head_init, CUTS[0])
        state["a"], state["b"], state["own"] = side_a, side_b, own
        far_a = [halo(x, 0) for x in side_a]
        far_b = [halo(x, 1) for x in side_b]
        state["far"] = [v for v in zip(far_a, far_b)]
        sides = (side_a, side_b, far_a, far_b)
        state["perms"] = {("p", n): span(v, CUTS[0]) for n, v in zip(names, sides)}
        state["new"] = {1: [], 2: []}
        state["every"] = lax.all_gather(own, "ens", axis=0)
        after(own)

    def gather_step():
        *patch, state["forcing"] = gather_of(
            well_cells,
            well_rates,
            obs_cells,
            head_init,
            storage,
            spans,
            slabs,
            state["a"],
            state["b"],
            after=state["token"],
        )
        state["patches"] = swaps(patch, "space")
        after(patch[0])

    def local_step():
        seen = local_of(
            depth, across, obs_cells, perturb, state["patches"], after=state["token"]
        )
        state["local"] = seen
        seen = sum(swaps([seen] * slabs, "space"))
        state["summed"] = [seen]
        after(state["local"])

    def solve_step():
        seen = gather_by_swaps(state["summed"][0], "ens", state["token"])
        state["mixing"] = solve_of(
            seen, peers, obs_values, noise_var, step_size, after=state["token"]
        )
        after(state["mixing"])

    def update_step():
        state["updated"] = update_of(
            state["mixing"], log_perm, state["every"], after=state["token"]
        )
        after(state["updated"])

    def sweep_step(sweep, part):
        first, last = sweep == 1, sweep == 3
        lo, hi = row_spans(depth, CUTS[sweep])[part]
        lines = [state["forcing"]] + ([storage, head_init] if first else [])
        fields = {k: v[: part + 1] if k[1][0] == "r" else v for k, v in state["perms"].items()}
        if not first:
            columns = list(zip(*state["new"][sweep - 1]))
            for k, n in enumerate(names):
                fields["h", n] = span(columns[k], CUTS[sweep - 1])
            weights = list(zip(*state["new"][1]))[4]
            fields["w", "w"] = span(weights, CUTS[1])
        token = () if "head" in state else state["token"]
        for key in WAITS.get((sweep, part), ()):
            token = token + tuple(state[key])
        out = sweep_of(first, last, lo, hi, shape, lines, fields, state.get("head"), after=token)
        if last:
            state["head"] = out[0]
        else:
            far = (halo(out[0], 0), halo(out[1], 1))
            state["new"][sweep].append((out[0], out[1]) + far + tuple(out[2:]))
        after(out[0])

    steps = dict(
        planes=planes_step,
        gather=gather_step,
        local=local_step,
        solve=solve_step,
        update=update_step,
    )
    for step in ORDER:
        if isinstance(step, tuple):
            sweep_step(*step)
        else:
            steps[step]()
    return (state["head"], state["updated"])


def solution(mesh):
    return jax.shard_map(
        shards,
        mesh=mesh,
        in_specs=(
            P("ens", "space", None, None),
            P("space", None, None),
            P("space", None, None),
            P(),
            P(),
            P(),
            P(),
            P(),
            P(),
            P("ens", None),
        ),
        out_specs=(P("ens", "space", None, None), P("ens", "space", None, None)),
        check_vma=False,
    )
```

time: 293 us -> 159 us (0.54)
  other arithmetic: 91.8 us -> 3.96 us
  Pallas kernels: 0 us -> 77.4 us
  waiting for transfers between devices: 72.4 us -> 18.2 us
  local copies, waits for them, and re-layouts: 48.4 us -> 0 us
  blocking collectives: 27.2 us -> 0 us
  starting transfers between devices: 23 us -> 44.1 us
  matrix products: 13.7 us -> 0 us
    pallas_call x0 -> x11, Pallas kernels: none -> 77.4 us  [the longest x6 48.7 us: sweep_of(): call(functools.partial(sweep_kernel, cfg), 'sweep', out_shape, [ANY] * le...]
    add x3 -> x1, other arithmetic: 69.5 us -> 1.29 us  [local_step(): seen = sum(swaps([seen] * slabs, 'space'))]
    ppermute x8 -> x21, waiting for transfers between devices: 72.4 us -> 18.1 us  [the longest x9 15.1 us: swap(): lax.ppermute(x, axis, [(i, i ^ bit) for i in range(lax.axis_size(axis))])]
    ppermute x8 -> x21, starting transfers between devices: 22.9 us -> 44.1 us  [the longest x12 27.4 us: halo(): return lax.ppermute(x, 'space', pairs + [(b, a) for a, b in pairs])]
    all_gather x2 -> x0, blocking collectives: 18.3 us -> none  [the longest x1 9.28 us: shards(): piece_dev = lax.all_gather(deviation, 'ens', axis=0, tiled=True)]
    add x1 -> x0, local copies, waits for them, and re-layouts: 18 us -> none  [shards(): (1.0 - OMEGA) * head_field + OMEGA * (forcing + gathered) / diagonal]
    dot_general x4 -> x0, matrix products: 13.5 us -> none  [the longest x1 11 us: shards(): lax.dot_general(mixing, piece_field, (((0,), (0,)), ((), ())), precision=...]
    gather x2 -> x0, local copies, waits for them, and re-layouts: 11.2 us -> none  [shards(): jnp.take(head_field.reshape(members, cell_count), jnp.clip(local_obs, 0,...]
  transfers between devices with their start and end apart: 9 -> 22, of which waited for: 8 -> 6; matrix products, arithmetic and copies ran while one was open for 46% -> 2% of each run, Pallas kernels for 0% -> 40%
where the time goes in v1:
time: 159 us; the launch traced here: 158 us
  Pallas kernels  77.4 us (49%)
  starting transfers between devices  44.1 us (28%)
  waiting for transfers between devices  18.2 us (11%)
  between operations  14.8 us (9%)
  other arithmetic  3.96 us (2%)
    pallas_call x6, Pallas kernels, sweep_of(): call(functools.partial(sweep_kernel, cfg), 'sweep', out_shape, [ANY] * le...  48.7 us
    ppermute x12, starting transfers between devices, halo(): return lax.ppermute(x, 'space', pairs + [(b, a) for a, b in pairs])  27.4 us
    ppermute x9, starting transfers between devices, swap(): lax.ppermute(x, axis, [(i, i ^ bit) for i in range(lax.axis_size(axis))])  16.7 us
    ppermute x9, waiting for transfers between devices, swap(): lax.ppermute(x, axis, [(i, i ^ bit) for i in range(lax.axis_size(axis))])  15.1 us
    pallas_call x1, Pallas kernels, update_of(): call(functools.partial(update_kernel, step), 'update', jax.ShapeDtypeStru...  9.14 us
    pallas_call x1, Pallas kernels, gather_of(): call(functools.partial(gather_kernel, spans, slabs), 'gather', [jax.Shape...  6.72 us
    pallas_call x1, Pallas kernels, solve_of(): call(functools.partial(solve_kernel, nobs, peers), 'solve', jax.ShapeDtyp...  4.71 us
    pallas_call x1, Pallas kernels, planes_of(): call(functools.partial(planes_kernel, step, cut), 'planes', sides * 2 + [...  4.36 us
  transfers between devices with their start and end apart: 22, of which 6 were waited for; matrix products, arithmetic and copies ran while one was open for 2% of the time, Pallas kernels for 40%

profile of v1, /device:TPU:0, one launch (start us, length us, event | category | flops | bytes accessed | tf_op | source)
XLA Modules:
  0.0 158.5 jit_solution(9240354458109920469)
XLA Ops:
  7.2 4.4 %planes.1 = (f32[43,8,512]{2,1,0:T(8,128)}, f32[29,8,512]{2,1,0:T(8,128)}, f32[43,8,512]{2,1,0:T(8,128)}, f32[29,8,512]{2,1,0:T(8,128)}, f32[2,64,8,512]{3,2,1,0:T(8,128)}) custom-call(f32[8,2,64,512]{3,2,1,0:T(8,128)} %refs_2_.7, f32[2,64,512]{2,1,0:T(8,128)} %refs_7_.1), custom_call_target="tpu_custom_call" | custom-call | bytes 12000000 | tf_op jit(solution)/shard_map/planes/pallas_call | solution.py:126
  11.6 3.1 %collective-permute-start = (f32[43,8,512]{2,1,0:T(8,128)}, f32[43,8,512]{2,1,0:T(8,128)}, u32[]{:S(2)}, u32[]{:S(2)}) collective-permute-start(f32[43,8,512]{2,1,0:T(8,128)} %get-tuple-element.24.refs_6_.refs_4_.refs_8_.refs_2_.refs_3_.refs_1_), channel_id=1, source_target_pairs={{0,8},{16,24},{8,0},{24,16},{1,9},{17,25},{9,1},{25,17},{2,10},{18... | collective-permute-start | bytes 2113544 | tf_op jit(solution)/shard_map/ppermute | solution.py:861
  16.2 3.6 %collective-permute-start.1 = (f32[29,8,512]{2,1,0:T(8,128)}, f32[29,8,512]{2,1,0:T(8,128)}, u32[]{:S(2)}, u32[]{:S(2)}) collective-permute-start(f32[29,8,512]{2,1,0:T(8,128)} %get-tuple-element.25.refs_7_.refs_5_.refs_9_.refs_3_.refs_4_.refs_2_), channel_id=1, source_target_pairs={{0,8},{16,24},{8,0},{24,16},{1,9},{17,25},{9,1},{25,17},{2,10},{18... | collective-permute-start | bytes 1425416 | tf_op jit(solution)/shard_map/ppermute | solution.py:861
  21.3 6.7 %gather.1 = (f32[2,7,8,128]{3,2,1,0:T(8,128)}, f32[2,7,8,128]{3,2,1,0:T(8,128)}, f32[2,7,8,128]{3,2,1,0:T(8,128)}, f32[2,7,8,128]{3,2,1,0:T(8,128)}, f32[2,64,512]{2,1,0:T(8,128)}) custom-call(f32[2,64,8,512]{3,2,1,0:T(8,128)} %get-tuple-element.23.refs_0_, s32[16]{0:T(128)} %refs_1_.4, f32[16]{0:T(128)} %refs_2_.4, s32[32]{0:T(128)} %refs_1_.5, ...), custom_call_target="tpu_custom_call" | custom-call | bytes 15000000 | tf_op jit(solution)/shard_map/gather/pallas_call | solution.py:608
  28.6 3.0 %collective-permute-done.refs_8_.refs_12_.refs_6_.refs_7_.refs_5_ = f32[43,8,512]{2,1,0:T(8,128)} collective-permute-done((f32[43,8,512]{2,1,0:T(8,128)}, f32[43,8,512]{2,1,0:T(8,128)}, u32[]{:S(2)}, u32[]{:S(2)}) %collective-permute-start) | collective-permute-done | bytes 704544 | tf_op jit(solution)/shard_map/ppermute | solution.py:861
  31.6 3.1 %collective-permute-start.5 = (f32[2,7,8,128]{3,2,1,0:T(8,128)}, f32[2,7,8,128]{3,2,1,0:T(8,128)}, u32[]{:S(2)}, u32[]{:S(2)}) collective-permute-start(f32[2,7,8,128]{3,2,1,0:T(8,128)} %get-tuple-element.32), channel_id=1, source_target_pairs={{0,16},{8,24},{16,0},{24,8},{1,17},{9,25},{17,1},{25,9},{2,18},{10... | collective-permute-start | bytes 172040 | tf_op jit(solution)/shard_map/ppermute | solution.py:843
  34.7 8.5 %sweep.6 = (f32[34,8,512]{2,1,0:T(8,128)}, f32[34,8,512]{2,1,0:T(8,128)}, f32[2,34,8,512]{3,2,1,0:T(8,128)}) custom-call(f32[2,7,8,128]{3,2,1,0:T(8,128)} %get-tuple-element.29.refs_0_.refs_1_.refs_3_, f32[2,64,512]{2,1,0:T(8,128)} %get-tuple-element.28.refs_1_.refs_5_.refs_2_.refs_18_.refs_0_, f32[2,64,512]{2,1,0:T(8,128)} %refs_6_.1, ...), custom_call_target="tpu_custom_call" | custom-call | bytes 39000000 | tf_op jit(solution)/shard_map/sweep/pallas_call | solution.py:451
  43.2 2.1 %collective-permute-start.7 = (f32[34,8,512]{2,1,0:T(8,128)}, f32[34,8,512]{2,1,0:T(8,128)}, u32[]{:S(2)}, u32[]{:S(2)}) collective-permute-start(f32[34,8,512]{2,1,0:T(8,128)} %get-tuple-element.30.refs_0_.refs_8_.refs_11_), channel_id=1, source_target_pairs={{0,8},{16,24},{8,0},{24,16},{1,9},{17,25},{9,1},{25,17},{2,10},{18... | collective-permute-start | bytes 1671176 | tf_op jit(solution)/shard_map/ppermute | solution.py:861
  47.8 3.0 %collective-permute-start.6 = (f32[2,7,8,128]{3,2,1,0:T(8,128)}, f32[2,7,8,128]{3,2,1,0:T(8,128)}, u32[]{:S(2)}, u32[]{:S(2)}) collective-permute-start(f32[2,7,8,128]{3,2,1,0:T(8,128)} %get-tuple-element.33), channel_id=1, source_target_pairs={{0,24},{8,16},{16,8},{24,0},{1,25},{9,17},{17,9},{25,1},{2,26},{10... | collective-permute-start | bytes 172040 | tf_op jit(solution)/shard_map/ppermute | solution.py:843
  50.8 8.8 %collective-permute-done.6.refs_4_.refs_6_ = f32[2,7,8,128]{3,2,1,0:T(8,128)} collective-permute-done((f32[2,7,8,128]{3,2,1,0:T(8,128)}, f32[2,7,8,128]{3,2,1,0:T(8,128)}, u32[]{:S(2)}, u32[]{:S(2)}) %collective-permute-start.6) | collective-permute-done | bytes 57376 | tf_op jit(solution)/shard_map/ppermute | solution.py:843
  59.6 8.4 %sweep.7 = (f32[30,8,512]{2,1,0:T(8,128)}, f32[30,8,512]{2,1,0:T(8,128)}, f32[2,30,8,512]{3,2,1,0:T(8,128)}) custom-call(f32[34,8,512]{2,1,0:T(8,128)} %get-tuple-element.30.refs_0_.refs_8_.refs_11_, f32[2,7,8,128]{3,2,1,0:T(8,128)} %get-tuple-element.29.refs_0_.refs_1_.refs_3_, f32[2,7,8,128]{3,2,1,0:T(8,128)} %collective-permute-done.4.refs_2_.refs_4_, ...), custom_call_target="tpu_custom_call" | custom-call | bytes 39000000 | tf_op jit(solution)/shard_map/sweep/pallas_call | solution.py:451
  69.5 5.3 %collective-permute-start.8 = (f32[30,8,512]{2,1,0:T(8,128)}, f32[30,8,512]{2,1,0:T(8,128)}, u32[]{:S(2)}, u32[]{:S(2)}) collective-permute-start(f32[30,8,512]{2,1,0:T(8,128)} %get-tuple-element.34.refs_0_.refs_9_.refs_12_), channel_id=1, source_target_pairs={{0,8},{16,24},{8,0},{24,16},{1,9},{17,25},{9,1},{25,17},{2,10},{18... | collective-permute-start | bytes 1474568 | tf_op jit(solution)/shard_map/ppermute | solution.py:861
  74.8 3.7 %local_heads.1.refs_0_ = f32[8,128]{1,0:T(8,128)} custom-call(f32[30,8,512]{2,1,0:T(8,128)} %get-tuple-element.34.refs_0_.refs_9_.refs_12_, s32[32]{0:T(128)} %refs_1_.5, f32[8,32]{1,0:T(8,128)} %refs_2_.6, f32[2,7,8,128]{3,2,1,0:T(8,128)} %get-tuple-element.29.refs_0_.refs_1_.refs_3_, f32[2,7,8,128]{3,2,1,0:T(8,128)} %collective-permute-done.4.refs_2_.refs_4_, ...), custom_call_target="tpu_custom_call" | custom-call | bytes 15000000 | tf_op jit(solution)/shard_map/local_heads/pallas_call | solution.py:716
  78.5 6.0 %collective-permute-start.12 = (f32[8,128]{1,0:T(8,128)}, f32[8,128]{1,0:T(8,128)}, u32[]{:S(2)}, u32[]{:S(2)}) collective-permute-start(f32[8,128]{1,0:T(8,128)} %local_heads.1.refs_0_), channel_id=1, source_target_pairs={{0,16},{8,24},{16,0},{24,8},{1,17},{9,25},{17,1},{25,9},{2,18},{10... | collective-permute-start | bytes 12296 | tf_op jit(solution)/shard_map/ppermute | solution.py:843
  85.7 7.6 %sweep.8 = (f32[33,8,512]{2,1,0:T(8,128)}, f32[33,8,512]{2,1,0:T(8,128)}) custom-call(f32[8,128]{1,0:T(8,128)} %local_heads.1.refs_0_, f32[2,64,512]{2,1,0:T(8,128)} %get-tuple-element.28.refs_1_.refs_5_.refs_2_.refs_18_.refs_0_, f32[43,8,512]{2,1,0:T(8,128)} %get-tuple-element.24.refs_6_.refs_4_.refs_8_.refs_2_.refs_3_.refs_1_, ...), custom_call_target="tpu_custom_call" | custom-call | bytes 39000000 | tf_op jit(solution)/shard_map/sweep/pallas_call | solution.py:451
  93.4 1.5 collective-permute-start.16
  96.2 8.0 %sweep.9 = (f32[31,8,512]{2,1,0:T(8,128)}, f32[31,8,512]{2,1,0:T(8,128)}) custom-call(f32[33,8,512]{2,1,0:T(8,128)} %get-tuple-element.39.refs_0_.refs_8_.refs_9_, f32[8,128]{1,0:T(8,128)} %add_add_fusion.refs_1_, f32[2,64,512]{2,1,0:T(8,128)} %get-tuple-element.28.refs_1_.refs_5_.refs_2_.refs_18_.refs_0_, ...), custom_call_target="tpu_custom_call" | custom-call | bytes 39000000 | tf_op jit(solution)/shard_map/sweep/pallas_call | solution.py:451
  104.2 4.4 %collective-permute-start.15 = (f32[31,8,512]{2,1,0:T(8,128)}, f32[31,8,512]{2,1,0:T(8,128)}, u32[]{:S(2)}, u32[]{:S(2)}) collective-permute-start(f32[31,8,512]{2,1,0:T(8,128)} %get-tuple-element.40.refs_0_.refs_9_.refs_10_), channel_id=1, source_target_pairs={{0,8},{16,24},{8,0},{24,16},{1,9},{17,25},{9,1},{25,17},{2,10},{18... | collective-permute-start | bytes 1523720 | tf_op jit(solution)/shard_map/ppermute | solution.py:861
  113.6 2.2 %collective-permute-done.19 = f32[16,128]{1,0:T(8,128)S(1)} collective-permute-done((f32[16,128]{1,0:T(8,128)S(1)}, f32[16,128]{1,0:T(8,128)S(1)}, u32[]{:S(2)}, u32[]{:S(2)}) %collective-permute-start.19) | collective-permute-done | bytes 8224 | tf_op jit(solution)/shard_map/ppermute | solution.py:843
  118.6 1.7 %collective-permute-done.20 = f32[32,128]{1,0:T(8,128)S(1)} collective-permute-done((f32[32,128]{1,0:T(8,128)S(1)}, f32[32,128]{1,0:T(8,128)S(1)}, u32[]{:S(2)}, u32[]{:S(2)}) %collective-permute-start.20) | collective-permute-done | bytes 16416 | tf_op jit(solution)/shard_map/ppermute | solution.py:843
  121.5 4.7 %solve.1.refs_0_.refs_1_ = f32[8,64]{1,0:T(8,128)} custom-call(f32[31,8,512]{2,1,0:T(8,128)} %get-tuple-element.40.refs_0_.refs_9_.refs_10_, f32[1,32]{1,0:T(1,128)} %bitcast.4, f32[1,32]{1,0:T(1,128)} %bitcast.5, f32[1]{0:T(128)S(6)} %copy.14.refs_3_, f32[64,128]{1,0:T(8,128)} %pad_maximum_fusion.refs_4_), custom_call_target="tpu_custom_call" | custom-call | bytes 15000000 | tf_op jit(solution)/shard_map/solve/pallas_call | solution.py:758
  126.3 7.7 %sweep.10.refs_19_ = f32[8,2,64,512]{3,2,1,0:T(8,128)} custom-call(f32[8,64]{1,0:T(8,128)} %solve.1.refs_0_.refs_1_, f32[2,64,512]{2,1,0:T(8,128)} %get-tuple-element.28.refs_1_.refs_5_.refs_2_.refs_18_.refs_0_, f32[43,8,512]{2,1,0:T(8,128)} %get-tuple-element.24.refs_6_.refs_4_.refs_8_.refs_2_.refs_3_.refs_1_, ...), custom_call_target="tpu_custom_call" | custom-call | bytes 39000000 | tf_op jit(solution)/shard_map/sweep/pallas_call | solution.py:451
  134.0 8.4 %sweep.11.refs_0_ = f32[8,2,64,512]{3,2,1,0:T(8,128)} custom-call(f32[2,64,512]{2,1,0:T(8,128)} %get-tuple-element.28.refs_1_.refs_5_.refs_2_.refs_18_.refs_0_, f32[43,8,512]{2,1,0:T(8,128)} %get-tuple-element.24.refs_6_.refs_4_.refs_8_.refs_2_.refs_3_.refs_1_, ...), custom_call_target="tpu_custom_call", output_to_operand_aliasing={{}: (19, {})} | custom-call | bytes 39000000 | tf_op jit(solution)/shard_map/sweep/pallas_call | solution.py:451
  142.5 9.1 %update.1 = f32[8,2,64,512]{3,2,1,0:T(8,128)} custom-call(f32[8,2,64,512]{3,2,1,0:T(8,128)} %sweep.11.refs_0_, f32[8,64]{1,0:T(8,128)} %solve.1.refs_0_.refs_1_, f32[8,2,64,512]{3,2,1,0:T(8,128)} %refs_2_.7, f32[8,2,64,8,512]{4,3,2,1,0:T(8,128)} %bitcast.3), custom_call_target="tpu_custom_call" | custom-call | bytes 12000000 | tf_op jit(solution)/shard_map/update/pallas_call | solution.py:825
  (36 shorter events, 18.6 us)
Async XLA Ops:
  7.2 135.3 %all-gather.3.cloned.1.call-start = ((), (), s32[]{:S(2)}) async-start(), calls=%async_computation | async-start | bytes 18874368 | tf_op jit(solution)/shard_map/all_gather | solution.py:899
  11.6 20.0 %collective-permute-start = (f32[43,8,512]{2,1,0:T(8,128)}, f32[43,8,512]{2,1,0:T(8,128)}, u32[]{:S(2)}, u32[]{:S(2)}) collective-permute-start(f32[43,8,512]{2,1,0:T(8,128)} %get-tuple-element.24.refs_6_.refs_4_.refs_8_.refs_2_.refs_3_.refs_1_), channel_id=1, source_target_pairs={{0,8},{16,24},{8,0},{24,16},{1,9},{17,25},{9,1},{25,17},{2,10},{18... | collective-permute-start | bytes 2113544 | tf_op jit(solution)/shard_map/ppermute | solution.py:861
  14.7 20.0 %collective-permute-start.2 = (f32[43,8,512]{2,1,0:T(8,128)}, f32[43,8,512]{2,1,0:T(8,128)}, u32[]{:S(2)}, u32[]{:S(2)}) collective-permute-start(f32[43,8,512]{2,1,0:T(8,128)} %get-tuple-element.26.refs_8_.refs_6_.refs_10_.refs_4_.refs_5_.refs_3_), channel_id=1, source_target_pairs={{8,16},{16,8},{9,17},{17,9},{10,18},{18,10},{11,19},{19,11},{12,20... | collective-permute-start | bytes 2113544 | tf_op jit(solution)/shard_map/ppermute | solution.py:861
  16.2 43.4 %collective-permute-start.1 = (f32[29,8,512]{2,1,0:T(8,128)}, f32[29,8,512]{2,1,0:T(8,128)}, u32[]{:S(2)}, u32[]{:S(2)}) collective-permute-start(f32[29,8,512]{2,1,0:T(8,128)} %get-tuple-element.25.refs_7_.refs_5_.refs_9_.refs_3_.refs_4_.refs_2_), channel_id=1, source_target_pairs={{0,8},{16,24},{8,0},{24,16},{1,9},{17,25},{9,1},{25,17},{2,10},{18... | collective-permute-start | bytes 1425416 | tf_op jit(solution)/shard_map/ppermute | solution.py:861
  19.8 39.8 %collective-permute-start.3 = (f32[29,8,512]{2,1,0:T(8,128)}, f32[29,8,512]{2,1,0:T(8,128)}, u32[]{:S(2)}, u32[]{:S(2)}) collective-permute-start(f32[29,8,512]{2,1,0:T(8,128)} %get-tuple-element.27.refs_9_.refs_7_.refs_11_.refs_5_.refs_6_.refs_4_), channel_id=1, source_target_pairs={{8,16},{16,8},{9,17},{17,9},{10,18},{18,10},{11,19},{19,11},{12,20... | collective-permute-start | bytes 1425416 | tf_op jit(solution)/shard_map/ppermute | solution.py:861
  28.0 17.3 %collective-permute-start.4 = (f32[2,7,8,128]{3,2,1,0:T(8,128)}, f32[2,7,8,128]{3,2,1,0:T(8,128)}, u32[]{:S(2)}, u32[]{:S(2)}) collective-permute-start(f32[2,7,8,128]{3,2,1,0:T(8,128)} %get-tuple-element.31), channel_id=1, source_target_pairs={{0,8},{8,0},{16,24},{24,16},{1,9},{9,1},{17,25},{25,17},{2,10},{10... | collective-permute-start | bytes 172040 | tf_op jit(solution)/shard_map/ppermute | solution.py:843
  31.6 16.2 %collective-permute-start.5 = (f32[2,7,8,128]{3,2,1,0:T(8,128)}, f32[2,7,8,128]{3,2,1,0:T(8,128)}, u32[]{:S(2)}, u32[]{:S(2)}) collective-permute-start(f32[2,7,8,128]{3,2,1,0:T(8,128)} %get-tuple-element.32), channel_id=1, source_target_pairs={{0,16},{8,24},{16,0},{24,8},{1,17},{9,25},{17,1},{25,9},{2,18},{10... | collective-permute-start | bytes 172040 | tf_op jit(solution)/shard_map/ppermute | solution.py:843
  43.2 42.5 %collective-permute-start.7 = (f32[34,8,512]{2,1,0:T(8,128)}, f32[34,8,512]{2,1,0:T(8,128)}, u32[]{:S(2)}, u32[]{:S(2)}) collective-permute-start(f32[34,8,512]{2,1,0:T(8,128)} %get-tuple-element.30.refs_0_.refs_8_.refs_11_), channel_id=1, source_target_pairs={{0,8},{16,24},{8,0},{24,16},{1,9},{17,25},{9,1},{25,17},{2,10},{18... | collective-permute-start | bytes 1671176 | tf_op jit(solution)/shard_map/ppermute | solution.py:861
  45.3 40.4 %collective-permute-start.9 = (f32[34,8,512]{2,1,0:T(8,128)}, f32[34,8,512]{2,1,0:T(8,128)}, u32[]{:S(2)}, u32[]{:S(2)}) collective-permute-start(f32[34,8,512]{2,1,0:T(8,128)} %get-tuple-element.35.refs_10_.refs_13_), channel_id=1, source_target_pairs={{8,16},{16,8},{9,17},{17,9},{10,18},{18,10},{11,19},{19,11},{12,20... | collective-permute-start | bytes 1671176 | tf_op jit(solution)/shard_map/ppermute | solution.py:861
  47.8 11.7 %collective-permute-start.6 = (f32[2,7,8,128]{3,2,1,0:T(8,128)}, f32[2,7,8,128]{3,2,1,0:T(8,128)}, u32[]{:S(2)}, u32[]{:S(2)}) collective-permute-start(f32[2,7,8,128]{3,2,1,0:T(8,128)} %get-tuple-element.33), channel_id=1, source_target_pairs={{0,24},{8,16},{16,8},{24,0},{1,25},{9,17},{17,9},{25,1},{2,26},{10... | collective-permute-start | bytes 172040 | tf_op jit(solution)/shard_map/ppermute | solution.py:843
  68.0 10.5 %collective-permute-start.10 = (f32[30,8,512]{2,1,0:T(8,128)}, f32[30,8,512]{2,1,0:T(8,128)}, u32[]{:S(2)}, u32[]{:S(2)}) collective-permute-start(f32[30,8,512]{2,1,0:T(8,128)} %get-tuple-element.36.refs_11_.refs_14_), channel_id=1, source_target_pairs={{8,16},{16,8},{9,17},{17,9},{10,18},{18,10},{11,19},{19,11},{12,20... | collective-permute-start | bytes 1474568 | tf_op jit(solution)/shard_map/ppermute | solution.py:861
  69.5 15.0 %collective-permute-start.8 = (f32[30,8,512]{2,1,0:T(8,128)}, f32[30,8,512]{2,1,0:T(8,128)}, u32[]{:S(2)}, u32[]{:S(2)}) collective-permute-start(f32[30,8,512]{2,1,0:T(8,128)} %get-tuple-element.34.refs_0_.refs_9_.refs_12_), channel_id=1, source_target_pairs={{0,8},{16,24},{8,0},{24,16},{1,9},{17,25},{9,1},{25,17},{2,10},{18... | collective-permute-start | bytes 1474568 | tf_op jit(solution)/shard_map/ppermute | solution.py:861
  78.5 16.4 %collective-permute-start.11 = (f32[8,128]{1,0:T(8,128)}, f32[8,128]{1,0:T(8,128)}, u32[]{:S(2)}, u32[]{:S(2)}) collective-permute-start(f32[8,128]{1,0:T(8,128)} %local_heads.1.refs_0_), channel_id=1, source_target_pairs={{0,8},{8,0},{16,24},{24,16},{1,9},{9,1},{17,25},{25,17},{2,10},{10... | collective-permute-start | bytes 12296 | tf_op jit(solution)/shard_map/ppermute | solution.py:843
  78.5 16.4 %collective-permute-start.12 = (f32[8,128]{1,0:T(8,128)}, f32[8,128]{1,0:T(8,128)}, u32[]{:S(2)}, u32[]{:S(2)}) collective-permute-start(f32[8,128]{1,0:T(8,128)} %local_heads.1.refs_0_), channel_id=1, source_target_pairs={{0,16},{8,24},{16,0},{24,8},{1,17},{9,25},{17,1},{25,9},{2,18},{10... | collective-permute-start | bytes 12296 | tf_op jit(solution)/shard_map/ppermute | solution.py:843
  84.5 10.3 %collective-permute-start.13 = (f32[8,128]{1,0:T(8,128)}, f32[8,128]{1,0:T(8,128)}, u32[]{:S(2)}, u32[]{:S(2)}) collective-permute-start(f32[8,128]{1,0:T(8,128)} %local_heads.1.refs_0_), channel_id=1, source_target_pairs={{0,24},{8,16},{16,8},{24,0},{1,25},{9,17},{17,9},{25,1},{2,26},{10... | collective-permute-start | bytes 12296 | tf_op jit(solution)/shard_map/ppermute | solution.py:843
  93.3 33.0 %collective-permute-start.14 = (f32[33,8,512]{2,1,0:T(8,128)}, f32[33,8,512]{2,1,0:T(8,128)}, u32[]{:S(2)}, u32[]{:S(2)}) collective-permute-start(f32[33,8,512]{2,1,0:T(8,128)} %get-tuple-element.39.refs_0_.refs_8_.refs_9_), channel_id=1, source_target_pairs={{0,8},{16,24},{8,0},{24,16},{1,9},{17,25},{9,1},{25,17},{2,10},{18... | collective-permute-start | bytes 1622024 | tf_op jit(solution)/shard_map/ppermute | solution.py:861
  93.4 32.9 %collective-permute-start.16 = (f32[33,8,512]{2,1,0:T(8,128)}, f32[33,8,512]{2,1,0:T(8,128)}, u32[]{:S(2)}, u32[]{:S(2)}) collective-permute-start(f32[33,8,512]{2,1,0:T(8,128)} %get-tuple-element.41.refs_10_.refs_11_), channel_id=1, source_target_pairs={{8,16},{16,8},{9,17},{17,9},{10,18},{18,10},{11,19},{19,11},{12,20... | collective-permute-start | bytes 1622024 | tf_op jit(solution)/shard_map/ppermute | solution.py:861
  104.2 22.0 %collective-permute-start.15 = (f32[31,8,512]{2,1,0:T(8,128)}, f32[31,8,512]{2,1,0:T(8,128)}, u32[]{:S(2)}, u32[]{:S(2)}) collective-permute-start(f32[31,8,512]{2,1,0:T(8,128)} %get-tuple-element.40.refs_0_.refs_9_.refs_10_), channel_id=1, source_target_pairs={{0,8},{16,24},{8,0},{24,16},{1,9},{17,25},{9,1},{25,17},{2,10},{18... | collective-permute-start | bytes 1523720 | tf_op jit(solution)/shard_map/ppermute | solution.py:861
  108.7 17.6 %collective-permute-start.17 = (f32[31,8,512]{2,1,0:T(8,128)}, f32[31,8,512]{2,1,0:T(8,128)}, u32[]{:S(2)}, u32[]{:S(2)}) collective-permute-start(f32[31,8,512]{2,1,0:T(8,128)} %get-tuple-element.42.refs_11_.refs_12_), channel_id=1, source_target_pairs={{8,16},{16,8},{9,17},{17,9},{10,18},{18,10},{11,19},{19,11},{12,20... | collective-permute-start | bytes 1523720 | tf_op jit(solution)/shard_map/ppermute | solution.py:861
  110.1 1.4 collective-permute-start.18
  112.2 3.7 %collective-permute-start.19 = (f32[16,128]{1,0:T(8,128)S(1)}, f32[16,128]{1,0:T(8,128)S(1)}, u32[]{:S(2)}, u32[]{:S(2)}) collective-permute-start(f32[16,128]{1,0:T(8,128)S(1)} %pad_maximum_fusion.2), channel_id=1, source_target_pairs={{0,2},{1,3},{2,0},{3,1},{4,6},{5,7},{6,4},{7,5},{8,10},{9,11},{10,... | collective-permute-start | bytes 24584 | tf_op jit(solution)/shard_map/ppermute | solution.py:843
  116.5 3.7 %collective-permute-start.20 = (f32[32,128]{1,0:T(8,128)S(1)}, f32[32,128]{1,0:T(8,128)S(1)}, u32[]{:S(2)}, u32[]{:S(2)}) collective-permute-start(f32[32,128]{1,0:T(8,128)S(1)} %pad_maximum_fusion.1), channel_id=1, source_target_pairs={{0,4},{1,5},{2,6},{3,7},{4,0},{5,1},{6,2},{7,3},{8,12},{9,13},{10,... | collective-permute-start | bytes 49160 | tf_op jit(solution)/shard_map/ppermute | solution.py:843
Sparse Core Ops, SparseCore 0:
  11.7 92.5 all-gather.2

commit v2 on v1

--- a/solution.py
+++ b/solution.py
@@ -17,7 +17,7 @@
 REACH = 3
 DEEP = 3
 MICROSECOND = 3.0e6
-EXPECTED = dict(planes=4, gather=5, sweep=13, local_heads=5, solve=5, mix=4, update=4)
+EXPECTED = dict(planes=4, gather=6, sweep=13, local_heads=5, solve=5, mix=4, update=4)
 SLOT = 8
 SIDE = 2 * REACH + 1
 
@@ -460,20 +460,17 @@
     )(*operands)
 
 
-WAITS = {(1, 1): ("patches",), (2, 1): ("summed",)}
-CUTS = (35, 34, 33, 32)
+WAITS = {(1, 0): ("patches",), (2, 0): ("partial",)}
+CUTS = (None, None, None, None)
 ORDER = (
     "planes",
     "gather",
     (1, 0),
-    (1, 1),
     "local",
     (2, 0),
-    (2, 1),
     "solve",
+    "update",
     (3, 0),
-    (3, 1),
-    "update",
 )
 
 
@@ -500,32 +497,20 @@
     return lax.div(line, depth), lax.rem(line, depth), y
 
 
-def gather_kernel(spans, slabs, wells, rates, cells, head, storage, *refs):
-    parts = len(spans)
-    sides = (refs[:parts], refs[parts : 2 * parts])
-    outs = refs[2 * parts : 2 * parts + slabs]
-    forcing, field, picked, held_p, held_e, packed, sems, sem_out = refs[2 * parts + slabs :]
+def gather_kernel(slabs, wells, rates, cells, head, storage, own, *refs):
+    outs = refs[:slabs]
+    forcing, field, picked, held_p, held_e, packed, sems, sem_out = refs[slabs:]
     out = held_p
     planes, depth, across = head.shape
     members, lanes = picked.shape[2:]
-    odd, _, slab = spot()
+    _, _, slab = spot()
     step = 16
-    copies = {}
+    copies = []
     for b in range(depth // step):
-        for lo, hi in spans:
-            s, e = max(lo, b * step), min(hi, (b + 1) * step)
-            if s >= e:
-                continue
-            for side, plane in enumerate((1 - odd, odd)):
-                ref = sides[side][spans.index((lo, hi))]
-                batch = copies.setdefault(b, [])
-                copy = pltpu.make_async_copy(
-                    ref.at[pl.ds(s - lo, e - s)],
-                    field.at[plane, pl.ds(s, e - s)],
-                    sems.at[b, len(batch)],
-                )
-                copy.start()
-                batch.append(copy)
+        rows = pl.ds(b * step, step)
+        copy = pltpu.make_async_copy(own.at[:, rows], field.at[:, rows], sems.at[b])
+        copy.start()
+        copies.append(copy)
 
     forcing[...] = storage[...] * head[...]
     lane = lax.broadcasted_iota(jnp.int32, (1, across), 1)
@@ -558,9 +543,9 @@
                 here = zcol + (d - REACH) == depth_ids
                 line = jnp.sum(jnp.where(here, lines, 0.0), axis=0, keepdims=True)
                 held_e[i, d, pl.ds(a, 1), :] = line
+    results = []
     for b in range(depth // step):
-        for copy in copies[b]:
-            copy.wait()
+        copies[b].wait()
         some = pl.ds(step * b, step)
         for i in range(planes):
             rows = field[i, some].reshape(step * members, across)
@@ -590,7 +575,6 @@
                 p = pltpu.roll(held_p[i, d, :, tile], (128 - shift) % 128, 1)
                 e = pltpu.roll(held_e[i, d, :, tile], (192 - shift) % 128, 1)
                 packed[t, i, d] = jnp.where(first, p, e)
-    results = []
     for k in range(slabs):
         copy = pltpu.make_async_copy(packed.at[slab ^ k], outs[k], sem_out.at[k])
         copy.start()
@@ -599,36 +583,36 @@
         copy.wait()
 
 
-def gather_of(wells, rates, cells, head, storage, spans, slabs, side_a, side_b, after=()):
-    planes, depth, across = head.shape
-    members = side_a[0].shape[1]
+def gather_of(wells, rates, cells, head, storage, own, slabs, after=()):
+    planes, depth, members, across = own.shape
     lanes = cells.shape[0] * SLOT
     held = (planes, SIDE, members, lanes)
     packed = (planes, SIDE, members, 128)
     return call(
-        functools.partial(gather_kernel, spans, slabs),
+        functools.partial(gather_kernel, slabs),
         "gather",
-        [jax.ShapeDtypeStruct(packed, F32)] * slabs + [jax.ShapeDtypeStruct(head.shape, F32)],
-        [SMEM] * 3 + [VMEM] * 2 + [ANY] * (2 * len(spans)),
+        [jax.ShapeDtypeStruct(packed, F32)] * slabs
+        + [jax.ShapeDtypeStruct(head.shape, F32)],
+        [SMEM] * 3 + [VMEM] * 2 + [ANY],
         [ANY] * slabs + [VMEM],
         [
-            pltpu.VMEM((planes, depth, members, across), F32),
+            pltpu.VMEM(own.shape, F32),
             pltpu.VMEM((planes, depth, members, lanes), F32),
             pltpu.VMEM(held, F32),
             pltpu.VMEM(held, F32),
             pltpu.VMEM((slabs,) + packed, F32),
-            pltpu.SemaphoreType.DMA((depth // 16, 4)),
+            pltpu.SemaphoreType.DMA((depth // 16,)),
             pltpu.SemaphoreType.DMA((slabs,)),
         ],
         after=after,
-    )(wells, rates, cells, head, storage, *side_a, *side_b)
-
-
-def local_kernel(nz, ny, nobs, slabs, cells, perturb, *refs):
+    )(wells, rates, cells, head, storage, own)
+
+
+def local_kernel(nz, ny, nobs, slabs, peers, cells, *refs):
     blocks = refs[:slabs]
     out, R, RM, RP, H, HM, HP, ST, FO, W, NEW = refs[slabs:]
     members, lanes = R.shape[2:]
-    _, _, slab = spot()
+    _, block, slab = spot()
     share = nobs // slabs
     x0, zcol, ycol = columns_of(cells, slab * share, share, 64, lanes, nz, ny)
 
@@ -649,7 +633,7 @@
                 both = jnp.where(masks[g], blocks[g // 2][g % 2, d], both)
             perm = both
             rest = pltpu.roll(both, 64, 1)
-            r = jnp.where(inside, recip(perm), jnp.inf)
+            r = jnp.where(inside, jnp.exp(-perm), jnp.inf)
             spread(R, RM, RP, i, d, r)
             head = jnp.broadcast_to(jnp.where(inside, rest[0:1], 0.0), (members, lanes))
             spread(H, HM, HP, i, d, head)
@@ -698,36 +682,48 @@
                 spread(H, HM, HP, i, d, NEW[i, d])
     final = update(REACH, REACH, False)
     lane = lax.broadcasted_iota(jnp.int32, (lanes, 128), 0)
-    target = lax.broadcasted_iota(jnp.int32, (lanes, 128), 1) - slab * share
+    target = lax.broadcasted_iota(jnp.int32, (lanes, 128), 1) - block * (128 // peers)
     onehot = (lane == target * SLOT + REACH) & (target >= 0) & (target < share)
-    observed = exact_pick(final, jnp.where(onehot, 1.0, 0.0).astype(jnp.bfloat16))
-    rest = jnp.zeros((members, 128 - 2 * nobs), F32)
-    part = perturb[...] * (1.0 / slabs)
-    out[...] = jnp.concatenate([observed[:, :nobs], part, rest], 1)
-
-
-def local_of(nz, ny, cells, perturb, blocks, after=()):
+    out[...] = exact_pick(final, jnp.where(onehot, 1.0, 0.0).astype(jnp.bfloat16))
+
+
+def local_of(nz, ny, cells, peers, blocks, after=()):
     nobs = cells.shape[0]
     lanes = 128
-    members = perturb.shape[0]
+    members = blocks[0].shape[2]
     slabs = len(blocks)
     full = pltpu.VMEM((SIDE, SIDE, members, lanes), F32)
     line = pltpu.VMEM((SIDE, SIDE, 1, lanes), F32)
     return call(
-        functools.partial(local_kernel, nz, ny, nobs, slabs),
+        functools.partial(local_kernel, nz, ny, nobs, slabs, peers),
         "local_heads",
         jax.ShapeDtypeStruct((members, 128), F32),
-        [SMEM] + [VMEM] * (1 + slabs),
+        [SMEM] + [VMEM] * slabs,
         VMEM,
         [full] * 6 + [line] * 2 + [full] * 2,
         after=after,
-    )(cells, perturb, *blocks)
-
-
-def solve_kernel(nobs, peers, values, noise, step, seen, out, aug):
-    every = seen[...]
-    total = every.shape[0]
-    heads = every[:, :nobs]
+    )(cells, *blocks)
+
+
+def solve_kernel(nobs, peers, values, noise, step, perturb, *refs):
+    *seen, out, aug = refs
+    _, block, slab = spot()
+    members = perturb.shape[0]
+    total = peers * members
+    width = 128 // peers
+    share = nobs // len(seen)
+    row = lax.broadcasted_iota(jnp.int32, (total, 128), 0)
+    lane = lax.broadcasted_iota(jnp.int32, (total, 128), 1)
+    mine = lax.div(row, members) == lax.div(lane, width)
+    source = lax.broadcasted_iota(jnp.int32, (128, nobs), 0)
+    target = lax.broadcasted_iota(jnp.int32, (128, nobs), 1)
+    spot_of = lax.rem(source, width)
+    heads = jnp.zeros((total, nobs), F32)
+    for k, ref in enumerate(seen):
+        line = jnp.where(mine, jnp.concatenate([ref[...]] * peers, 0), 0.0)
+        onehot = (spot_of < share) & (target == (slab ^ k) * share + spot_of)
+        heads = heads + exact_pick(line, jnp.where(onehot, 1.0, 0.0).astype(jnp.bfloat16))
+    aug[pl.ds(0, total), pl.ds(0, nobs)] = heads
     mean = jnp.sum(heads, axis=0, keepdims=True) * (1.0 / total)
     dev = heads - mean
     contract = (((0,), (0,)), ((), ()))
@@ -742,34 +738,33 @@
     for k in range(nobs):
         pivot = work[k : k + 1, :] * (1.0 / work[k : k + 1, k : k + 1])
         work = jnp.where(line == k, pivot, work - work[:, k : k + 1] * pivot)
-    aug[...] = work
-    inverse = aug[:, pl.ds(nobs, nobs)]
-    mine = every[: every.shape[0] // peers]
-    residual = values[...] + mine[:, nobs : 2 * nobs] - mine[:, :nobs]
+    own = aug[pl.ds(pl.multiple_of(block * members, members), members), pl.ds(0, nobs)]
+    inverse = work[:, nobs:]
+    residual = values[...] + perturb[...] - own
     gain = jnp.dot(residual, inverse, precision=HIGHEST, preferred_element_type=F32)
     nt = (((1,), (1,)), ((), ()))
     mixing = lax.dot_general(gain, dev, nt, precision=HIGHEST, preferred_element_type=F32)
     out[...] = mixing * (1.0 / (total - 1))
 
 
-def solve_of(seen, peers, values, noise, step, after=()):
+def solve_of(seen, peers, values, noise, step, perturb, after=()):
     nobs = values.shape[0]
-    total = seen.shape[0]
+    members = perturb.shape[0]
+    total = members * peers
     return call(
         functools.partial(solve_kernel, nobs, peers),
         "solve",
-        jax.ShapeDtypeStruct((total // peers, total), F32),
-        [VMEM, VMEM, SMEM, VMEM],
+        jax.ShapeDtypeStruct((members, total), F32),
+        [VMEM, VMEM, SMEM] + [VMEM] * (1 + len(seen)),
         VMEM,
-        [pltpu.VMEM((nobs, 2 * nobs), F32)],
+        [pltpu.VMEM((total, 128), F32)],
         after=after,
-    )(values[None], noise[None], step, seen)
+    )(values[None], noise[None], step, perturb, *seen)
 
 
 def update_kernel(step, mixing, lp, every, out, x, a, sem_lp, sem_in, sem_out):
     members, planes, depth, across = lp.shape
     peers = every.shape[0]
-    _, me, _ = spot()
     blocks = [(b, i) for b in range(depth // step) for i in range(planes)]
     ahead = a.shape[0]
     ins, outs, fields = [], [], []
@@ -799,7 +794,7 @@
         for g in range(step // 8):
             lines = []
             for z in range(8 * g, 8 * g + 8):
-                f = jnp.concatenate([a[n % ahead, me ^ k, z] for k in range(peers)], 0)
+                f = jnp.concatenate([a[n % ahead, k, z] for k in range(peers)], 0)
                 top = f.astype(jnp.bfloat16)
                 low = (f - top.astype(F32)).astype(jnp.bfloat16)
                 both = jnp.concatenate([top, low], 0)
@@ -847,15 +842,6 @@
     return [parts[0]] + [swap(parts[k], axis, k) for k in range(1, lax.axis_size(axis))]
 
 
-def gather_by_swaps(x, axis, token):
-    x = lax.optimization_barrier((x, *token))[0]
-    bit = 1
-    while bit < lax.axis_size(axis):
-        x = jnp.concatenate([x, swap(x, axis, bit)], 0)
-        bit *= 2
-    return x
-
-
 def halo(x, side):
     pairs = [(i, i + 1) for i in range(side, lax.axis_size("space") - 1, 2)]
     return lax.ppermute(x, "space", pairs + [(b, a) for a, b in pairs])
@@ -877,7 +863,6 @@
     members, planes, depth, across = shape
     slabs = lax.axis_size("space")
     peers = lax.axis_size("ens")
-    spans = row_spans(depth, CUTS[0])
     names = ("a", "b", "ra", "rb")
     state = {"token": ()}
 
@@ -889,45 +874,35 @@
 
     def planes_step():
         side_a, side_b, own = planes_of(log_perm, head_init, CUTS[0])
-        state["a"], state["b"], state["own"] = side_a, side_b, own
         far_a = [halo(x, 0) for x in side_a]
         far_b = [halo(x, 1) for x in side_b]
-        state["far"] = [v for v in zip(far_a, far_b)]
         sides = (side_a, side_b, far_a, far_b)
         state["perms"] = {("p", n): span(v, CUTS[0]) for n, v in zip(names, sides)}
         state["new"] = {1: [], 2: []}
+        state["own"] = own
         state["every"] = lax.all_gather(own, "ens", axis=0)
-        after(own)
 
     def gather_step():
         *patch, state["forcing"] = gather_of(
-            well_cells,
-            well_rates,
-            obs_cells,
-            head_init,
-            storage,
-            spans,
-            slabs,
-            state["a"],
-            state["b"],
-            after=state["token"],
+            well_cells, well_rates, obs_cells, head_init, storage, state["own"], slabs
         )
         state["patches"] = swaps(patch, "space")
         after(patch[0])
 
     def local_step():
         seen = local_of(
-            depth, across, obs_cells, perturb, state["patches"], after=state["token"]
+            depth, across, obs_cells, peers, state["patches"], after=state["token"]
         )
-        state["local"] = seen
-        seen = sum(swaps([seen] * slabs, "space"))
-        state["summed"] = [seen]
-        after(state["local"])
+        after(seen)
+        bit = 1
+        while bit < peers:
+            seen = seen + swap(seen, "ens", bit)
+            bit *= 2
+        state["partial"] = swaps([seen] * slabs, "space")
 
     def solve_step():
-        seen = gather_by_swaps(state["summed"][0], "ens", state["token"])
         state["mixing"] = solve_of(
-            seen, peers, obs_values, noise_var, step_size, after=state["token"]
+            state["partial"], peers, obs_values, noise_var, step_size, perturb, after=state["token"]
         )
         after(state["mixing"])
 

time: 159 us -> 143 us (0.90)
  starting transfers between devices: 44.1 us -> 23.8 us
  waiting for transfers between devices: 18.2 us -> 37.9 us
  Pallas kernels: 77.4 us -> 63.8 us
  other arithmetic: 3.96 us -> 0.69 us
    ppermute x9, waiting for transfers between devices: 15.1 us -> 33.2 us  [swap(): lax.ppermute(x, axis, [(i, i ^ bit) for i in range(lax.axis_size(axis))])]
    ppermute x12 -> x6, starting transfers between devices: 27.4 us -> 10.5 us  [halo(): return lax.ppermute(x, 'space', pairs + [(b, a) for a, b in pairs])]
    pallas_call x6 -> x3, Pallas kernels: 48.7 us -> 35.2 us  [sweep_of(): call(functools.partial(sweep_kernel, cfg), 'sweep', out_shape, [ANY] * le...]
    ppermute x9, starting transfers between devices: 16.7 us -> 13.3 us  [swap(): lax.ppermute(x, axis, [(i, i ^ bit) for i in range(lax.axis_size(axis))])]
    concatenate x3 -> x0, other arithmetic: 2.67 us -> none  [gather_by_swaps(): x = jnp.concatenate([x, swap(x, axis, bit)], 0)]
    ppermute x12 -> x6, waiting for transfers between devices: 3.07 us -> 4.66 us  [halo(): return lax.ppermute(x, 'space', pairs + [(b, a) for a, b in pairs])]
  transfers between devices with their start and end apart: 22 -> 16, of which waited for: 6 -> 8; matrix products, arithmetic and copies ran while one was open for 2% -> 0% of each run, Pallas kernels for 40% -> 34%
where the time goes in v2:
time: 143 us; the launch traced here: 142 us
  Pallas kernels  63.8 us (45%)
  waiting for transfers between devices  37.9 us (27%)
  starting transfers between devices  23.8 us (17%)
  between operations  14.8 us (10%)
    pallas_call x3, Pallas kernels, sweep_of(): call(functools.partial(sweep_kernel, cfg), 'sweep', out_shape, [ANY] * le...  35.2 us
    ppermute x9, waiting for transfers between devices, swap(): lax.ppermute(x, axis, [(i, i ^ bit) for i in range(lax.axis_size(axis))])  33.2 us
    ppermute x9, starting transfers between devices, swap(): lax.ppermute(x, axis, [(i, i ^ bit) for i in range(lax.axis_size(axis))])  13.3 us
    ppermute x6, starting transfers between devices, halo(): return lax.ppermute(x, 'space', pairs + [(b, a) for a, b in pairs])  10.5 us
    pallas_call x1, Pallas kernels, update_of(): call(functools.partial(update_kernel, step), 'update', jax.ShapeDtypeStru...  9.13 us
    pallas_call x1, Pallas kernels, gather_of(): call(functools.partial(gather_kernel, slabs), 'gather', [jax.ShapeDtypeSt...  6.46 us
    pallas_call x1, Pallas kernels, solve_of(): call(functools.partial(solve_kernel, nobs, peers), 'solve', jax.ShapeDtyp...  5.02 us
    ppermute x6, waiting for transfers between devices, halo(): return lax.ppermute(x, 'space', pairs + [(b, a) for a, b in pairs])  4.66 us
  transfers between devices with their start and end apart: 16, of which 8 were waited for; matrix products, arithmetic and copies ran while one was open for 0% of the time, Pallas kernels for 34%

profile of v2, /device:TPU:0, one launch (start us, length us, event | category | flops | bytes accessed | tf_op | source)
XLA Modules:
  0.0 141.6 jit_solution(2728005355968996422)
XLA Ops:
  7.2 4.3 %planes.1 = (f32[72,8,512]{2,1,0:T(8,128)}, f32[72,8,512]{2,1,0:T(8,128)}, f32[2,64,8,512]{3,2,1,0:T(8,128)}) custom-call(f32[8,2,64,512]{3,2,1,0:T(8,128)} %refs_2_.3, f32[2,64,512]{2,1,0:T(8,128)} %refs_7_.1), custom_call_target="tpu_custom_call" | custom-call | bytes 12000000 | tf_op jit(solution)/shard_map/planes/pallas_call | solution.py:126
  11.6 3.1 %collective-permute-start.3 = (f32[72,8,512]{2,1,0:T(8,128)}, f32[72,8,512]{2,1,0:T(8,128)}, u32[]{:S(2)}, u32[]{:S(2)}) collective-permute-start(f32[72,8,512]{2,1,0:T(8,128)} %get-tuple-element.21.refs_8_.refs_6_.refs_2_), channel_id=1, source_target_pairs={{0,8},{16,24},{8,0},{24,16},{1,9},{17,25},{9,1},{25,17},{2,10},{18... | collective-permute-start | bytes 3538952 | tf_op jit(solution)/shard_map/ppermute | solution.py:847
  14.7 1.7 %collective-permute-start.4 = (f32[72,8,512]{2,1,0:T(8,128)}, f32[72,8,512]{2,1,0:T(8,128)}, u32[]{:S(2)}, u32[]{:S(2)}) collective-permute-start(f32[72,8,512]{2,1,0:T(8,128)} %get-tuple-element.22.refs_9_.refs_7_.refs_3_), channel_id=1, source_target_pairs={{8,16},{16,8},{9,17},{17,9},{10,18},{18,10},{11,19},{19,11},{12,20... | collective-permute-start | bytes 3538952 | tf_op jit(solution)/shard_map/ppermute | solution.py:847
  16.4 6.5 %gather.1 = (f32[2,7,8,128]{3,2,1,0:T(8,128)}, f32[2,7,8,128]{3,2,1,0:T(8,128)}, f32[2,7,8,128]{3,2,1,0:T(8,128)}, f32[2,7,8,128]{3,2,1,0:T(8,128)}, f32[2,64,512]{2,1,0:T(8,128)}) custom-call(s32[16]{0:T(128)} %refs_0_.3, f32[16]{0:T(128)} %refs_1_.4, s32[32]{0:T(128)} %refs_1_.5, f32[2,64,512]{2,1,0:T(8,128)} %refs_7_.1, f32[2,64,512]{2,1,0:T(8,128)} %refs_6_.1, ...), custom_call_target="tpu_custom_call" | custom-call | bytes 18000000 | tf_op jit(solution)/shard_map/gather/pallas_call | solution.py:591
  22.8 3.4 %collective-permute-start = (f32[2,7,8,128]{3,2,1,0:T(8,128)}, f32[2,7,8,128]{3,2,1,0:T(8,128)}, u32[]{:S(2)}, u32[]{:S(2)}) collective-permute-start(f32[2,7,8,128]{3,2,1,0:T(8,128)} %get-tuple-element.17), channel_id=1, source_target_pairs={{0,8},{8,0},{16,24},{24,16},{1,9},{9,1},{17,25},{25,17},{2,10},{10... | collective-permute-start | bytes 172040 | tf_op jit(solution)/shard_map/ppermute | solution.py:838
  26.3 2.4 %collective-permute-start.2 = (f32[2,7,8,128]{3,2,1,0:T(8,128)}, f32[2,7,8,128]{3,2,1,0:T(8,128)}, u32[]{:S(2)}, u32[]{:S(2)}) collective-permute-start(f32[2,7,8,128]{3,2,1,0:T(8,128)} %get-tuple-element.19), channel_id=1, source_target_pairs={{0,24},{8,16},{16,8},{24,0},{1,25},{9,17},{17,9},{25,1},{2,26},{10... | collective-permute-start | bytes 172040 | tf_op jit(solution)/shard_map/ppermute | solution.py:838
  28.7 13.9 %collective-permute-done.refs_2_.refs_3_ = f32[2,7,8,128]{3,2,1,0:T(8,128)} collective-permute-done((f32[2,7,8,128]{3,2,1,0:T(8,128)}, f32[2,7,8,128]{3,2,1,0:T(8,128)}, u32[]{:S(2)}, u32[]{:S(2)}) %collective-permute-start) | collective-permute-done | bytes 57376 | tf_op jit(solution)/shard_map/ppermute | solution.py:838
  42.6 6.9 %collective-permute-done.1.refs_3_.refs_4_ = f32[2,7,8,128]{3,2,1,0:T(8,128)} collective-permute-done((f32[2,7,8,128]{3,2,1,0:T(8,128)}, f32[2,7,8,128]{3,2,1,0:T(8,128)}, u32[]{:S(2)}, u32[]{:S(2)}) %collective-permute-start.1) | collective-permute-done | bytes 57376 | tf_op jit(solution)/shard_map/ppermute | solution.py:838
  49.5 12.9 %sweep.3 = (f32[64,8,512]{2,1,0:T(8,128)}, f32[64,8,512]{2,1,0:T(8,128)}, f32[2,64,8,512]{3,2,1,0:T(8,128)}) custom-call(f32[2,7,8,128]{3,2,1,0:T(8,128)} %get-tuple-element.16.refs_0_.refs_1_.refs_2_, f32[2,7,8,128]{3,2,1,0:T(8,128)} %get-tuple-element.16.refs_0_.refs_1_.refs_2_, f32[2,7,8,128]{3,2,1,0:T(8,128)} %collective-permute-done.refs_2_.refs_3_, ...), custom_call_target="tpu_custom_call" | custom-call | bytes 39000000 | tf_op jit(solution)/shard_map/sweep/pallas_call | solution.py:451
  63.6 1.6 %collective-permute-start.12 = (f32[64,8,512]{2,1,0:T(8,128)}, f32[64,8,512]{2,1,0:T(8,128)}, u32[]{:S(2)}, u32[]{:S(2)}) collective-permute-start(f32[64,8,512]{2,1,0:T(8,128)} %get-tuple-element.24.refs_11_), channel_id=1, source_target_pairs={{8,16},{16,8},{9,17},{17,9},{10,18},{18,10},{11,19},{19,11},{12,20... | collective-permute-start | bytes 3145736 | tf_op jit(solution)/shard_map/ppermute | solution.py:847
  65.2 3.7 %local_heads.1.refs_0_ = f32[8,128]{1,0:T(8,128)} custom-call(f32[64,8,512]{2,1,0:T(8,128)} %get-tuple-element.23.refs_0_.refs_10_, s32[32]{0:T(128)} %refs_1_.5, f32[2,7,8,128]{3,2,1,0:T(8,128)} %get-tuple-element.16.refs_0_.refs_1_.refs_2_, f32[2,7,8,128]{3,2,1,0:T(8,128)} %collective-permute-done.refs_2_.refs_3_, ...), custom_call_target="tpu_custom_call" | custom-call | bytes 15000000 | tf_op jit(solution)/shard_map/local_heads/pallas_call | solution.py:697
  68.9 1.4 collective-permute-done.5
  71.0 1.5 %collective-permute-start.6 = (f32[8,128]{1,0:T(8,128)S(1)}, f32[8,128]{1,0:T(8,128)S(1)}, u32[]{:S(2)}, u32[]{:S(2)}) collective-permute-start(f32[8,128]{1,0:T(8,128)S(1)} %add.9), channel_id=1, source_target_pairs={{0,2},{1,3},{2,0},{3,1},{4,6},{5,7},{6,4},{7,5},{8,10},{9,11},{10,... | collective-permute-start | bytes 12296 | tf_op jit(solution)/shard_map/ppermute | solution.py:838
  72.5 2.2 %collective-permute-done.6 = f32[8,128]{1,0:T(8,128)S(1)} collective-permute-done((f32[8,128]{1,0:T(8,128)S(1)}, f32[8,128]{1,0:T(8,128)S(1)}, u32[]{:S(2)}, u32[]{:S(2)}) %collective-permute-start.6) | collective-permute-done | bytes 4128 | tf_op jit(solution)/shard_map/ppermute | solution.py:838
  74.6 1.5 %collective-permute-start.7 = (f32[8,128]{1,0:T(8,128)S(1)}, f32[8,128]{1,0:T(8,128)S(1)}, u32[]{:S(2)}, u32[]{:S(2)}) collective-permute-start(f32[8,128]{1,0:T(8,128)S(1)} %add.10), channel_id=1, source_target_pairs={{0,4},{1,5},{2,6},{3,7},{4,0},{5,1},{6,2},{7,3},{8,12},{9,13},{10,... | collective-permute-start | bytes 12296 | tf_op jit(solution)/shard_map/ppermute | solution.py:838
  76.2 2.1 %collective-permute-done.7 = f32[8,128]{1,0:T(8,128)S(1)} collective-permute-done((f32[8,128]{1,0:T(8,128)S(1)}, f32[8,128]{1,0:T(8,128)S(1)}, u32[]{:S(2)}, u32[]{:S(2)}) %collective-permute-start.7) | collective-permute-done | bytes 4128 | tf_op jit(solution)/shard_map/ppermute | solution.py:838
  78.3 2.6 %collective-permute-start.10 = (f32[8,128]{1,0:T(8,128)S(1)}, f32[8,128]{1,0:T(8,128)S(1)}, u32[]{:S(2)}, u32[]{:S(2)}) collective-permute-start(f32[8,128]{1,0:T(8,128)S(1)} %add.11.refs_1_.refs_5_), channel_id=1, source_target_pairs={{0,24},{8,16},{16,8},{24,0},{1,25},{9,17},{17,9},{25,1},{2,26},{10... | collective-permute-start | bytes 12296 | tf_op jit(solution)/shard_map/ppermute | solution.py:838
  82.7 5.7 %collective-permute-done.10.refs_4_.refs_8_ = f32[8,128]{1,0:T(8,128)S(1)} collective-permute-done((f32[8,128]{1,0:T(8,128)S(1)}, f32[8,128]{1,0:T(8,128)S(1)}, u32[]{:S(2)}, u32[]{:S(2)}) %collective-permute-start.10) | collective-permute-done | bytes 4128 | tf_op jit(solution)/shard_map/ppermute | solution.py:838
  90.1 10.9 %sweep.4 = (f32[64,8,512]{2,1,0:T(8,128)}, f32[64,8,512]{2,1,0:T(8,128)}) custom-call(f32[8,128]{1,0:T(8,128)} %local_heads.1.refs_0_, f32[8,128]{1,0:T(8,128)} %copy-done, f32[8,128]{1,0:T(8,128)} %copy-done.2, f32[8,128]{1,0:T(8,128)} %copy-done.3, f32[8,128]{1,0:T(8,128)} %copy-done.1, f32[2,64,512]{2,1,0:T(8,128)} %get-tuple-element.20.refs_5_.refs_1_.refs_11_, ...), custom_call_target="tpu_custom_call" | custom-call | bytes 39000000 | tf_op jit(solution)/shard_map/sweep/pallas_call | solution.py:451
  102.2 1.6 %collective-permute-start.14 = (f32[64,8,512]{2,1,0:T(8,128)}, f32[64,8,512]{2,1,0:T(8,128)}, u32[]{:S(2)}, u32[]{:S(2)}) collective-permute-start(f32[64,8,512]{2,1,0:T(8,128)} %get-tuple-element.27.refs_7_), channel_id=1, source_target_pairs={{8,16},{16,8},{9,17},{17,9},{10,18},{18,10},{11,19},{19,11},{12,20... | collective-permute-start | bytes 3145736 | tf_op jit(solution)/shard_map/ppermute | solution.py:847
  104.5 5.0 %solve.1.refs_0_.refs_1_ = f32[8,64]{1,0:T(8,128)} custom-call(f32[64,8,512]{2,1,0:T(8,128)} %get-tuple-element.26.refs_0_.refs_6_, f32[1,32]{1,0:T(1,128)} %bitcast.4, f32[1,32]{1,0:T(1,128)} %bitcast.5, f32[1]{0:T(128)S(6)} %copy.12.refs_3_, f32[8,32]{1,0:T(8,128)} %refs_4_.3, f32[8,128]{1,0:T(8,128)} %copy-done, f32[8,128]{1,0:T(8,128)} %copy-done.2, ...), custom_call_target="tpu_custom_call" | custom-call | bytes 15000000 | tf_op jit(solution)/shard_map/solve/pallas_call | solution.py:754
  109.5 9.1 %update.1.refs_0_ = f32[8,2,64,512]{3,2,1,0:T(8,128)} custom-call(f32[8,64]{1,0:T(8,128)} %solve.1.refs_0_.refs_1_, f32[8,64]{1,0:T(8,128)} %solve.1.refs_0_.refs_1_, f32[8,2,64,512]{3,2,1,0:T(8,128)} %refs_2_.3, f32[8,2,64,8,512]{4,3,2,1,0:T(8,128)} %bitcast.3), custom_call_target="tpu_custom_call" | custom-call | bytes 12000000 | tf_op jit(solution)/shard_map/update/pallas_call | solution.py:820
  118.7 4.7 %collective-permute-done.13.refs_8_ = f32[64,8,512]{2,1,0:T(8,128)} collective-permute-done((f32[64,8,512]{2,1,0:T(8,128)}, f32[64,8,512]{2,1,0:T(8,128)}, u32[]{:S(2)}, u32[]{:S(2)}) %collective-permute-start.13) | collective-permute-done | bytes 1048608 | tf_op jit(solution)/shard_map/ppermute | solution.py:847
  123.3 11.4 %sweep.5 = f32[8,2,64,512]{3,2,1,0:T(8,128)} custom-call(f32[8,2,64,512]{3,2,1,0:T(8,128)} %update.1.refs_0_, f32[2,64,512]{2,1,0:T(8,128)} %get-tuple-element.20.refs_5_.refs_1_.refs_11_, f32[72,8,512]{2,1,0:T(8,128)} %get-tuple-element.21.refs_8_.refs_6_.refs_2_, f32[72,8,512]{2,1,0:T(8,128)} %get-tuple-element.22.refs_9_.refs_7_.refs_3_, ...), custom_call_target="tpu_custom_call" | custom-call | bytes 39000000 | tf_op jit(solution)/shard_map/sweep/pallas_call | solution.py:451
  (28 shorter events, 6.7 us)
Async XLA Ops:
  7.2 102.4 %all-gather.3.cloned.1.call-start = ((), (), s32[]{:S(2)}) async-start(), calls=%async_computation | async-start | bytes 18874368 | tf_op jit(solution)/shard_map/all_gather | solution.py:883
  11.6 37.9 %collective-permute-start.3 = (f32[72,8,512]{2,1,0:T(8,128)}, f32[72,8,512]{2,1,0:T(8,128)}, u32[]{:S(2)}, u32[]{:S(2)}) collective-permute-start(f32[72,8,512]{2,1,0:T(8,128)} %get-tuple-element.21.refs_8_.refs_6_.refs_2_), channel_id=1, source_target_pairs={{0,8},{16,24},{8,0},{24,16},{1,9},{17,25},{9,1},{25,17},{2,10},{18... | collective-permute-start | bytes 3538952 | tf_op jit(solution)/shard_map/ppermute | solution.py:847
  14.7 34.8 %collective-permute-start.4 = (f32[72,8,512]{2,1,0:T(8,128)}, f32[72,8,512]{2,1,0:T(8,128)}, u32[]{:S(2)}, u32[]{:S(2)}) collective-permute-start(f32[72,8,512]{2,1,0:T(8,128)} %get-tuple-element.22.refs_9_.refs_7_.refs_3_), channel_id=1, source_target_pairs={{8,16},{16,8},{9,17},{17,9},{10,18},{18,10},{11,19},{19,11},{12,20... | collective-permute-start | bytes 3538952 | tf_op jit(solution)/shard_map/ppermute | solution.py:847
  22.8 19.7 %collective-permute-start = (f32[2,7,8,128]{3,2,1,0:T(8,128)}, f32[2,7,8,128]{3,2,1,0:T(8,128)}, u32[]{:S(2)}, u32[]{:S(2)}) collective-permute-start(f32[2,7,8,128]{3,2,1,0:T(8,128)} %get-tuple-element.17), channel_id=1, source_target_pairs={{0,8},{8,0},{16,24},{24,16},{1,9},{9,1},{17,25},{25,17},{2,10},{10... | collective-permute-start | bytes 172040 | tf_op jit(solution)/shard_map/ppermute | solution.py:838
  26.3 23.2 %collective-permute-start.1 = (f32[2,7,8,128]{3,2,1,0:T(8,128)}, f32[2,7,8,128]{3,2,1,0:T(8,128)}, u32[]{:S(2)}, u32[]{:S(2)}) collective-permute-start(f32[2,7,8,128]{3,2,1,0:T(8,128)} %get-tuple-element.18), channel_id=1, source_target_pairs={{0,16},{8,24},{16,0},{24,8},{1,17},{9,25},{17,1},{25,9},{2,18},{10... | collective-permute-start | bytes 172040 | tf_op jit(solution)/shard_map/ppermute | solution.py:838
  26.3 23.2 %collective-permute-start.2 = (f32[2,7,8,128]{3,2,1,0:T(8,128)}, f32[2,7,8,128]{3,2,1,0:T(8,128)}, u32[]{:S(2)}, u32[]{:S(2)}) collective-permute-start(f32[2,7,8,128]{3,2,1,0:T(8,128)} %get-tuple-element.19), channel_id=1, source_target_pairs={{0,24},{8,16},{16,8},{24,0},{1,25},{9,17},{17,9},{25,1},{2,26},{10... | collective-permute-start | bytes 172040 | tf_op jit(solution)/shard_map/ppermute | solution.py:838
  62.3 27.2 %collective-permute-start.11 = (f32[64,8,512]{2,1,0:T(8,128)}, f32[64,8,512]{2,1,0:T(8,128)}, u32[]{:S(2)}, u32[]{:S(2)}) collective-permute-start(f32[64,8,512]{2,1,0:T(8,128)} %get-tuple-element.23.refs_0_.refs_10_), channel_id=1, source_target_pairs={{0,8},{16,24},{8,0},{24,16},{1,9},{17,25},{9,1},{25,17},{2,10},{18... | collective-permute-start | bytes 3145736 | tf_op jit(solution)/shard_map/ppermute | solution.py:847
  63.6 26.0 %collective-permute-start.12 = (f32[64,8,512]{2,1,0:T(8,128)}, f32[64,8,512]{2,1,0:T(8,128)}, u32[]{:S(2)}, u32[]{:S(2)}) collective-permute-start(f32[64,8,512]{2,1,0:T(8,128)} %get-tuple-element.24.refs_11_), channel_id=1, source_target_pairs={{8,16},{16,8},{9,17},{17,9},{10,18},{18,10},{11,19},{19,11},{12,20... | collective-permute-start | bytes 3145736 | tf_op jit(solution)/shard_map/ppermute | solution.py:847
  68.9 1.4 collective-permute-start.5
  71.0 3.7 %collective-permute-start.6 = (f32[8,128]{1,0:T(8,128)S(1)}, f32[8,128]{1,0:T(8,128)S(1)}, u32[]{:S(2)}, u32[]{:S(2)}) collective-permute-start(f32[8,128]{1,0:T(8,128)S(1)} %add.9), channel_id=1, source_target_pairs={{0,2},{1,3},{2,0},{3,1},{4,6},{5,7},{6,4},{7,5},{8,10},{9,11},{10,... | collective-permute-start | bytes 12296 | tf_op jit(solution)/shard_map/ppermute | solution.py:838
  74.6 3.7 %collective-permute-start.7 = (f32[8,128]{1,0:T(8,128)S(1)}, f32[8,128]{1,0:T(8,128)S(1)}, u32[]{:S(2)}, u32[]{:S(2)}) collective-permute-start(f32[8,128]{1,0:T(8,128)S(1)} %add.10), channel_id=1, source_target_pairs={{0,4},{1,5},{2,6},{3,7},{4,0},{5,1},{6,2},{7,3},{8,12},{9,13},{10,... | collective-permute-start | bytes 12296 | tf_op jit(solution)/shard_map/ppermute | solution.py:838
  78.3 3.2 %copy-start = (f32[8,128]{1,0:T(8,128)}, f32[8,128]{1,0:T(8,128)S(1)}, u32[]{:S(2)}) copy-start(f32[8,128]{1,0:T(8,128)S(1)} %add.11.refs_1_.refs_5_) | copy-start | bytes 12292
  78.3 10.1 %collective-permute-start.10 = (f32[8,128]{1,0:T(8,128)S(1)}, f32[8,128]{1,0:T(8,128)S(1)}, u32[]{:S(2)}, u32[]{:S(2)}) collective-permute-start(f32[8,128]{1,0:T(8,128)S(1)} %add.11.refs_1_.refs_5_), channel_id=1, source_target_pairs={{0,24},{8,16},{16,8},{24,0},{1,25},{9,17},{17,9},{25,1},{2,26},{10... | collective-permute-start | bytes 12296 | tf_op jit(solution)/shard_map/ppermute | solution.py:838
  80.9 7.4 %collective-permute-start.8 = (f32[8,128]{1,0:T(8,128)S(1)}, f32[8,128]{1,0:T(8,128)S(1)}, u32[]{:S(2)}, u32[]{:S(2)}) collective-permute-start(f32[8,128]{1,0:T(8,128)S(1)} %add.11.refs_1_.refs_5_), channel_id=1, source_target_pairs={{0,8},{8,0},{16,24},{24,16},{1,9},{9,1},{17,25},{25,17},{2,10},{10... | collective-permute-start | bytes 12296 | tf_op jit(solution)/shard_map/ppermute | solution.py:838
  81.5 8.0 %collective-permute-start.9 = (f32[8,128]{1,0:T(8,128)S(1)}, f32[8,128]{1,0:T(8,128)S(1)}, u32[]{:S(2)}, u32[]{:S(2)}) collective-permute-start(f32[8,128]{1,0:T(8,128)S(1)} %add.11.refs_1_.refs_5_), channel_id=1, source_target_pairs={{0,16},{8,24},{16,0},{24,8},{1,17},{9,25},{17,1},{25,9},{2,18},{10... | collective-permute-start | bytes 12296 | tf_op jit(solution)/shard_map/ppermute | solution.py:838
  88.4 1.1 copy-start.1
  88.4 1.1 copy-start.2
  89.5 0.6 copy-start.3
  101.0 22.3 %collective-permute-start.13 = (f32[64,8,512]{2,1,0:T(8,128)}, f32[64,8,512]{2,1,0:T(8,128)}, u32[]{:S(2)}, u32[]{:S(2)}) collective-permute-start(f32[64,8,512]{2,1,0:T(8,128)} %get-tuple-element.26.refs_0_.refs_6_), channel_id=1, source_target_pairs={{0,8},{16,24},{8,0},{24,16},{1,9},{17,25},{9,1},{25,17},{2,10},{18... | collective-permute-start | bytes 3145736 | tf_op jit(solution)/shard_map/ppermute | solution.py:847
  102.2 21.1 %collective-permute-start.14 = (f32[64,8,512]{2,1,0:T(8,128)}, f32[64,8,512]{2,1,0:T(8,128)}, u32[]{:S(2)}, u32[]{:S(2)}) collective-permute-start(f32[64,8,512]{2,1,0:T(8,128)} %get-tuple-element.27.refs_7_), channel_id=1, source_target_pairs={{8,16},{16,8},{9,17},{17,9},{10,18},{18,10},{11,19},{19,11},{12,20... | collective-permute-start | bytes 3145736 | tf_op jit(solution)/shard_map/ppermute | solution.py:847
Sparse Core Ops, SparseCore 0:
  11.7 92.6 all-gather.2

commit v3 on v2

--- a/solution.py
+++ b/solution.py
@@ -143,17 +143,24 @@
 
 
 def sweep_kernel(cfg, *refs):
-    first, last, za, zb, depth, members, across, pieces = cfg
+    mode, first, last, za, zb, depth, members, across, pieces = cfg
+    pre, post = mode == "pre", mode == "post"
     refs = list(refs)
     odd, _, _ = spot()
-    lines = {"f": refs.pop(0)}
+    lines = {}
     if first:
+        lines["d"] = refs.pop(0)
+    if not (pre and first or post and not first):
+        lines["f"] = refs.pop(0)
+    if first and not pre:
         lines["s"] = refs.pop(0)
-        lines["d"] = refs.pop(0)
     named = {}
     for key, spans in pieces:
         named[key] = [(refs.pop(0), lo, hi) for lo, hi in spans]
-    if last:
+    if pre:
+        outs = [refs.pop(0)]
+        w_out = refs.pop(0) if first else None
+    elif last:
         refs.pop(0)
         natural = refs.pop(0)
     else:
@@ -162,11 +169,15 @@
     R, RP, H, HP, S, A, O, W, forcing = refs[:9]
     refs = refs[9:]
     dests = {"p": R, "h": H, "f": forcing}
+    flat = {"w": W}
+    if post:
+        flat["t"] = refs.pop(0)
+        flat["u"] = refs.pop(0)
     if first:
         DS, DA, HH, storage, head = refs[:5]
         refs = refs[5:]
         dests.update({"s": storage, "d": head})
-    if last:
+    if last and not pre:
         NAT = refs.pop(0)
     sem_in, sem_out = refs
     zlo = max(za - 1, 0)
@@ -194,20 +205,20 @@
     for end in ends:
         batch = []
         for (kind, name), spans in named.items():
-            low_row = za if kind == "w" else zlo
-            high_row = zb if kind == "w" else zhi + 1
+            low_row = za if kind in flat else zlo
+            high_row = zb if kind in flat else zhi + 1
             for ref, lo, hi in spans:
                 s, e = max(start, lo, low_row), min(end, hi, high_row)
                 if s < e:
                     src, dst = pl.ds(s - lo, e - s), pl.ds(s - low_row, e - s)
-                    if kind == "w":
-                        copy_in(batch, ref.at[:, src], W.at[:, dst])
+                    if kind in flat:
+                        copy_in(batch, ref.at[:, src], flat[kind].at[:, dst])
                     else:
                         copy_in(batch, ref.at[src], dests[kind].at[slots[name], dst])
         if start == zlo:
             for kind, ref in lines.items():
                 copy_in(batch, ref, dests[kind])
-            if first:
+            if first and not pre:
                 for q, name in enumerate(("ra", "rb")):
                     ref, lo, hi = named["p", name][0]
                     some = pl.ds(hi - lo, depth // 8)
@@ -238,7 +249,9 @@
 
     tile = [pl.ds(t * 128, 128) for t in range(tiles)]
 
-    def load_row(z, chosen=range(4)):
+    used_planes = own if pre else range(4)
+
+    def load_row(z, chosen=used_planes):
         q = z - zlo
         for i in chosen:
             r = [recip(R[i, q, :, ys]) for ys in tile]
@@ -246,6 +259,8 @@
             for t, ys in enumerate(tile):
                 R[i, q, :, ys] = r[t]
                 RP[i, q, :, ys] = rp[t]
+            if post and i in own:
+                continue
             if first:
                 if i in own:
                     row = head[i - 1, pl.ds(z, 1), :]
@@ -268,9 +283,14 @@
         for t, ys in enumerate(tile):
 
             def get(ref):
-                return [[ref[i, q, :, ys] for q in both] for i in range(4)]
-
-            r, rp, h, hp = get(R), get(RP), get(H), get(HP)
+                return {i: [ref[i, q, :, ys] for q in both] for i in used_planes}
+
+            r, rp = get(R), get(RP)
+            h, hp = ({}, {}) if post else (get(H), get(HP))
+            if post:
+                for i in (0, 3):
+                    h[i] = [H[i, q, :, ys] for q in both]
+                    hp[i] = [HP[i, q, :, ys] for q in both]
             total = {}
             for k, i in enumerate(own):
                 total["s", i, 0] = S[k, :, ys]
@@ -296,14 +316,17 @@
 
             w1, w2, w3 = 0.5, 1.0, 2.0
             sides = ((0, 1), (1, 2), (2, 3))
-            for i in own:
+            if mode != "full":
+                sides = sides[1:2] if pre else sides[::2]
+            inside = () if post else own
+            for i in inside:
                 pair(w1, i, 0, i, 0, True)
             for i, j in sides:
                 pair(w1, i, 0, j, 0, False)
                 pair(w2, i, 0, j, 0, True)
                 pair(w2, j, 0, i, 0, True)
             if inner:
-                for i in own:
+                for i in inside:
                     pair(w1, i, 0, i, 1, False)
                     pair(w2, i, 0, i, 1, True)
                     pair(w2, i, 1, i, 0, True)
@@ -324,28 +347,44 @@
                 if key[2] == 0:
                     done.setdefault(key[:2], []).append(value)
             if load:
-                load_row(z + 2, range(t * 4 // tiles, (t + 1) * 4 // tiles))
+                count = len(used_planes)
+                load_row(z + 2, used_planes[t * count // tiles : (t + 1) * count // tiles])
         if not emit:
             return
         o = z - za
         for k, i in enumerate(own):
             moved = behind(done["a", i])
-            source = forcing[k, pl.ds(z, 1), :]
-            if first:
-                store = storage[k, pl.ds(z, 1), :]
+            if "f" in lines:
+                source = forcing[k, pl.ds(z, 1), :]
             if first:
                 da = behind(done["da", i])
+                old_row = head[k, pl.ds(z, 1), :]
+                if not pre:
+                    store = storage[k, pl.ds(z, 1), :]
             for t, ys in enumerate(tile):
                 cut = slice(t * 128, (t + 1) * 128)
                 gathered = done["s", i][t] + moved[t]
                 if first:
-                    diagonal = store[:, cut] + (done["ds", i][t] + da[t])
-                    w = OMEGA * recip(diagonal)
+                    weight = done["ds", i][t] + da[t]
+                    old = old_row[:, cut]
+                elif not post:
+                    old = H[i, c, :, ys]
+                if pre and first:
+                    O[k, o, :, ys] = gathered
+                    W[k, o, :, ys] = weight
+                    continue
+                if first:
+                    if post:
+                        gathered = gathered + flat["t"][k, o, :, ys]
+                        weight = weight + flat["u"][k, o, :, ys]
+                    w = OMEGA * recip(store[:, cut] + weight)
                     W[k, o, :, ys] = w
                 else:
                     w = W[k, o, :, ys]
-                old = H[i, c, :, ys]
-                O[k, o, :, ys] = (1.0 - OMEGA) * old + w * (source[:, cut] + gathered)
+                if post and not first:
+                    O[k, o, :, ys] = flat["t"][k, o, :, ys] + w * gathered
+                else:
+                    O[k, o, :, ys] = (1.0 - OMEGA) * old + w * (source[:, cut] + gathered)
 
     results = []
 
@@ -357,13 +396,18 @@
     progress = [za]
 
     def flush(upto):
-        if last:
+        if last and not pre:
             upto = upto // 8 * 8
         begin = progress[0]
         if upto <= begin:
             return
         progress[0] = upto
         rows = pl.ds(begin - za, upto - begin)
+        if pre:
+            start_out(O.at[:, rows], outs[0].at[:, rows])
+            if first:
+                start_out(W.at[:, rows], w_out.at[:, rows])
+            return
         if last:
 
             def turn(b, carry):
@@ -417,37 +461,36 @@
         copy.wait()
 
 
-def sweep_of(first, last, za, zb, shape, lines, fields, into=None, after=()):
+def sweep_of(mode, first, last, shape, lines, fields, after=()):
     members, planes, depth, across = shape
-    zlo = max(za - 1, 0)
-    zhi = min(zb, depth - 1)
-    rows = zb - za
+    za, zb = 0, depth
     pieces = tuple((key, tuple((lo, hi) for _, lo, hi in spans)) for key, spans in fields.items())
     operands = list(lines)
     for spans in fields.values():
         operands += [ref for ref, _, _ in spans]
-    copies = sum(len(spans) for spans in fields.values()) * 7 + 8
-    field = pltpu.VMEM((4, zhi + 1 - zlo, members, across), F32)
+    copies = sum(len(spans) for spans in fields.values()) * 8 + 8
+    field = pltpu.VMEM((4, depth, members, across), F32)
     line = pltpu.VMEM((2, members, across), F32)
     flat = pltpu.VMEM((2, depth, across), F32)
-    both = pltpu.VMEM((2, rows, members, across), F32)
+    both = pltpu.VMEM((2, depth, members, across), F32)
     scratch = [field] * 4 + [line] * 2 + [both] * 2 + [flat]
+    if mode == "post":
+        scratch += [both] * 2
     if first:
         scratch += [line] * 2 + [pltpu.VMEM((2, depth // 8, 8, across), F32)] + [flat] * 2
-    alias = {}
-    if last:
-        scratch += [pltpu.VMEM((members, 2, rows, across), F32)]
+    pair = jax.ShapeDtypeStruct((2, depth, members, across), F32)
+    if mode == "pre":
+        out_shape = [pair] * (2 if first else 1)
+    elif last:
+        scratch += [pltpu.VMEM((members, 2, depth, across), F32)]
         out_shape = [jax.ShapeDtypeStruct(shape, F32)]
-        operands.append(lines[0] if into is None else into)
-        if into is not None:
-            alias = {len(operands) - 1: 0}
+        operands.append(operands[0])
     else:
-        out_shape = [jax.ShapeDtypeStruct((rows, members, across), F32)] * 2
+        out_shape = [jax.ShapeDtypeStruct((depth, members, across), F32)] * 2
         if first:
-            out_shape += [jax.ShapeDtypeStruct((2, rows, members, across), F32)]
+            out_shape += [pair]
     scratch += [pltpu.SemaphoreType.DMA((copies,)), pltpu.SemaphoreType.DMA((32,))]
-    cfg = (first, last, za, zb, depth, members, across, pieces)
-    cells = 2 * rows * members * across
+    cfg = (mode, first, last, za, zb, depth, members, across, pieces)
     return call(
         functools.partial(sweep_kernel, cfg),
         "sweep",
@@ -455,22 +498,24 @@
         [ANY] * len(operands),
         [ANY] * len(out_shape),
         scratch,
-        alias=alias,
         after=after,
     )(*operands)
 
 
-WAITS = {(1, 0): ("patches",), (2, 0): ("partial",)}
-CUTS = (None, None, None, None)
+WAITS = {1: ("patches",), 2: ("partial",)}
+CUTS = (None,)
 ORDER = (
     "planes",
     "gather",
-    (1, 0),
+    (1,),
+    (1, "post"),
     "local",
-    (2, 0),
+    (2,),
+    (2, "post"),
     "solve",
     "update",
-    (3, 0),
+    (3,),
+    (3, "post"),
 )
 
 
@@ -878,7 +923,6 @@
         far_b = [halo(x, 1) for x in side_b]
         sides = (side_a, side_b, far_a, far_b)
         state["perms"] = {("p", n): span(v, CUTS[0]) for n, v in zip(names, sides)}
-        state["new"] = {1: [], 2: []}
         state["own"] = own
         state["every"] = lax.all_gather(own, "ens", axis=0)
 
@@ -912,26 +956,52 @@
         )
         after(state["updated"])
 
-    def sweep_step(sweep, part):
+    def whole(ref):
+        return [(ref, 0, depth)]
+
+    def pre_step(sweep):
+        first = sweep == 1
+        perms = state["perms"]
+        fields = {k: perms[k] for k in (("p", "a"), ("p", "b"))}
+        if first:
+            lines = [head_init]
+        else:
+            lines = [state["forcing"]]
+            fields["h", "a"], fields["h", "b"] = (whole(x) for x in state["new"][:2])
+            fields["w", "w"] = whole(state["weights"])
+        state["pre"] = sweep_of(
+            "pre", first, sweep == 3, shape, lines, fields, after=state["token"]
+        )
+        after(state["pre"][0])
+
+    def sweep_step(sweep, mode):
         first, last = sweep == 1, sweep == 3
-        lo, hi = row_spans(depth, CUTS[sweep])[part]
-        lines = [state["forcing"]] + ([storage, head_init] if first else [])
-        fields = {k: v[: part + 1] if k[1][0] == "r" else v for k, v in state["perms"].items()}
+        post = mode == "post"
+        lines = [head_init] if first else []
+        if first or not post:
+            lines.append(state["forcing"])
+        if first:
+            lines.append(storage)
+        fields = dict(state["perms"])
         if not first:
-            columns = list(zip(*state["new"][sweep - 1]))
+            fields["w", "w"] = whole(state["weights"])
             for k, n in enumerate(names):
-                fields["h", n] = span(columns[k], CUTS[sweep - 1])
-            weights = list(zip(*state["new"][1]))[4]
-            fields["w", "w"] = span(weights, CUTS[1])
-        token = () if "head" in state else state["token"]
-        for key in WAITS.get((sweep, part), ()):
+                if k >= 2 or not post:
+                    fields["h", n] = whole(state["new"][k])
+        if post:
+            fields["t", "t"] = whole(state["pre"][0])
+            if first:
+                fields["u", "u"] = whole(state["pre"][1])
+        token = state["token"]
+        for key in WAITS.get(sweep, ()):
             token = token + tuple(state[key])
-        out = sweep_of(first, last, lo, hi, shape, lines, fields, state.get("head"), after=token)
+        out = sweep_of(mode, first, last, shape, lines, fields, after=token)
         if last:
             state["head"] = out[0]
         else:
-            far = (halo(out[0], 0), halo(out[1], 1))
-            state["new"][sweep].append((out[0], out[1]) + far + tuple(out[2:]))
+            if first:
+                state["weights"] = out[2]
+            state["new"] = (out[0], out[1], halo(out[0], 0), halo(out[1], 1))
         after(out[0])
 
     steps = dict(
@@ -943,7 +1013,7 @@
     )
     for step in ORDER:
         if isinstance(step, tuple):
-            sweep_step(*step)
+            (pre_step if len(step) == 1 else sweep_step)(*step)
         else:
             steps[step]()
     return (state["head"], state["updated"])

time: 143 us -> 137 us (0.958)
  waiting for transfers between devices: 37.9 us -> 19.7 us
  Pallas kernels: 63.8 us -> 75.9 us
    ppermute x9, waiting for transfers between devices: 33.2 us -> 18.4 us  [swap(): lax.ppermute(x, axis, [(i, i ^ bit) for i in range(lax.axis_size(axis))])]
    pallas_call x3 -> x6, Pallas kernels: 35.2 us -> 47.2 us  [sweep_of(): call(functools.partial(sweep_kernel, cfg), 'sweep', out_shape, [ANY] * le...]
    ppermute x6, waiting for transfers between devices: 4.66 us -> 0.02 us  [halo(): return lax.ppermute(x, 'space', pairs + [(b, a) for a, b in pairs])]
  transfers between devices with their start and end apart: 16 -> 16, of which waited for: 8 -> 6; matrix products, arithmetic and copies ran while one was open for 0% -> 1% of each run, Pallas kernels for 34% -> 46%
where the time goes in v3:
time: 137 us; the launch traced here: 136 us
  Pallas kernels  75.9 us (55%)
  starting transfers between devices  24.7 us (18%)
  waiting for transfers between devices  19.7 us (14%)
  between operations  14.8 us (11%)
    pallas_call x6, Pallas kernels, sweep_of(): call(functools.partial(sweep_kernel, cfg), 'sweep', out_shape, [ANY] * le...  47.2 us
    ppermute x9, waiting for transfers between devices, swap(): lax.ppermute(x, axis, [(i, i ^ bit) for i in range(lax.axis_size(axis))])  18.4 us
    ppermute x9, starting transfers between devices, swap(): lax.ppermute(x, axis, [(i, i ^ bit) for i in range(lax.axis_size(axis))])  13.2 us
    ppermute x6, starting transfers between devices, halo(): return lax.ppermute(x, 'space', pairs + [(b, a) for a, b in pairs])  11.4 us
    pallas_call x1, Pallas kernels, update_of(): call(functools.partial(update_kernel, step), 'update', jax.ShapeDtypeStru...  9.12 us
    pallas_call x1, Pallas kernels, gather_of(): call(functools.partial(gather_kernel, slabs), 'gather', [jax.ShapeDtypeSt...  6.48 us
    pallas_call x1, Pallas kernels, solve_of(): call(functools.partial(solve_kernel, nobs, peers), 'solve', jax.ShapeDtyp...  5 us
    pallas_call x1, Pallas kernels, planes_of(): call(functools.partial(planes_kernel, step, cut), 'planes', sides * 2 + [...  4.35 us
  transfers between devices with their start and end apart: 16, of which 6 were waited for; matrix products, arithmetic and copies ran while one was open for 1% of the time, Pallas kernels for 46%

profile of v3, /device:TPU:0, one launch (start us, length us, event | category | flops | bytes accessed | tf_op | source)
XLA Modules:
  0.0 136.4 jit_solution(2105797846564212754)
XLA Ops:
  7.2 4.3 %planes.1 = (f32[72,8,512]{2,1,0:T(8,128)}, f32[72,8,512]{2,1,0:T(8,128)}, f32[2,64,8,512]{3,2,1,0:T(8,128)}) custom-call(f32[8,2,64,512]{3,2,1,0:T(8,128)} %refs_2_.3, f32[2,64,512]{2,1,0:T(8,128)} %refs_5_.1), custom_call_target="tpu_custom_call" | custom-call | bytes 12000000 | tf_op jit(solution)/shard_map/planes/pallas_call | solution.py:126
  11.6 3.1 %collective-permute-start.3 = (f32[72,8,512]{2,1,0:T(8,128)}, f32[72,8,512]{2,1,0:T(8,128)}, u32[]{:S(2)}, u32[]{:S(2)}) collective-permute-start(f32[72,8,512]{2,1,0:T(8,128)} %get-tuple-element.19.refs_2_.refs_8_.refs_5_.refs_1_.refs_9_), channel_id=1, source_target_pairs={{0,8},{16,24},{8,0},{24,16},{1,9},{17,25},{9,1},{25,17},{2,10},{18... | collective-permute-start | bytes 3538952 | tf_op jit(solution)/shard_map/ppermute | solution.py:892
  14.7 1.7 %collective-permute-start.4 = (f32[72,8,512]{2,1,0:T(8,128)}, f32[72,8,512]{2,1,0:T(8,128)}, u32[]{:S(2)}, u32[]{:S(2)}) collective-permute-start(f32[72,8,512]{2,1,0:T(8,128)} %get-tuple-element.20.refs_3_.refs_9_.refs_6_.refs_2_), channel_id=1, source_target_pairs={{8,16},{16,8},{9,17},{17,9},{10,18},{18,10},{11,19},{19,11},{12,20... | collective-permute-start | bytes 3538952 | tf_op jit(solution)/shard_map/ppermute | solution.py:892
  16.4 6.5 %gather.1 = (f32[2,7,8,128]{3,2,1,0:T(8,128)}, f32[2,7,8,128]{3,2,1,0:T(8,128)}, f32[2,7,8,128]{3,2,1,0:T(8,128)}, f32[2,7,8,128]{3,2,1,0:T(8,128)}, f32[2,64,512]{2,1,0:T(8,128)}) custom-call(s32[16]{0:T(128)} %refs_0_.3, f32[16]{0:T(128)} %refs_1_.5, s32[32]{0:T(128)} %refs_1_.7, f32[2,64,512]{2,1,0:T(8,128)} %refs_5_.1, f32[2,64,512]{2,1,0:T(8,128)} %refs_7_.1, ...), custom_call_target="tpu_custom_call" | custom-call | bytes 18000000 | tf_op jit(solution)/shard_map/gather/pallas_call | solution.py:636
  22.9 3.4 %collective-permute-start = (f32[2,7,8,128]{3,2,1,0:T(8,128)}, f32[2,7,8,128]{3,2,1,0:T(8,128)}, u32[]{:S(2)}, u32[]{:S(2)}) collective-permute-start(f32[2,7,8,128]{3,2,1,0:T(8,128)} %get-tuple-element.22), channel_id=1, source_target_pairs={{0,8},{8,0},{16,24},{24,16},{1,9},{9,1},{17,25},{25,17},{2,10},{10... | collective-permute-start | bytes 172040 | tf_op jit(solution)/shard_map/ppermute | solution.py:883
  26.3 2.4 %collective-permute-start.2 = (f32[2,7,8,128]{3,2,1,0:T(8,128)}, f32[2,7,8,128]{3,2,1,0:T(8,128)}, u32[]{:S(2)}, u32[]{:S(2)}) collective-permute-start(f32[2,7,8,128]{3,2,1,0:T(8,128)} %get-tuple-element.24), channel_id=1, source_target_pairs={{0,24},{8,16},{16,8},{24,0},{1,25},{9,17},{17,9},{25,1},{2,26},{10... | collective-permute-start | bytes 172040 | tf_op jit(solution)/shard_map/ppermute | solution.py:883
  28.7 8.1 %sweep.6 = (f32[2,64,8,512]{3,2,1,0:T(8,128)}, f32[2,64,8,512]{3,2,1,0:T(8,128)}) custom-call(f32[2,7,8,128]{3,2,1,0:T(8,128)} %get-tuple-element.18.refs_0_.refs_1_.refs_2_, f32[2,64,512]{2,1,0:T(8,128)} %refs_5_.1, f32[72,8,512]{2,1,0:T(8,128)} %get-tuple-element.19.refs_2_.refs_8_.refs_5_.refs_1_.refs_9_, ...), custom_call_target="tpu_custom_call" | custom-call | bytes 39000000 | tf_op jit(solution)/shard_map/sweep/pallas_call | solution.py:494
  36.8 5.8 %collective-permute-done.refs_2_.refs_3_ = f32[2,7,8,128]{3,2,1,0:T(8,128)} collective-permute-done((f32[2,7,8,128]{3,2,1,0:T(8,128)}, f32[2,7,8,128]{3,2,1,0:T(8,128)}, u32[]{:S(2)}, u32[]{:S(2)}) %collective-permute-start) | collective-permute-done | bytes 57376 | tf_op jit(solution)/shard_map/ppermute | solution.py:883
  42.6 6.9 %collective-permute-done.1.refs_3_.refs_4_ = f32[2,7,8,128]{3,2,1,0:T(8,128)} collective-permute-done((f32[2,7,8,128]{3,2,1,0:T(8,128)}, f32[2,7,8,128]{3,2,1,0:T(8,128)}, u32[]{:S(2)}, u32[]{:S(2)}) %collective-permute-start.1) | collective-permute-done | bytes 57376 | tf_op jit(solution)/shard_map/ppermute | solution.py:883
  49.5 8.6 %sweep.7 = (f32[64,8,512]{2,1,0:T(8,128)}, f32[64,8,512]{2,1,0:T(8,128)}, f32[2,64,8,512]{3,2,1,0:T(8,128)}) custom-call(f32[2,64,8,512]{3,2,1,0:T(8,128)} %get-tuple-element.21.refs_0_.refs_12_, f32[2,7,8,128]{3,2,1,0:T(8,128)} %get-tuple-element.18.refs_0_.refs_1_.refs_2_, f32[2,7,8,128]{3,2,1,0:T(8,128)} %collective-permute-done.refs_2_.refs_3_, ...), custom_call_target="tpu_custom_call" | custom-call | bytes 39000000 | tf_op jit(solution)/shard_map/sweep/pallas_call | solution.py:494
  59.3 1.6 %collective-permute-start.12 = (f32[64,8,512]{2,1,0:T(8,128)}, f32[64,8,512]{2,1,0:T(8,128)}, u32[]{:S(2)}, u32[]{:S(2)}) collective-permute-start(f32[64,8,512]{2,1,0:T(8,128)} %get-tuple-element.28.refs_5_), channel_id=1, source_target_pairs={{8,16},{16,8},{9,17},{17,9},{10,18},{18,10},{11,19},{19,11},{12,20... | collective-permute-start | bytes 3145736 | tf_op jit(solution)/shard_map/ppermute | solution.py:892
  60.9 3.7 %local_heads.1.refs_0_ = f32[8,128]{1,0:T(8,128)} custom-call(f32[64,8,512]{2,1,0:T(8,128)} %get-tuple-element.27.refs_0_.refs_4_, s32[32]{0:T(128)} %refs_1_.7, f32[2,7,8,128]{3,2,1,0:T(8,128)} %get-tuple-element.18.refs_0_.refs_1_.refs_2_, f32[2,7,8,128]{3,2,1,0:T(8,128)} %collective-permute-done.refs_2_.refs_3_, ...), custom_call_target="tpu_custom_call" | custom-call | bytes 15000000 | tf_op jit(solution)/shard_map/local_heads/pallas_call | solution.py:742
  68.2 2.2 %collective-permute-done.6 = f32[8,128]{1,0:T(8,128)S(1)} collective-permute-done((f32[8,128]{1,0:T(8,128)S(1)}, f32[8,128]{1,0:T(8,128)S(1)}, u32[]{:S(2)}, u32[]{:S(2)}) %collective-permute-start.6) | collective-permute-done | bytes 4128 | tf_op jit(solution)/shard_map/ppermute | solution.py:883
  70.4 1.5 %collective-permute-start.7 = (f32[8,128]{1,0:T(8,128)S(1)}, f32[8,128]{1,0:T(8,128)S(1)}, u32[]{:S(2)}, u32[]{:S(2)}) collective-permute-start(f32[8,128]{1,0:T(8,128)S(1)} %add.10), channel_id=1, source_target_pairs={{0,4},{1,5},{2,6},{3,7},{4,0},{5,1},{6,2},{7,3},{8,12},{9,13},{10,... | collective-permute-start | bytes 12296 | tf_op jit(solution)/shard_map/ppermute | solution.py:883
  71.9 2.1 %collective-permute-done.7 = f32[8,128]{1,0:T(8,128)S(1)} collective-permute-done((f32[8,128]{1,0:T(8,128)S(1)}, f32[8,128]{1,0:T(8,128)S(1)}, u32[]{:S(2)}, u32[]{:S(2)}) %collective-permute-start.7) | collective-permute-done | bytes 4128 | tf_op jit(solution)/shard_map/ppermute | solution.py:883
  74.7 2.6 %collective-permute-start.10 = (f32[8,128]{1,0:T(8,128)}, f32[8,128]{1,0:T(8,128)}, u32[]{:S(2)}, u32[]{:S(2)}) collective-permute-start(f32[8,128]{1,0:T(8,128)} %add.11.refs_1_.refs_5_), channel_id=1, source_target_pairs={{0,24},{8,16},{16,8},{24,0},{1,25},{9,17},{17,9},{25,1},{2,26},{10... | collective-permute-start | bytes 12296 | tf_op jit(solution)/shard_map/ppermute | solution.py:883
  79.0 7.3 %sweep.8.refs_0_.refs_12_ = f32[2,64,8,512]{3,2,1,0:T(8,128)} custom-call(f32[8,128]{1,0:T(8,128)} %local_heads.1.refs_0_, f32[2,64,512]{2,1,0:T(8,128)} %get-tuple-element.25.refs_6_.refs_1_, f32[72,8,512]{2,1,0:T(8,128)} %get-tuple-element.19.refs_2_.refs_8_.refs_5_.refs_1_.refs_9_, f32[72,8,512]{2,1,0:T(8,128)} %get-tuple-element.20.refs_3_.refs_9_.refs_6_.refs_2_, ...), custom_call_target="tpu_custom_call" | custom-call | bytes 39000000 | tf_op jit(solution)/shard_map/sweep/pallas_call | solution.py:494
  86.4 7.8 %sweep.9 = (f32[64,8,512]{2,1,0:T(8,128)}, f32[64,8,512]{2,1,0:T(8,128)}) custom-call(f32[2,64,8,512]{3,2,1,0:T(8,128)} %sweep.8.refs_0_.refs_12_, f32[8,128]{1,0:T(8,128)} %add.11.refs_1_.refs_5_, f32[8,128]{1,0:T(8,128)} %collective-permute-done.8.refs_2_.refs_6_, f32[8,128]{1,0:T(8,128)} %collective-permute-done.9.refs_3_.refs_7_, ...), custom_call_target="tpu_custom_call" | custom-call | bytes 39000000 | tf_op jit(solution)/shard_map/sweep/pallas_call | solution.py:494
  94.2 2.1 %collective-permute-start.13 = (f32[64,8,512]{2,1,0:T(8,128)}, f32[64,8,512]{2,1,0:T(8,128)}, u32[]{:S(2)}, u32[]{:S(2)}) collective-permute-start(f32[64,8,512]{2,1,0:T(8,128)} %get-tuple-element.30.refs_0_.refs_4_), channel_id=1, source_target_pairs={{0,8},{16,24},{8,0},{24,16},{1,9},{17,25},{9,1},{25,17},{2,10},{18... | collective-permute-start | bytes 3145736 | tf_op jit(solution)/shard_map/ppermute | solution.py:892
  96.2 1.6 %collective-permute-start.14 = (f32[64,8,512]{2,1,0:T(8,128)}, f32[64,8,512]{2,1,0:T(8,128)}, u32[]{:S(2)}, u32[]{:S(2)}) collective-permute-start(f32[64,8,512]{2,1,0:T(8,128)} %get-tuple-element.31.refs_5_), channel_id=1, source_target_pairs={{8,16},{16,8},{9,17},{17,9},{10,18},{18,10},{11,19},{19,11},{12,20... | collective-permute-start | bytes 3145736 | tf_op jit(solution)/shard_map/ppermute | solution.py:892
  98.5 5.0 %solve.1.refs_0_.refs_1_ = f32[8,64]{1,0:T(8,128)} custom-call(f32[64,8,512]{2,1,0:T(8,128)} %get-tuple-element.30.refs_0_.refs_4_, f32[1,32]{1,0:T(1,128)} %bitcast.4, f32[1,32]{1,0:T(1,128)} %bitcast.5, f32[1]{0:T(128)S(6)} %copy.12.refs_3_, f32[8,32]{1,0:T(8,128)} %refs_4_.3, f32[8,128]{1,0:T(8,128)} %add.11.refs_1_.refs_5_, ...), custom_call_target="tpu_custom_call" | custom-call | bytes 15000000 | tf_op jit(solution)/shard_map/solve/pallas_call | solution.py:799
  104.9 9.1 %update.1.refs_0_ = f32[8,2,64,512]{3,2,1,0:T(8,128)} custom-call(f32[8,64]{1,0:T(8,128)} %solve.1.refs_0_.refs_1_, f32[8,64]{1,0:T(8,128)} %solve.1.refs_0_.refs_1_, f32[8,2,64,512]{3,2,1,0:T(8,128)} %refs_2_.3, f32[8,2,64,8,512]{4,3,2,1,0:T(8,128)} %bitcast.3), custom_call_target="tpu_custom_call" | custom-call | bytes 12000000 | tf_op jit(solution)/shard_map/update/pallas_call | solution.py:865
  114.0 7.3 %sweep.10.refs_0_.refs_8_ = f32[2,64,8,512]{3,2,1,0:T(8,128)} custom-call(f32[8,2,64,512]{3,2,1,0:T(8,128)} %update.1.refs_0_, f32[2,64,512]{2,1,0:T(8,128)} %get-tuple-element.25.refs_6_.refs_1_, f32[72,8,512]{2,1,0:T(8,128)} %get-tuple-element.19.refs_2_.refs_8_.refs_5_.refs_1_.refs_9_, f32[72,8,512]{2,1,0:T(8,128)} %get-tuple-element.20.refs_3_.refs_9_.refs_6_.refs_2_, ...), custom_call_target="tpu_custom_call" | custom-call | bytes 39000000 | tf_op jit(solution)/shard_map/sweep/pallas_call | solution.py:494
  121.3 8.2 %sweep.11 = f32[8,2,64,512]{3,2,1,0:T(8,128)} custom-call(f32[2,64,8,512]{3,2,1,0:T(8,128)} %sweep.10.refs_0_.refs_8_, f32[72,8,512]{2,1,0:T(8,128)} %get-tuple-element.19.refs_2_.refs_8_.refs_5_.refs_1_.refs_9_, f32[72,8,512]{2,1,0:T(8,128)} %get-tuple-element.20.refs_3_.refs_9_.refs_6_.refs_2_, ...), custom_call_target="tpu_custom_call" | custom-call | bytes 39000000 | tf_op jit(solution)/shard_map/sweep/pallas_call | solution.py:494
  (23 shorter events, 8.6 us)
Async XLA Ops:
  7.2 97.7 %all-gather.3.cloned.1.call-start = ((), (), s32[]{:S(2)}) async-start(), calls=%async_computation | async-start | bytes 18874368 | tf_op jit(solution)/shard_map/all_gather | solution.py:927
  11.6 37.9 %collective-permute-start.3 = (f32[72,8,512]{2,1,0:T(8,128)}, f32[72,8,512]{2,1,0:T(8,128)}, u32[]{:S(2)}, u32[]{:S(2)}) collective-permute-start(f32[72,8,512]{2,1,0:T(8,128)} %get-tuple-element.19.refs_2_.refs_8_.refs_5_.refs_1_.refs_9_), channel_id=1, source_target_pairs={{0,8},{16,24},{8,0},{24,16},{1,9},{17,25},{9,1},{25,17},{2,10},{18... | collective-permute-start | bytes 3538952 | tf_op jit(solution)/shard_map/ppermute | solution.py:892
  14.7 34.8 %collective-permute-start.4 = (f32[72,8,512]{2,1,0:T(8,128)}, f32[72,8,512]{2,1,0:T(8,128)}, u32[]{:S(2)}, u32[]{:S(2)}) collective-permute-start(f32[72,8,512]{2,1,0:T(8,128)} %get-tuple-element.20.refs_3_.refs_9_.refs_6_.refs_2_), channel_id=1, source_target_pairs={{8,16},{16,8},{9,17},{17,9},{10,18},{18,10},{11,19},{19,11},{12,20... | collective-permute-start | bytes 3538952 | tf_op jit(solution)/shard_map/ppermute | solution.py:892
  22.9 19.7 %collective-permute-start = (f32[2,7,8,128]{3,2,1,0:T(8,128)}, f32[2,7,8,128]{3,2,1,0:T(8,128)}, u32[]{:S(2)}, u32[]{:S(2)}) collective-permute-start(f32[2,7,8,128]{3,2,1,0:T(8,128)} %get-tuple-element.22), channel_id=1, source_target_pairs={{0,8},{8,0},{16,24},{24,16},{1,9},{9,1},{17,25},{25,17},{2,10},{10... | collective-permute-start | bytes 172040 | tf_op jit(solution)/shard_map/ppermute | solution.py:883
  26.3 23.2 %collective-permute-start.1 = (f32[2,7,8,128]{3,2,1,0:T(8,128)}, f32[2,7,8,128]{3,2,1,0:T(8,128)}, u32[]{:S(2)}, u32[]{:S(2)}) collective-permute-start(f32[2,7,8,128]{3,2,1,0:T(8,128)} %get-tuple-element.23), channel_id=1, source_target_pairs={{0,16},{8,24},{16,0},{24,8},{1,17},{9,25},{17,1},{25,9},{2,18},{10... | collective-permute-start | bytes 172040 | tf_op jit(solution)/shard_map/ppermute | solution.py:883
  26.3 23.2 %collective-permute-start.2 = (f32[2,7,8,128]{3,2,1,0:T(8,128)}, f32[2,7,8,128]{3,2,1,0:T(8,128)}, u32[]{:S(2)}, u32[]{:S(2)}) collective-permute-start(f32[2,7,8,128]{3,2,1,0:T(8,128)} %get-tuple-element.24), channel_id=1, source_target_pairs={{0,24},{8,16},{16,8},{24,0},{1,25},{9,17},{17,9},{25,1},{2,26},{10... | collective-permute-start | bytes 172040 | tf_op jit(solution)/shard_map/ppermute | solution.py:883
  58.1 28.3 %collective-permute-start.11 = (f32[64,8,512]{2,1,0:T(8,128)}, f32[64,8,512]{2,1,0:T(8,128)}, u32[]{:S(2)}, u32[]{:S(2)}) collective-permute-start(f32[64,8,512]{2,1,0:T(8,128)} %get-tuple-element.27.refs_0_.refs_4_), channel_id=1, source_target_pairs={{0,8},{16,24},{8,0},{24,16},{1,9},{17,25},{9,1},{25,17},{2,10},{18... | collective-permute-start | bytes 3145736 | tf_op jit(solution)/shard_map/ppermute | solution.py:892
  59.3 27.1 %collective-permute-start.12 = (f32[64,8,512]{2,1,0:T(8,128)}, f32[64,8,512]{2,1,0:T(8,128)}, u32[]{:S(2)}, u32[]{:S(2)}) collective-permute-start(f32[64,8,512]{2,1,0:T(8,128)} %get-tuple-element.28.refs_5_), channel_id=1, source_target_pairs={{8,16},{16,8},{9,17},{17,9},{10,18},{18,10},{11,19},{19,11},{12,20... | collective-permute-start | bytes 3145736 | tf_op jit(solution)/shard_map/ppermute | solution.py:892
  64.7 1.4 %collective-permute-start.5 = (f32[8,128]{1,0:T(8,128)}, f32[8,128]{1,0:T(8,128)S(1)}, u32[]{:S(2)}, u32[]{:S(2)}) collective-permute-start(f32[8,128]{1,0:T(8,128)} %local_heads.1.refs_0_), channel_id=1, source_target_pairs={{0,1},{1,0},{2,3},{3,2},{4,5},{5,4},{6,7},{7,6},{8,9},{9,8},{10,11... | collective-permute-start | bytes 12296 | tf_op jit(solution)/shard_map/ppermute | solution.py:883
  66.7 3.7 %collective-permute-start.6 = (f32[8,128]{1,0:T(8,128)S(1)}, f32[8,128]{1,0:T(8,128)S(1)}, u32[]{:S(2)}, u32[]{:S(2)}) collective-permute-start(f32[8,128]{1,0:T(8,128)S(1)} %add.9), channel_id=1, source_target_pairs={{0,2},{1,3},{2,0},{3,1},{4,6},{5,7},{6,4},{7,5},{8,10},{9,11},{10,... | collective-permute-start | bytes 12296 | tf_op jit(solution)/shard_map/ppermute | solution.py:883
  70.4 3.7 %collective-permute-start.7 = (f32[8,128]{1,0:T(8,128)S(1)}, f32[8,128]{1,0:T(8,128)S(1)}, u32[]{:S(2)}, u32[]{:S(2)}) collective-permute-start(f32[8,128]{1,0:T(8,128)S(1)} %add.10), channel_id=1, source_target_pairs={{0,4},{1,5},{2,6},{3,7},{4,0},{5,1},{6,2},{7,3},{8,12},{9,13},{10,... | collective-permute-start | bytes 12296 | tf_op jit(solution)/shard_map/ppermute | solution.py:883
  74.7 11.7 %collective-permute-start.10 = (f32[8,128]{1,0:T(8,128)}, f32[8,128]{1,0:T(8,128)}, u32[]{:S(2)}, u32[]{:S(2)}) collective-permute-start(f32[8,128]{1,0:T(8,128)} %add.11.refs_1_.refs_5_), channel_id=1, source_target_pairs={{0,24},{8,16},{16,8},{24,0},{1,25},{9,17},{17,9},{25,1},{2,26},{10... | collective-permute-start | bytes 12296 | tf_op jit(solution)/shard_map/ppermute | solution.py:883
  77.3 9.1 %collective-permute-start.8 = (f32[8,128]{1,0:T(8,128)}, f32[8,128]{1,0:T(8,128)}, u32[]{:S(2)}, u32[]{:S(2)}) collective-permute-start(f32[8,128]{1,0:T(8,128)} %add.11.refs_1_.refs_5_), channel_id=1, source_target_pairs={{0,8},{8,0},{16,24},{24,16},{1,9},{9,1},{17,25},{25,17},{2,10},{10... | collective-permute-start | bytes 12296 | tf_op jit(solution)/shard_map/ppermute | solution.py:883
  77.8 8.5 %collective-permute-start.9 = (f32[8,128]{1,0:T(8,128)}, f32[8,128]{1,0:T(8,128)}, u32[]{:S(2)}, u32[]{:S(2)}) collective-permute-start(f32[8,128]{1,0:T(8,128)} %add.11.refs_1_.refs_5_), channel_id=1, source_target_pairs={{0,16},{8,24},{16,0},{24,8},{1,17},{9,25},{17,1},{25,9},{2,18},{10... | collective-permute-start | bytes 12296 | tf_op jit(solution)/shard_map/ppermute | solution.py:883
  94.2 27.1 %collective-permute-start.13 = (f32[64,8,512]{2,1,0:T(8,128)}, f32[64,8,512]{2,1,0:T(8,128)}, u32[]{:S(2)}, u32[]{:S(2)}) collective-permute-start(f32[64,8,512]{2,1,0:T(8,128)} %get-tuple-element.30.refs_0_.refs_4_), channel_id=1, source_target_pairs={{0,8},{16,24},{8,0},{24,16},{1,9},{17,25},{9,1},{25,17},{2,10},{18... | collective-permute-start | bytes 3145736 | tf_op jit(solution)/shard_map/ppermute | solution.py:892
  96.2 25.1 %collective-permute-start.14 = (f32[64,8,512]{2,1,0:T(8,128)}, f32[64,8,512]{2,1,0:T(8,128)}, u32[]{:S(2)}, u32[]{:S(2)}) collective-permute-start(f32[64,8,512]{2,1,0:T(8,128)} %get-tuple-element.31.refs_5_), channel_id=1, source_target_pairs={{8,16},{16,8},{9,17},{17,9},{10,18},{18,10},{11,19},{19,11},{12,20... | collective-permute-start | bytes 3145736 | tf_op jit(solution)/shard_map/ppermute | solution.py:892
Sparse Core Ops, SparseCore 0:
  11.7 93.1 all-gather.2

commit v4 on v3

--- a/solution.py
+++ b/solution.py
@@ -512,9 +512,8 @@
     "local",
     (2,),
     (2, "post"),
-    "solve",
+    (3,),
     "update",
-    (3,),
     (3, "post"),
 )
 
@@ -750,8 +749,7 @@
     )(cells, *blocks)
 
 
-def solve_kernel(nobs, peers, values, noise, step, perturb, *refs):
-    *seen, out, aug = refs
+def mixing_rows(nobs, peers, values, noise, step, perturb, seen, aug):
     _, block, slab = spot()
     members = perturb.shape[0]
     total = peers * members
@@ -789,45 +787,28 @@
     gain = jnp.dot(residual, inverse, precision=HIGHEST, preferred_element_type=F32)
     nt = (((1,), (1,)), ((), ()))
     mixing = lax.dot_general(gain, dev, nt, precision=HIGHEST, preferred_element_type=F32)
-    out[...] = mixing * (1.0 / (total - 1))
-
-
-def solve_of(seen, peers, values, noise, step, perturb, after=()):
-    nobs = values.shape[0]
-    members = perturb.shape[0]
-    total = members * peers
-    return call(
-        functools.partial(solve_kernel, nobs, peers),
-        "solve",
-        jax.ShapeDtypeStruct((members, total), F32),
-        [VMEM, VMEM, SMEM] + [VMEM] * (1 + len(seen)),
-        VMEM,
-        [pltpu.VMEM((total, 128), F32)],
-        after=after,
-    )(values[None], noise[None], step, perturb, *seen)
-
-
-def update_kernel(step, mixing, lp, every, out, x, a, sem_lp, sem_in, sem_out):
-    members, planes, depth, across = lp.shape
+    return mixing * (1.0 / (total - 1))
+
+
+def update_kernel(step, nobs, values, noise, size, perturb, *refs):
+    *seen, every, out, x, a, aug, sem_in, sem_out = refs
+    members, planes, depth, across = out.shape
     peers = every.shape[0]
+    _, me, _ = spot()
     blocks = [(b, i) for b in range(depth // step) for i in range(planes)]
     ahead = a.shape[0]
-    ins, outs, fields = [], [], []
+    ins, outs = [], []
     for n, (b, i) in enumerate(blocks):
         rows = pl.ds(b * step, step)
         ins.append(
             pltpu.make_async_copy(every.at[:, i, rows], a.at[n % ahead], sem_in.at[n])
-        )
-        fields.append(
-            pltpu.make_async_copy(lp.at[:, i, rows, :], x.at[:, i, rows, :], sem_lp.at[n])
         )
         outs.append(
             pltpu.make_async_copy(x.at[:, i, rows, :], out.at[:, i, rows, :], sem_out.at[n])
         )
     for n in range(ahead):
         ins[n].start()
-        fields[n].start()
-    m = mixing[...]
+    m = mixing_rows(nobs, peers, values, noise, size, perturb, seen, aug)
     m_top = m.astype(jnp.bfloat16)
     m_low = (m - m_top.astype(F32)).astype(jnp.bfloat16)
     left = jnp.concatenate([m_top, m_top], 1)
@@ -835,7 +816,6 @@
     left = jnp.concatenate([left, right], 0)
     for n, (b, i) in enumerate(blocks):
         ins[n].wait()
-        fields[n].wait()
         for g in range(step // 8):
             lines = []
             for z in range(8 * g, 8 * g + 8):
@@ -844,39 +824,38 @@
                 low = (f - top.astype(F32)).astype(jnp.bfloat16)
                 both = jnp.concatenate([top, low], 0)
                 y = jnp.dot(left, both, preferred_element_type=F32)
-                lines.append(y[:members] + y[members:])
-            change = jnp.stack(lines, 0)
+                lines.append(a[n % ahead, me, z] + (y[:members] + y[members:]))
             some = pl.ds(b * step + 8 * g, 8)
-            x[:, i, some, :] = x[:, i, some, :] + jnp.swapaxes(change, 0, 1)
+            x[:, i, some, :] = jnp.swapaxes(jnp.stack(lines, 0), 0, 1)
         outs[n].start()
         if n + ahead < len(blocks):
             ins[n + ahead].start()
-            fields[n + ahead].start()
     for copy in outs:
         copy.wait()
 
 
-def update_of(mixing, lp, every, after=()):
-    members, planes, depth, across = lp.shape
-    peers = every.shape[0]
+def update_of(seen, values, noise, size, perturb, every, after=()):
+    peers, planes, depth, members, across = every.shape
+    nobs = values.shape[0]
     step = 8
-    ahead = 6
+    ahead = 12
     count = planes * depth // step
+    shape = (members, planes, depth, across)
     return call(
-        functools.partial(update_kernel, step),
+        functools.partial(update_kernel, step, nobs),
         "update",
-        jax.ShapeDtypeStruct(lp.shape, F32),
-        [VMEM, ANY, ANY],
+        jax.ShapeDtypeStruct(shape, F32),
+        [VMEM, VMEM, SMEM, VMEM] + [VMEM] * len(seen) + [ANY],
         ANY,
         [
-            pltpu.VMEM(lp.shape, F32),
+            pltpu.VMEM(shape, F32),
             pltpu.VMEM((ahead, peers, step, members, across), F32),
-            pltpu.SemaphoreType.DMA((count,)),
+            pltpu.VMEM((peers * members, 128), F32),
             pltpu.SemaphoreType.DMA((count,)),
             pltpu.SemaphoreType.DMA((count,)),
         ],
         after=after,
-    )(mixing, lp, every)
+    )(values[None], noise[None], size, perturb, *seen, every)
 
 
 def swap(x, axis, bit):
@@ -944,15 +923,15 @@
             bit *= 2
         state["partial"] = swaps([seen] * slabs, "space")
 
-    def solve_step():
-        state["mixing"] = solve_of(
-            state["partial"], peers, obs_values, noise_var, step_size, perturb, after=state["token"]
-        )
-        after(state["mixing"])
-
     def update_step():
         state["updated"] = update_of(
-            state["mixing"], log_perm, state["every"], after=state["token"]
+            state["partial"],
+            obs_values,
+            noise_var,
+            step_size,
+            perturb,
+            state["every"],
+            after=state["token"],
         )
         after(state["updated"])
 
@@ -1008,7 +987,6 @@
         planes=planes_step,
         gather=gather_step,
         local=local_step,
-        solve=solve_step,
         update=update_step,
     )
     for step in ORDER:

time: 137 us -> 134 us (0.978)
  Pallas kernels: 75.9 us -> 72.6 us
    pallas_call x2 -> x1, Pallas kernels: 14.1 us -> 10.9 us  [update_of(): call(functools.partial(update_kernel, step, nobs), 'update', jax.ShapeDty...]
  transfers between devices with their start and end apart: 16 -> 16, of which waited for: 6 -> 6; matrix products, arithmetic and copies ran while one was open for 1% -> 1% of each run, Pallas kernels for 46% -> 45%
where the time goes in v4:
time: 134 us; the launch traced here: 133 us
  Pallas kernels  72.6 us (54%)
  starting transfers between devices  24.6 us (18%)
  waiting for transfers between devices  19.4 us (14%)
  between operations  14.8 us (11%)
    pallas_call x6, Pallas kernels, sweep_of(): call(functools.partial(sweep_kernel, cfg), 'sweep', out_shape, [ANY] * le...  47.2 us
    ppermute x9, waiting for transfers between devices, swap(): lax.ppermute(x, axis, [(i, i ^ bit) for i in range(lax.axis_size(axis))])  18.3 us
    ppermute x9, starting transfers between devices, swap(): lax.ppermute(x, axis, [(i, i ^ bit) for i in range(lax.axis_size(axis))])  13.2 us
    ppermute x6, starting transfers between devices, halo(): return lax.ppermute(x, 'space', pairs + [(b, a) for a, b in pairs])  11.4 us
    pallas_call x1, Pallas kernels, update_of(): call(functools.partial(update_kernel, step, nobs), 'update', jax.ShapeDty...  10.9 us
    pallas_call x1, Pallas kernels, gather_of(): call(functools.partial(gather_kernel, slabs), 'gather', [jax.ShapeDtypeSt...  6.49 us
    pallas_call x1, Pallas kernels, planes_of(): call(functools.partial(planes_kernel, step, cut), 'planes', sides * 2 + [...  4.35 us
    pallas_call x1, Pallas kernels, local_of(): call(functools.partial(local_kernel, nz, ny, nobs, slabs, peers), 'local_...  3.71 us
  transfers between devices with their start and end apart: 16, of which 6 were waited for; matrix products, arithmetic and copies ran while one was open for 1% of the time, Pallas kernels for 45%

profile of v4, /device:TPU:0, one launch (start us, length us, event | category | flops | bytes accessed | tf_op | source)
XLA Modules:
  0.0 132.8 jit_solution(4888139255586969979)
XLA Ops:
  7.2 4.3 %planes.1 = (f32[72,8,512]{2,1,0:T(8,128)}, f32[72,8,512]{2,1,0:T(8,128)}, f32[2,64,8,512]{3,2,1,0:T(8,128)}) custom-call(f32[8,2,64,512]{3,2,1,0:T(8,128)} %refs_0_.2, f32[2,64,512]{2,1,0:T(8,128)} %refs_5_.1), custom_call_target="tpu_custom_call" | custom-call | bytes 12000000 | tf_op jit(solution)/shard_map/planes/pallas_call | solution.py:126
  11.6 3.1 %collective-permute-start.3 = (f32[72,8,512]{2,1,0:T(8,128)}, f32[72,8,512]{2,1,0:T(8,128)}, u32[]{:S(2)}, u32[]{:S(2)}) collective-permute-start(f32[72,8,512]{2,1,0:T(8,128)} %get-tuple-element.19.refs_2_.refs_8_.refs_5_.refs_1_.refs_9_), channel_id=1, source_target_pairs={{0,8},{16,24},{8,0},{24,16},{1,9},{17,25},{9,1},{25,17},{2,10},{18... | collective-permute-start | bytes 3538952 | tf_op jit(solution)/shard_map/ppermute | solution.py:871
  14.7 1.7 %collective-permute-start.4 = (f32[72,8,512]{2,1,0:T(8,128)}, f32[72,8,512]{2,1,0:T(8,128)}, u32[]{:S(2)}, u32[]{:S(2)}) collective-permute-start(f32[72,8,512]{2,1,0:T(8,128)} %get-tuple-element.20.refs_3_.refs_9_.refs_6_.refs_2_), channel_id=1, source_target_pairs={{8,16},{16,8},{9,17},{17,9},{10,18},{18,10},{11,19},{19,11},{12,20... | collective-permute-start | bytes 3538952 | tf_op jit(solution)/shard_map/ppermute | solution.py:871
  16.4 6.5 %gather.1 = (f32[2,7,8,128]{3,2,1,0:T(8,128)}, f32[2,7,8,128]{3,2,1,0:T(8,128)}, f32[2,7,8,128]{3,2,1,0:T(8,128)}, f32[2,7,8,128]{3,2,1,0:T(8,128)}, f32[2,64,512]{2,1,0:T(8,128)}) custom-call(s32[16]{0:T(128)} %refs_0_.3, f32[16]{0:T(128)} %refs_1_.5, s32[32]{0:T(128)} %refs_1_.7, f32[2,64,512]{2,1,0:T(8,128)} %refs_5_.1, f32[2,64,512]{2,1,0:T(8,128)} %refs_7_.1, ...), custom_call_target="tpu_custom_call" | custom-call | bytes 18000000 | tf_op jit(solution)/shard_map/gather/pallas_call | solution.py:635
  22.9 3.4 %collective-permute-start = (f32[2,7,8,128]{3,2,1,0:T(8,128)}, f32[2,7,8,128]{3,2,1,0:T(8,128)}, u32[]{:S(2)}, u32[]{:S(2)}) collective-permute-start(f32[2,7,8,128]{3,2,1,0:T(8,128)} %get-tuple-element.22), channel_id=1, source_target_pairs={{0,8},{8,0},{16,24},{24,16},{1,9},{9,1},{17,25},{25,17},{2,10},{10... | collective-permute-start | bytes 172040 | tf_op jit(solution)/shard_map/ppermute | solution.py:862
  26.3 2.4 %collective-permute-start.2 = (f32[2,7,8,128]{3,2,1,0:T(8,128)}, f32[2,7,8,128]{3,2,1,0:T(8,128)}, u32[]{:S(2)}, u32[]{:S(2)}) collective-permute-start(f32[2,7,8,128]{3,2,1,0:T(8,128)} %get-tuple-element.24), channel_id=1, source_target_pairs={{0,24},{8,16},{16,8},{24,0},{1,25},{9,17},{17,9},{25,1},{2,26},{10... | collective-permute-start | bytes 172040 | tf_op jit(solution)/shard_map/ppermute | solution.py:862
  28.7 8.1 %sweep.6 = (f32[2,64,8,512]{3,2,1,0:T(8,128)}, f32[2,64,8,512]{3,2,1,0:T(8,128)}) custom-call(f32[2,7,8,128]{3,2,1,0:T(8,128)} %get-tuple-element.18.refs_0_.refs_1_.refs_2_, f32[2,64,512]{2,1,0:T(8,128)} %refs_5_.1, f32[72,8,512]{2,1,0:T(8,128)} %get-tuple-element.19.refs_2_.refs_8_.refs_5_.refs_1_.refs_9_, ...), custom_call_target="tpu_custom_call" | custom-call | bytes 39000000 | tf_op jit(solution)/shard_map/sweep/pallas_call | solution.py:494
  36.8 5.8 %collective-permute-done.refs_2_.refs_3_ = f32[2,7,8,128]{3,2,1,0:T(8,128)} collective-permute-done((f32[2,7,8,128]{3,2,1,0:T(8,128)}, f32[2,7,8,128]{3,2,1,0:T(8,128)}, u32[]{:S(2)}, u32[]{:S(2)}) %collective-permute-start) | collective-permute-done | bytes 57376 | tf_op jit(solution)/shard_map/ppermute | solution.py:862
  42.6 6.9 %collective-permute-done.1.refs_3_.refs_4_ = f32[2,7,8,128]{3,2,1,0:T(8,128)} collective-permute-done((f32[2,7,8,128]{3,2,1,0:T(8,128)}, f32[2,7,8,128]{3,2,1,0:T(8,128)}, u32[]{:S(2)}, u32[]{:S(2)}) %collective-permute-start.1) | collective-permute-done | bytes 57376 | tf_op jit(solution)/shard_map/ppermute | solution.py:862
  49.5 8.6 %sweep.7 = (f32[64,8,512]{2,1,0:T(8,128)}, f32[64,8,512]{2,1,0:T(8,128)}, f32[2,64,8,512]{3,2,1,0:T(8,128)}) custom-call(f32[2,64,8,512]{3,2,1,0:T(8,128)} %get-tuple-element.21.refs_0_.refs_12_, f32[2,7,8,128]{3,2,1,0:T(8,128)} %get-tuple-element.18.refs_0_.refs_1_.refs_2_, f32[2,7,8,128]{3,2,1,0:T(8,128)} %collective-permute-done.refs_2_.refs_3_, ...), custom_call_target="tpu_custom_call" | custom-call | bytes 39000000 | tf_op jit(solution)/shard_map/sweep/pallas_call | solution.py:494
  59.3 1.6 %collective-permute-start.12 = (f32[64,8,512]{2,1,0:T(8,128)}, f32[64,8,512]{2,1,0:T(8,128)}, u32[]{:S(2)}, u32[]{:S(2)}) collective-permute-start(f32[64,8,512]{2,1,0:T(8,128)} %get-tuple-element.28.refs_5_), channel_id=1, source_target_pairs={{8,16},{16,8},{9,17},{17,9},{10,18},{18,10},{11,19},{19,11},{12,20... | collective-permute-start | bytes 3145736 | tf_op jit(solution)/shard_map/ppermute | solution.py:871
  60.9 3.7 %local_heads.1.refs_0_ = f32[8,128]{1,0:T(8,128)} custom-call(f32[64,8,512]{2,1,0:T(8,128)} %get-tuple-element.27.refs_0_.refs_4_, s32[32]{0:T(128)} %refs_1_.7, f32[2,7,8,128]{3,2,1,0:T(8,128)} %get-tuple-element.18.refs_0_.refs_1_.refs_2_, f32[2,7,8,128]{3,2,1,0:T(8,128)} %collective-permute-done.refs_2_.refs_3_, ...), custom_call_target="tpu_custom_call" | custom-call | bytes 15000000 | tf_op jit(solution)/shard_map/local_heads/pallas_call | solution.py:741
  66.7 1.5 %collective-permute-start.6 = (f32[8,128]{1,0:T(8,128)S(1)}, f32[8,128]{1,0:T(8,128)S(1)}, u32[]{:S(2)}, u32[]{:S(2)}) collective-permute-start(f32[8,128]{1,0:T(8,128)S(1)} %add.9), channel_id=1, source_target_pairs={{0,2},{1,3},{2,0},{3,1},{4,6},{5,7},{6,4},{7,5},{8,10},{9,11},{10,... | collective-permute-start | bytes 12296 | tf_op jit(solution)/shard_map/ppermute | solution.py:862
  68.2 2.2 %collective-permute-done.6 = f32[8,128]{1,0:T(8,128)S(1)} collective-permute-done((f32[8,128]{1,0:T(8,128)S(1)}, f32[8,128]{1,0:T(8,128)S(1)}, u32[]{:S(2)}, u32[]{:S(2)}) %collective-permute-start.6) | collective-permute-done | bytes 4128 | tf_op jit(solution)/shard_map/ppermute | solution.py:862
  70.4 1.5 %collective-permute-start.7 = (f32[8,128]{1,0:T(8,128)S(1)}, f32[8,128]{1,0:T(8,128)S(1)}, u32[]{:S(2)}, u32[]{:S(2)}) collective-permute-start(f32[8,128]{1,0:T(8,128)S(1)} %add.10), channel_id=1, source_target_pairs={{0,4},{1,5},{2,6},{3,7},{4,0},{5,1},{6,2},{7,3},{8,12},{9,13},{10,... | collective-permute-start | bytes 12296 | tf_op jit(solution)/shard_map/ppermute | solution.py:862
  71.9 2.1 %collective-permute-done.7 = f32[8,128]{1,0:T(8,128)S(1)} collective-permute-done((f32[8,128]{1,0:T(8,128)S(1)}, f32[8,128]{1,0:T(8,128)S(1)}, u32[]{:S(2)}, u32[]{:S(2)}) %collective-permute-start.7) | collective-permute-done | bytes 4128 | tf_op jit(solution)/shard_map/ppermute | solution.py:862
  74.6 2.6 %collective-permute-start.10 = (f32[8,128]{1,0:T(8,128)}, f32[8,128]{1,0:T(8,128)}, u32[]{:S(2)}, u32[]{:S(2)}) collective-permute-start(f32[8,128]{1,0:T(8,128)} %add.11.refs_1_.refs_5_), channel_id=1, source_target_pairs={{0,24},{8,16},{16,8},{24,0},{1,25},{9,17},{17,9},{25,1},{2,26},{10... | collective-permute-start | bytes 12296 | tf_op jit(solution)/shard_map/ppermute | solution.py:862
  79.0 7.3 %sweep.8.refs_0_.refs_12_ = f32[2,64,8,512]{3,2,1,0:T(8,128)} custom-call(f32[8,128]{1,0:T(8,128)} %local_heads.1.refs_0_, f32[2,64,512]{2,1,0:T(8,128)} %get-tuple-element.25.refs_6_.refs_1_, f32[72,8,512]{2,1,0:T(8,128)} %get-tuple-element.19.refs_2_.refs_8_.refs_5_.refs_1_.refs_9_, f32[72,8,512]{2,1,0:T(8,128)} %get-tuple-element.20.refs_3_.refs_9_.refs_6_.refs_2_, ...), custom_call_target="tpu_custom_call" | custom-call | bytes 39000000 | tf_op jit(solution)/shard_map/sweep/pallas_call | solution.py:494
  86.4 7.8 %sweep.9 = (f32[64,8,512]{2,1,0:T(8,128)}, f32[64,8,512]{2,1,0:T(8,128)}) custom-call(f32[2,64,8,512]{3,2,1,0:T(8,128)} %sweep.8.refs_0_.refs_12_, f32[8,128]{1,0:T(8,128)} %add.11.refs_1_.refs_5_, f32[8,128]{1,0:T(8,128)} %collective-permute-done.8.refs_2_.refs_6_, f32[8,128]{1,0:T(8,128)} %collective-permute-done.9.refs_3_.refs_7_, ...), custom_call_target="tpu_custom_call" | custom-call | bytes 39000000 | tf_op jit(solution)/shard_map/sweep/pallas_call | solution.py:494
  94.1 2.1 %collective-permute-start.13 = (f32[64,8,512]{2,1,0:T(8,128)}, f32[64,8,512]{2,1,0:T(8,128)}, u32[]{:S(2)}, u32[]{:S(2)}) collective-permute-start(f32[64,8,512]{2,1,0:T(8,128)} %get-tuple-element.30.refs_0_.refs_4_), channel_id=1, source_target_pairs={{0,8},{16,24},{8,0},{24,16},{1,9},{17,25},{9,1},{25,17},{2,10},{18... | collective-permute-start | bytes 3145736 | tf_op jit(solution)/shard_map/ppermute | solution.py:871
  96.2 1.6 %collective-permute-start.14 = (f32[64,8,512]{2,1,0:T(8,128)}, f32[64,8,512]{2,1,0:T(8,128)}, u32[]{:S(2)}, u32[]{:S(2)}) collective-permute-start(f32[64,8,512]{2,1,0:T(8,128)} %get-tuple-element.31.refs_5_), channel_id=1, source_target_pairs={{8,16},{16,8},{9,17},{17,9},{10,18},{18,10},{11,19},{19,11},{12,20... | collective-permute-start | bytes 3145736 | tf_op jit(solution)/shard_map/ppermute | solution.py:871
  98.5 7.3 %sweep.10.refs_0_.refs_8_ = f32[2,64,8,512]{3,2,1,0:T(8,128)} custom-call(f32[64,8,512]{2,1,0:T(8,128)} %get-tuple-element.30.refs_0_.refs_4_, f32[2,64,512]{2,1,0:T(8,128)} %get-tuple-element.25.refs_6_.refs_1_, f32[72,8,512]{2,1,0:T(8,128)} %get-tuple-element.19.refs_2_.refs_8_.refs_5_.refs_1_.refs_9_, ...), custom_call_target="tpu_custom_call" | custom-call | bytes 39000000 | tf_op jit(solution)/shard_map/sweep/pallas_call | solution.py:494
  105.8 10.9 %update.1.refs_0_ = f32[8,2,64,512]{3,2,1,0:T(8,128)} custom-call(f32[2,64,8,512]{3,2,1,0:T(8,128)} %sweep.10.refs_0_.refs_8_, f32[1,32]{1,0:T(1,128)} %bitcast.4, f32[1,32]{1,0:T(1,128)} %bitcast.5, f32[1]{0:T(128)S(6)} %copy.12.refs_3_, f32[8,32]{1,0:T(8,128)} %refs_4_.3, f32[8,128]{1,0:T(8,128)} %add.11.refs_1_.refs_5_, ...), custom_call_target="tpu_custom_call" | custom-call | bytes 12000000 | tf_op jit(solution)/shard_map/update/pallas_call | solution.py:844
  117.7 8.2 %sweep.11 = f32[8,2,64,512]{3,2,1,0:T(8,128)} custom-call(f32[8,2,64,512]{3,2,1,0:T(8,128)} %update.1.refs_0_, f32[72,8,512]{2,1,0:T(8,128)} %get-tuple-element.19.refs_2_.refs_8_.refs_5_.refs_1_.refs_9_, f32[72,8,512]{2,1,0:T(8,128)} %get-tuple-element.20.refs_3_.refs_9_.refs_6_.refs_2_, f32[72,8,512]{2,1,0:T(8,128)} %collective-permute-done.3.refs_10_.refs_7_.refs_3_, ...), custom_call_target="tpu_custom_call" | custom-call | bytes 39000000 | tf_op jit(solution)/shard_map/sweep/pallas_call | solution.py:494
  (22 shorter events, 6.8 us)
Async XLA Ops:
  7.2 98.6 %all-gather.3.cloned.1.call-start = ((), (), s32[]{:S(2)}) async-start(), calls=%async_computation | async-start | bytes 18874368 | tf_op jit(solution)/shard_map/all_gather | solution.py:906
  11.6 37.9 %collective-permute-start.3 = (f32[72,8,512]{2,1,0:T(8,128)}, f32[72,8,512]{2,1,0:T(8,128)}, u32[]{:S(2)}, u32[]{:S(2)}) collective-permute-start(f32[72,8,512]{2,1,0:T(8,128)} %get-tuple-element.19.refs_2_.refs_8_.refs_5_.refs_1_.refs_9_), channel_id=1, source_target_pairs={{0,8},{16,24},{8,0},{24,16},{1,9},{17,25},{9,1},{25,17},{2,10},{18... | collective-permute-start | bytes 3538952 | tf_op jit(solution)/shard_map/ppermute | solution.py:871
  14.7 34.8 %collective-permute-start.4 = (f32[72,8,512]{2,1,0:T(8,128)}, f32[72,8,512]{2,1,0:T(8,128)}, u32[]{:S(2)}, u32[]{:S(2)}) collective-permute-start(f32[72,8,512]{2,1,0:T(8,128)} %get-tuple-element.20.refs_3_.refs_9_.refs_6_.refs_2_), channel_id=1, source_target_pairs={{8,16},{16,8},{9,17},{17,9},{10,18},{18,10},{11,19},{19,11},{12,20... | collective-permute-start | bytes 3538952 | tf_op jit(solution)/shard_map/ppermute | solution.py:871
  22.9 19.7 %collective-permute-start = (f32[2,7,8,128]{3,2,1,0:T(8,128)}, f32[2,7,8,128]{3,2,1,0:T(8,128)}, u32[]{:S(2)}, u32[]{:S(2)}) collective-permute-start(f32[2,7,8,128]{3,2,1,0:T(8,128)} %get-tuple-element.22), channel_id=1, source_target_pairs={{0,8},{8,0},{16,24},{24,16},{1,9},{9,1},{17,25},{25,17},{2,10},{10... | collective-permute-start | bytes 172040 | tf_op jit(solution)/shard_map/ppermute | solution.py:862
  26.3 23.2 %collective-permute-start.1 = (f32[2,7,8,128]{3,2,1,0:T(8,128)}, f32[2,7,8,128]{3,2,1,0:T(8,128)}, u32[]{:S(2)}, u32[]{:S(2)}) collective-permute-start(f32[2,7,8,128]{3,2,1,0:T(8,128)} %get-tuple-element.23), channel_id=1, source_target_pairs={{0,16},{8,24},{16,0},{24,8},{1,17},{9,25},{17,1},{25,9},{2,18},{10... | collective-permute-start | bytes 172040 | tf_op jit(solution)/shard_map/ppermute | solution.py:862
  26.3 23.2 %collective-permute-start.2 = (f32[2,7,8,128]{3,2,1,0:T(8,128)}, f32[2,7,8,128]{3,2,1,0:T(8,128)}, u32[]{:S(2)}, u32[]{:S(2)}) collective-permute-start(f32[2,7,8,128]{3,2,1,0:T(8,128)} %get-tuple-element.24), channel_id=1, source_target_pairs={{0,24},{8,16},{16,8},{24,0},{1,25},{9,17},{17,9},{25,1},{2,26},{10... | collective-permute-start | bytes 172040 | tf_op jit(solution)/shard_map/ppermute | solution.py:862
  58.1 28.3 %collective-permute-start.11 = (f32[64,8,512]{2,1,0:T(8,128)}, f32[64,8,512]{2,1,0:T(8,128)}, u32[]{:S(2)}, u32[]{:S(2)}) collective-permute-start(f32[64,8,512]{2,1,0:T(8,128)} %get-tuple-element.27.refs_0_.refs_4_), channel_id=1, source_target_pairs={{0,8},{16,24},{8,0},{24,16},{1,9},{17,25},{9,1},{25,17},{2,10},{18... | collective-permute-start | bytes 3145736 | tf_op jit(solution)/shard_map/ppermute | solution.py:871
  59.3 27.1 %collective-permute-start.12 = (f32[64,8,512]{2,1,0:T(8,128)}, f32[64,8,512]{2,1,0:T(8,128)}, u32[]{:S(2)}, u32[]{:S(2)}) collective-permute-start(f32[64,8,512]{2,1,0:T(8,128)} %get-tuple-element.28.refs_5_), channel_id=1, source_target_pairs={{8,16},{16,8},{9,17},{17,9},{10,18},{18,10},{11,19},{19,11},{12,20... | collective-permute-start | bytes 3145736 | tf_op jit(solution)/shard_map/ppermute | solution.py:871
  64.7 1.4 %collective-permute-start.5 = (f32[8,128]{1,0:T(8,128)}, f32[8,128]{1,0:T(8,128)S(1)}, u32[]{:S(2)}, u32[]{:S(2)}) collective-permute-start(f32[8,128]{1,0:T(8,128)} %local_heads.1.refs_0_), channel_id=1, source_target_pairs={{0,1},{1,0},{2,3},{3,2},{4,5},{5,4},{6,7},{7,6},{8,9},{9,8},{10,11... | collective-permute-start | bytes 12296 | tf_op jit(solution)/shard_map/ppermute | solution.py:862
  66.7 3.7 %collective-permute-start.6 = (f32[8,128]{1,0:T(8,128)S(1)}, f32[8,128]{1,0:T(8,128)S(1)}, u32[]{:S(2)}, u32[]{:S(2)}) collective-permute-start(f32[8,128]{1,0:T(8,128)S(1)} %add.9), channel_id=1, source_target_pairs={{0,2},{1,3},{2,0},{3,1},{4,6},{5,7},{6,4},{7,5},{8,10},{9,11},{10,... | collective-permute-start | bytes 12296 | tf_op jit(solution)/shard_map/ppermute | solution.py:862
  70.4 3.7 %collective-permute-start.7 = (f32[8,128]{1,0:T(8,128)S(1)}, f32[8,128]{1,0:T(8,128)S(1)}, u32[]{:S(2)}, u32[]{:S(2)}) collective-permute-start(f32[8,128]{1,0:T(8,128)S(1)} %add.10), channel_id=1, source_target_pairs={{0,4},{1,5},{2,6},{3,7},{4,0},{5,1},{6,2},{7,3},{8,12},{9,13},{10,... | collective-permute-start | bytes 12296 | tf_op jit(solution)/shard_map/ppermute | solution.py:862
  74.6 11.7 %collective-permute-start.10 = (f32[8,128]{1,0:T(8,128)}, f32[8,128]{1,0:T(8,128)}, u32[]{:S(2)}, u32[]{:S(2)}) collective-permute-start(f32[8,128]{1,0:T(8,128)} %add.11.refs_1_.refs_5_), channel_id=1, source_target_pairs={{0,24},{8,16},{16,8},{24,0},{1,25},{9,17},{17,9},{25,1},{2,26},{10... | collective-permute-start | bytes 12296 | tf_op jit(solution)/shard_map/ppermute | solution.py:862
  77.3 9.1 %collective-permute-start.8 = (f32[8,128]{1,0:T(8,128)}, f32[8,128]{1,0:T(8,128)}, u32[]{:S(2)}, u32[]{:S(2)}) collective-permute-start(f32[8,128]{1,0:T(8,128)} %add.11.refs_1_.refs_5_), channel_id=1, source_target_pairs={{0,8},{8,0},{16,24},{24,16},{1,9},{9,1},{17,25},{25,17},{2,10},{10... | collective-permute-start | bytes 12296 | tf_op jit(solution)/shard_map/ppermute | solution.py:862
  77.8 8.5 %collective-permute-start.9 = (f32[8,128]{1,0:T(8,128)}, f32[8,128]{1,0:T(8,128)}, u32[]{:S(2)}, u32[]{:S(2)}) collective-permute-start(f32[8,128]{1,0:T(8,128)} %add.11.refs_1_.refs_5_), channel_id=1, source_target_pairs={{0,16},{8,24},{16,0},{24,8},{1,17},{9,25},{17,1},{25,9},{2,18},{10... | collective-permute-start | bytes 12296 | tf_op jit(solution)/shard_map/ppermute | solution.py:862
  94.1 23.6 %collective-permute-start.13 = (f32[64,8,512]{2,1,0:T(8,128)}, f32[64,8,512]{2,1,0:T(8,128)}, u32[]{:S(2)}, u32[]{:S(2)}) collective-permute-start(f32[64,8,512]{2,1,0:T(8,128)} %get-tuple-element.30.refs_0_.refs_4_), channel_id=1, source_target_pairs={{0,8},{16,24},{8,0},{24,16},{1,9},{17,25},{9,1},{25,17},{2,10},{18... | collective-permute-start | bytes 3145736 | tf_op jit(solution)/shard_map/ppermute | solution.py:871
  96.2 21.5 %collective-permute-start.14 = (f32[64,8,512]{2,1,0:T(8,128)}, f32[64,8,512]{2,1,0:T(8,128)}, u32[]{:S(2)}, u32[]{:S(2)}) collective-permute-start(f32[64,8,512]{2,1,0:T(8,128)} %get-tuple-element.31.refs_5_), channel_id=1, source_target_pairs={{8,16},{16,8},{9,17},{17,9},{10,18},{18,10},{11,19},{19,11},{12,20... | collective-permute-start | bytes 3145736 | tf_op jit(solution)/shard_map/ppermute | solution.py:871
Sparse Core Ops, SparseCore 0:
  11.7 92.6 all-gather.2

commit v5 on v4

--- a/solution.py
+++ b/solution.py
@@ -502,7 +502,7 @@
     )(*operands)
 
 
-WAITS = {1: ("patches",), 2: ("partial",)}
+WAITS = {2: ("partial",)}
 CUTS = (None,)
 ORDER = (
     "planes",
@@ -685,7 +685,7 @@
             FO[i, d] = jnp.where(inside, rest[2:3], 0.0)
         return carry
 
-    lax.fori_loop(0, SIDE, select, 0)
+    lax.fori_loop(0, SIDE, select, 0, unroll=True)
     rs, hs = (RM, R, RP), (HM, H, HP)
 
     def update(i, d, first):
@@ -720,7 +720,7 @@
                 NEW[i, d] = update(i, d, sweep == 1)
             return carry
 
-        lax.fori_loop(sweep, SIDE - sweep, body, 0)
+        lax.fori_loop(sweep, SIDE - sweep, body, 0, unroll=True)
         for i in range(sweep, SIDE - sweep):
             for d in range(sweep, SIDE - sweep):
                 spread(H, HM, HP, i, d, NEW[i, d])
@@ -980,7 +980,11 @@
         else:
             if first:
                 state["weights"] = out[2]
-            state["new"] = (out[0], out[1], halo(out[0], 0), halo(out[1], 1))
+            sent = out[:2]
+            if first:
+                held = lax.optimization_barrier((*sent, *state["patches"]))
+                sent, state["patches"] = held[:2], list(held[2:])
+            state["new"] = (out[0], out[1], halo(sent[0], 0), halo(sent[1], 1))
         after(out[0])
 
     steps = dict(

time: 134 us -> 131 us (0.978)
  waiting for transfers between devices: 19.4 us -> 12.3 us
  starting transfers between devices: 24.6 us -> 30.5 us
    ppermute x9, waiting for transfers between devices: 18.3 us -> 5.7 us  [swap(): lax.ppermute(x, axis, [(i, i ^ bit) for i in range(lax.axis_size(axis))])]
    ppermute x6, starting transfers between devices: 11.4 us -> 17.2 us  [halo(): return lax.ppermute(x, 'space', pairs + [(b, a) for a, b in pairs])]
    ppermute x6, waiting for transfers between devices: 1.06 us -> 4.75 us  [halo(): return lax.ppermute(x, 'space', pairs + [(b, a) for a, b in pairs])]
    all_gather x1, waiting for transfers between devices: 0.02 us -> 1.83 us  [planes_step(): state['every'] = lax.all_gather(own, 'ens', axis=0)]
  transfers between devices with their start and end apart: 16 -> 16, of which waited for: 6 -> 5; matrix products, arithmetic and copies ran while one was open for 1% -> 1% of each run, Pallas kernels for 45% -> 45%
where the time goes in v5:
time: 131 us; the launch traced here: 130 us
  Pallas kernels  71.4 us (55%)
  starting transfers between devices  30.5 us (23%)
  between operations  14.8 us (11%)
  waiting for transfers between devices  12.3 us (9%)
    pallas_call x6, Pallas kernels, sweep_of(): call(functools.partial(sweep_kernel, cfg), 'sweep', out_shape, [ANY] * le...  47.2 us
    ppermute x6, starting transfers between devices, halo(): return lax.ppermute(x, 'space', pairs + [(b, a) for a, b in pairs])  17.2 us
    ppermute x9, starting transfers between devices, swap(): lax.ppermute(x, axis, [(i, i ^ bit) for i in range(lax.axis_size(axis))])  13.3 us
    pallas_call x1, Pallas kernels, update_of(): call(functools.partial(update_kernel, step, nobs), 'update', jax.ShapeDty...  10.9 us
    pallas_call x1, Pallas kernels, gather_of(): call(functools.partial(gather_kernel, slabs), 'gather', [jax.ShapeDtypeSt...  6.47 us
    ppermute x9, waiting for transfers between devices, swap(): lax.ppermute(x, axis, [(i, i ^ bit) for i in range(lax.axis_size(axis))])  5.7 us
    ppermute x6, waiting for transfers between devices, halo(): return lax.ppermute(x, 'space', pairs + [(b, a) for a, b in pairs])  4.75 us
    pallas_call x1, Pallas kernels, planes_of(): call(functools.partial(planes_kernel, step, cut), 'planes', sides * 2 + [...  4.35 us
  transfers between devices with their start and end apart: 16, of which 5 were waited for; matrix products, arithmetic and copies ran while one was open for 1% of the time, Pallas kernels for 45%

profile of v5, /device:TPU:0, one launch (start us, length us, event | category | flops | bytes accessed | tf_op | source)
XLA Modules:
  0.0 130.3 jit_solution(10000362507485148293)
XLA Ops:
  7.2 4.3 %planes.1 = (f32[72,8,512]{2,1,0:T(8,128)}, f32[72,8,512]{2,1,0:T(8,128)}, f32[2,64,8,512]{3,2,1,0:T(8,128)}) custom-call(f32[8,2,64,512]{3,2,1,0:T(8,128)} %refs_0_.2, f32[2,64,512]{2,1,0:T(8,128)} %refs_1_.8), custom_call_target="tpu_custom_call" | custom-call | bytes 12000000 | tf_op jit(solution)/shard_map/planes/pallas_call | solution.py:126
  11.6 3.1 %collective-permute-start = (f32[72,8,512]{2,1,0:T(8,128)}, f32[72,8,512]{2,1,0:T(8,128)}, u32[]{:S(2)}, u32[]{:S(2)}) collective-permute-start(f32[72,8,512]{2,1,0:T(8,128)} %get-tuple-element.25.refs_2_.refs_4_.refs_5_.refs_1_.refs_9_), channel_id=1, source_target_pairs={{0,8},{16,24},{8,0},{24,16},{1,9},{17,25},{9,1},{25,17},{2,10},{18... | collective-permute-start | bytes 3538952 | tf_op jit(solution)/shard_map/ppermute | solution.py:871
  14.7 1.7 %collective-permute-start.1 = (f32[72,8,512]{2,1,0:T(8,128)}, f32[72,8,512]{2,1,0:T(8,128)}, u32[]{:S(2)}, u32[]{:S(2)}) collective-permute-start(f32[72,8,512]{2,1,0:T(8,128)} %get-tuple-element.26.refs_3_.refs_5_.refs_6_.refs_2_), channel_id=1, source_target_pairs={{8,16},{16,8},{9,17},{17,9},{10,18},{18,10},{11,19},{19,11},{12,20... | collective-permute-start | bytes 3538952 | tf_op jit(solution)/shard_map/ppermute | solution.py:871
  16.4 6.5 %gather.1 = (f32[2,7,8,128]{3,2,1,0:T(8,128)}, f32[2,7,8,128]{3,2,1,0:T(8,128)}, f32[2,7,8,128]{3,2,1,0:T(8,128)}, f32[2,7,8,128]{3,2,1,0:T(8,128)}, f32[2,64,512]{2,1,0:T(8,128)}) custom-call(s32[16]{0:T(128)} %refs_0_.3, f32[16]{0:T(128)} %refs_1_.6, s32[32]{0:T(128)} %refs_1_.9, f32[2,64,512]{2,1,0:T(8,128)} %refs_1_.8, f32[2,64,512]{2,1,0:T(8,128)} %refs_3_.4, ...), custom_call_target="tpu_custom_call" | custom-call | bytes 18000000 | tf_op jit(solution)/shard_map/gather/pallas_call | solution.py:635
  22.9 3.4 %collective-permute-start.2 = (f32[2,7,8,128]{3,2,1,0:T(8,128)}, f32[2,7,8,128]{3,2,1,0:T(8,128)}, u32[]{:S(2)}, u32[]{:S(2)}) collective-permute-start(f32[2,7,8,128]{3,2,1,0:T(8,128)} %get-tuple-element.32), channel_id=1, source_target_pairs={{0,8},{8,0},{16,24},{24,16},{1,9},{9,1},{17,25},{25,17},{2,10},{10... | collective-permute-start | bytes 172040 | tf_op jit(solution)/shard_map/ppermute | solution.py:862
  26.3 2.4 %collective-permute-start.4 = (f32[2,7,8,128]{3,2,1,0:T(8,128)}, f32[2,7,8,128]{3,2,1,0:T(8,128)}, u32[]{:S(2)}, u32[]{:S(2)}) collective-permute-start(f32[2,7,8,128]{3,2,1,0:T(8,128)} %get-tuple-element.34), channel_id=1, source_target_pairs={{0,24},{8,16},{16,8},{24,0},{1,25},{9,17},{17,9},{25,1},{2,26},{10... | collective-permute-start | bytes 172040 | tf_op jit(solution)/shard_map/ppermute | solution.py:862
  28.8 8.1 %sweep.6 = (f32[2,64,8,512]{3,2,1,0:T(8,128)}, f32[2,64,8,512]{3,2,1,0:T(8,128)}) custom-call(f32[2,7,8,128]{3,2,1,0:T(8,128)} %get-tuple-element.35.refs_0_.refs_2_, f32[2,64,512]{2,1,0:T(8,128)} %refs_1_.8, f32[72,8,512]{2,1,0:T(8,128)} %get-tuple-element.25.refs_2_.refs_4_.refs_5_.refs_1_.refs_9_, ...), custom_call_target="tpu_custom_call" | custom-call | bytes 39000000 | tf_op jit(solution)/shard_map/sweep/pallas_call | solution.py:494
  36.8 4.7 %collective-permute-done.refs_6_.refs_7_.refs_3_ = f32[72,8,512]{2,1,0:T(8,128)} collective-permute-done((f32[72,8,512]{2,1,0:T(8,128)}, f32[72,8,512]{2,1,0:T(8,128)}, u32[]{:S(2)}, u32[]{:S(2)}) %collective-permute-start) | collective-permute-done | bytes 1179680 | tf_op jit(solution)/shard_map/ppermute | solution.py:871
  41.6 8.6 %sweep.7 = (f32[64,8,512]{2,1,0:T(8,128)}, f32[64,8,512]{2,1,0:T(8,128)}, f32[2,64,8,512]{3,2,1,0:T(8,128)}) custom-call(f32[2,64,8,512]{3,2,1,0:T(8,128)} %get-tuple-element.27.refs_0_.refs_8_, f32[2,64,512]{2,1,0:T(8,128)} %refs_1_.8, f32[2,64,512]{2,1,0:T(8,128)} %get-tuple-element.28.refs_2_.refs_1_, f32[2,64,512]{2,1,0:T(8,128)} %refs_3_.4, ...), custom_call_target="tpu_custom_call" | custom-call | bytes 39000000 | tf_op jit(solution)/shard_map/sweep/pallas_call | solution.py:494
  50.2 7.8 %collective-permute-start.11 = (f32[64,8,512]{2,1,0:T(8,128)}, f32[64,8,512]{2,1,0:T(8,128)}, u32[]{:S(2)}, u32[]{:S(2)}) collective-permute-start(f32[64,8,512]{2,1,0:T(8,128)} %get-tuple-element.40.refs_0_.refs_4_), channel_id=1, source_target_pairs={{0,8},{16,24},{8,0},{24,16},{1,9},{17,25},{9,1},{25,17},{2,10},{18... | collective-permute-start | bytes 3145736 | tf_op jit(solution)/shard_map/ppermute | solution.py:871
  58.0 1.6 %collective-permute-start.12 = (f32[64,8,512]{2,1,0:T(8,128)}, f32[64,8,512]{2,1,0:T(8,128)}, u32[]{:S(2)}, u32[]{:S(2)}) collective-permute-start(f32[64,8,512]{2,1,0:T(8,128)} %get-tuple-element.41.refs_5_), channel_id=1, source_target_pairs={{8,16},{16,8},{9,17},{17,9},{10,18},{18,10},{11,19},{19,11},{12,20... | collective-permute-start | bytes 3145736 | tf_op jit(solution)/shard_map/ppermute | solution.py:871
  59.7 2.6 %local_heads.1.refs_0_ = f32[8,128]{1,0:T(8,128)} custom-call(f32[64,8,512]{2,1,0:T(8,128)} %get-tuple-element.40.refs_0_.refs_4_, s32[32]{0:T(128)} %refs_1_.9, f32[2,7,8,128]{3,2,1,0:T(8,128)} %get-tuple-element.35.refs_0_.refs_2_, f32[2,7,8,128]{3,2,1,0:T(8,128)} %collective-permute-done.2.refs_3_, f32[2,7,8,128]{3,2,1,0:T(8,128)} %collective-permute-done.3.refs_4_, ...), custom_call_target="tpu_custom_call" | custom-call | bytes 15000000 | tf_op jit(solution)/shard_map/local_heads/pallas_call | solution.py:741
  65.8 2.2 %collective-permute-done.6 = f32[8,128]{1,0:T(8,128)S(1)} collective-permute-done((f32[8,128]{1,0:T(8,128)S(1)}, f32[8,128]{1,0:T(8,128)S(1)}, u32[]{:S(2)}, u32[]{:S(2)}) %collective-permute-start.6) | collective-permute-done | bytes 4128 | tf_op jit(solution)/shard_map/ppermute | solution.py:862
  67.9 1.5 %collective-permute-start.7 = (f32[8,128]{1,0:T(8,128)S(1)}, f32[8,128]{1,0:T(8,128)S(1)}, u32[]{:S(2)}, u32[]{:S(2)}) collective-permute-start(f32[8,128]{1,0:T(8,128)S(1)} %add.10), channel_id=1, source_target_pairs={{0,4},{1,5},{2,6},{3,7},{4,0},{5,1},{6,2},{7,3},{8,12},{9,13},{10,... | collective-permute-start | bytes 12296 | tf_op jit(solution)/shard_map/ppermute | solution.py:862
  69.5 2.1 %collective-permute-done.7 = f32[8,128]{1,0:T(8,128)S(1)} collective-permute-done((f32[8,128]{1,0:T(8,128)S(1)}, f32[8,128]{1,0:T(8,128)S(1)}, u32[]{:S(2)}, u32[]{:S(2)}) %collective-permute-start.7) | collective-permute-done | bytes 4128 | tf_op jit(solution)/shard_map/ppermute | solution.py:862
  72.2 2.7 %collective-permute-start.10 = (f32[8,128]{1,0:T(8,128)}, f32[8,128]{1,0:T(8,128)}, u32[]{:S(2)}, u32[]{:S(2)}) collective-permute-start(f32[8,128]{1,0:T(8,128)} %add.11.refs_1_.refs_5_), channel_id=1, source_target_pairs={{0,24},{8,16},{16,8},{24,0},{1,25},{9,17},{17,9},{25,1},{2,26},{10... | collective-permute-start | bytes 12296 | tf_op jit(solution)/shard_map/ppermute | solution.py:862
  74.9 1.7 %collective-permute-start.9 = (f32[8,128]{1,0:T(8,128)}, f32[8,128]{1,0:T(8,128)}, u32[]{:S(2)}, u32[]{:S(2)}) collective-permute-start(f32[8,128]{1,0:T(8,128)} %add.11.refs_1_.refs_5_), channel_id=1, source_target_pairs={{0,16},{8,24},{16,0},{24,8},{1,17},{9,25},{17,1},{25,9},{2,18},{10... | collective-permute-start | bytes 12296 | tf_op jit(solution)/shard_map/ppermute | solution.py:862
  76.6 7.3 %sweep.8.refs_0_.refs_12_ = f32[2,64,8,512]{3,2,1,0:T(8,128)} custom-call(f32[8,128]{1,0:T(8,128)} %local_heads.1.refs_0_, f32[2,64,512]{2,1,0:T(8,128)} %get-tuple-element.28.refs_2_.refs_1_, f32[72,8,512]{2,1,0:T(8,128)} %get-tuple-element.25.refs_2_.refs_4_.refs_5_.refs_1_.refs_9_, f32[72,8,512]{2,1,0:T(8,128)} %get-tuple-element.26.refs_3_.refs_5_.refs_6_.refs_2_, ...), custom_call_target="tpu_custom_call" | custom-call | bytes 39000000 | tf_op jit(solution)/shard_map/sweep/pallas_call | solution.py:494
  83.9 7.8 %sweep.9 = (f32[64,8,512]{2,1,0:T(8,128)}, f32[64,8,512]{2,1,0:T(8,128)}) custom-call(f32[2,64,8,512]{3,2,1,0:T(8,128)} %sweep.8.refs_0_.refs_12_, f32[8,128]{1,0:T(8,128)} %add.11.refs_1_.refs_5_, f32[8,128]{1,0:T(8,128)} %collective-permute-done.8.refs_2_.refs_6_, f32[8,128]{1,0:T(8,128)} %collective-permute-done.9.refs_3_.refs_7_, ...), custom_call_target="tpu_custom_call" | custom-call | bytes 39000000 | tf_op jit(solution)/shard_map/sweep/pallas_call | solution.py:494
  93.0 1.6 %collective-permute-start.14 = (f32[64,8,512]{2,1,0:T(8,128)}, f32[64,8,512]{2,1,0:T(8,128)}, u32[]{:S(2)}, u32[]{:S(2)}) collective-permute-start(f32[64,8,512]{2,1,0:T(8,128)} %get-tuple-element.43.refs_5_), channel_id=1, source_target_pairs={{8,16},{16,8},{9,17},{17,9},{10,18},{18,10},{11,19},{19,11},{12,20... | collective-permute-start | bytes 3145736 | tf_op jit(solution)/shard_map/ppermute | solution.py:871
  95.3 7.3 %sweep.10.refs_0_.refs_8_ = f32[2,64,8,512]{3,2,1,0:T(8,128)} custom-call(f32[64,8,512]{2,1,0:T(8,128)} %get-tuple-element.42.refs_0_.refs_4_, f32[2,64,512]{2,1,0:T(8,128)} %get-tuple-element.28.refs_2_.refs_1_, f32[72,8,512]{2,1,0:T(8,128)} %get-tuple-element.25.refs_2_.refs_4_.refs_5_.refs_1_.refs_9_, ...), custom_call_target="tpu_custom_call" | custom-call | bytes 39000000 | tf_op jit(solution)/shard_map/sweep/pallas_call | solution.py:494
  102.6 1.8 %all-gather.3.cloned.1.call-done = f32[16,64,8,512]{3,2,1,0:T(8,128)} async-done(((f32[2,64,8,512]{3,2,1,0:T(8,128)}), f32[16,64,8,512]{3,2,1,0:T(8,128)}) %all-gather.3.cloned.1.call-update) | async-done | bytes 16777232 | tf_op jit(solution)/shard_map/all_gather | solution.py:906
  104.4 10.9 %update.1.refs_0_ = f32[8,2,64,512]{3,2,1,0:T(8,128)} custom-call(f32[2,64,8,512]{3,2,1,0:T(8,128)} %sweep.10.refs_0_.refs_8_, f32[1,32]{1,0:T(1,128)} %bitcast.4, f32[1,32]{1,0:T(1,128)} %bitcast.5, f32[1]{0:T(128)S(6)} %copy.12.refs_3_, f32[8,32]{1,0:T(8,128)} %refs_4_.3, f32[8,128]{1,0:T(8,128)} %add.11.refs_1_.refs_5_, ...), custom_call_target="tpu_custom_call" | custom-call | bytes 12000000 | tf_op jit(solution)/shard_map/update/pallas_call | solution.py:844
  115.3 8.2 %sweep.11 = f32[8,2,64,512]{3,2,1,0:T(8,128)} custom-call(f32[8,2,64,512]{3,2,1,0:T(8,128)} %update.1.refs_0_, f32[72,8,512]{2,1,0:T(8,128)} %get-tuple-element.25.refs_2_.refs_4_.refs_5_.refs_1_.refs_9_, f32[72,8,512]{2,1,0:T(8,128)} %get-tuple-element.26.refs_3_.refs_5_.refs_6_.refs_2_, f32[72,8,512]{2,1,0:T(8,128)} %collective-permute-done.refs_6_.refs_7_.refs_3_, ...), custom_call_target="tpu_custom_call" | custom-call | bytes 39000000 | tf_op jit(solution)/shard_map/sweep/pallas_call | solution.py:494
  (22 shorter events, 5.5 us)
Async XLA Ops:
  7.2 97.2 %all-gather.3.cloned.1.call-start = ((), (), s32[]{:S(2)}) async-start(), calls=%async_computation | async-start | bytes 18874368 | tf_op jit(solution)/shard_map/all_gather | solution.py:906
  11.6 30.0 %collective-permute-start = (f32[72,8,512]{2,1,0:T(8,128)}, f32[72,8,512]{2,1,0:T(8,128)}, u32[]{:S(2)}, u32[]{:S(2)}) collective-permute-start(f32[72,8,512]{2,1,0:T(8,128)} %get-tuple-element.25.refs_2_.refs_4_.refs_5_.refs_1_.refs_9_), channel_id=1, source_target_pairs={{0,8},{16,24},{8,0},{24,16},{1,9},{17,25},{9,1},{25,17},{2,10},{18... | collective-permute-start | bytes 3538952 | tf_op jit(solution)/shard_map/ppermute | solution.py:871
  14.7 26.9 %collective-permute-start.1 = (f32[72,8,512]{2,1,0:T(8,128)}, f32[72,8,512]{2,1,0:T(8,128)}, u32[]{:S(2)}, u32[]{:S(2)}) collective-permute-start(f32[72,8,512]{2,1,0:T(8,128)} %get-tuple-element.26.refs_3_.refs_5_.refs_6_.refs_2_), channel_id=1, source_target_pairs={{8,16},{16,8},{9,17},{17,9},{10,18},{18,10},{11,19},{19,11},{12,20... | collective-permute-start | bytes 3538952 | tf_op jit(solution)/shard_map/ppermute | solution.py:871
  22.9 27.3 %collective-permute-start.2 = (f32[2,7,8,128]{3,2,1,0:T(8,128)}, f32[2,7,8,128]{3,2,1,0:T(8,128)}, u32[]{:S(2)}, u32[]{:S(2)}) collective-permute-start(f32[2,7,8,128]{3,2,1,0:T(8,128)} %get-tuple-element.32), channel_id=1, source_target_pairs={{0,8},{8,0},{16,24},{24,16},{1,9},{9,1},{17,25},{25,17},{2,10},{10... | collective-permute-start | bytes 172040 | tf_op jit(solution)/shard_map/ppermute | solution.py:862
  26.3 23.9 %collective-permute-start.3 = (f32[2,7,8,128]{3,2,1,0:T(8,128)}, f32[2,7,8,128]{3,2,1,0:T(8,128)}, u32[]{:S(2)}, u32[]{:S(2)}) collective-permute-start(f32[2,7,8,128]{3,2,1,0:T(8,128)} %get-tuple-element.33), channel_id=1, source_target_pairs={{0,16},{8,24},{16,0},{24,8},{1,17},{9,25},{17,1},{25,9},{2,18},{10... | collective-permute-start | bytes 172040 | tf_op jit(solution)/shard_map/ppermute | solution.py:862
  26.3 23.9 %collective-permute-start.4 = (f32[2,7,8,128]{3,2,1,0:T(8,128)}, f32[2,7,8,128]{3,2,1,0:T(8,128)}, u32[]{:S(2)}, u32[]{:S(2)}) collective-permute-start(f32[2,7,8,128]{3,2,1,0:T(8,128)} %get-tuple-element.34), channel_id=1, source_target_pairs={{0,24},{8,16},{16,8},{24,0},{1,25},{9,17},{17,9},{25,1},{2,26},{10... | collective-permute-start | bytes 172040 | tf_op jit(solution)/shard_map/ppermute | solution.py:862
  50.2 33.7 %collective-permute-start.11 = (f32[64,8,512]{2,1,0:T(8,128)}, f32[64,8,512]{2,1,0:T(8,128)}, u32[]{:S(2)}, u32[]{:S(2)}) collective-permute-start(f32[64,8,512]{2,1,0:T(8,128)} %get-tuple-element.40.refs_0_.refs_4_), channel_id=1, source_target_pairs={{0,8},{16,24},{8,0},{24,16},{1,9},{17,25},{9,1},{25,17},{2,10},{18... | collective-permute-start | bytes 3145736 | tf_op jit(solution)/shard_map/ppermute | solution.py:871
  58.0 25.9 %collective-permute-start.12 = (f32[64,8,512]{2,1,0:T(8,128)}, f32[64,8,512]{2,1,0:T(8,128)}, u32[]{:S(2)}, u32[]{:S(2)}) collective-permute-start(f32[64,8,512]{2,1,0:T(8,128)} %get-tuple-element.41.refs_5_), channel_id=1, source_target_pairs={{8,16},{16,8},{9,17},{17,9},{10,18},{18,10},{11,19},{19,11},{12,20... | collective-permute-start | bytes 3145736 | tf_op jit(solution)/shard_map/ppermute | solution.py:871
  62.2 1.4 %collective-permute-start.5 = (f32[8,128]{1,0:T(8,128)}, f32[8,128]{1,0:T(8,128)S(1)}, u32[]{:S(2)}, u32[]{:S(2)}) collective-permute-start(f32[8,128]{1,0:T(8,128)} %local_heads.1.refs_0_), channel_id=1, source_target_pairs={{0,1},{1,0},{2,3},{3,2},{4,5},{5,4},{6,7},{7,6},{8,9},{9,8},{10,11... | collective-permute-start | bytes 12296 | tf_op jit(solution)/shard_map/ppermute | solution.py:862
  64.3 3.7 %collective-permute-start.6 = (f32[8,128]{1,0:T(8,128)S(1)}, f32[8,128]{1,0:T(8,128)S(1)}, u32[]{:S(2)}, u32[]{:S(2)}) collective-permute-start(f32[8,128]{1,0:T(8,128)S(1)} %add.9), channel_id=1, source_target_pairs={{0,2},{1,3},{2,0},{3,1},{4,6},{5,7},{6,4},{7,5},{8,10},{9,11},{10,... | collective-permute-start | bytes 12296 | tf_op jit(solution)/shard_map/ppermute | solution.py:862
  67.9 3.7 %collective-permute-start.7 = (f32[8,128]{1,0:T(8,128)S(1)}, f32[8,128]{1,0:T(8,128)S(1)}, u32[]{:S(2)}, u32[]{:S(2)}) collective-permute-start(f32[8,128]{1,0:T(8,128)S(1)} %add.10), channel_id=1, source_target_pairs={{0,4},{1,5},{2,6},{3,7},{4,0},{5,1},{6,2},{7,3},{8,12},{9,13},{10,... | collective-permute-start | bytes 12296 | tf_op jit(solution)/shard_map/ppermute | solution.py:862
  72.2 11.7 %collective-permute-start.10 = (f32[8,128]{1,0:T(8,128)}, f32[8,128]{1,0:T(8,128)}, u32[]{:S(2)}, u32[]{:S(2)}) collective-permute-start(f32[8,128]{1,0:T(8,128)} %add.11.refs_1_.refs_5_), channel_id=1, source_target_pairs={{0,24},{8,16},{16,8},{24,0},{1,25},{9,17},{17,9},{25,1},{2,26},{10... | collective-permute-start | bytes 12296 | tf_op jit(solution)/shard_map/ppermute | solution.py:862
  74.9 9.0 %collective-permute-start.8 = (f32[8,128]{1,0:T(8,128)}, f32[8,128]{1,0:T(8,128)}, u32[]{:S(2)}, u32[]{:S(2)}) collective-permute-start(f32[8,128]{1,0:T(8,128)} %add.11.refs_1_.refs_5_), channel_id=1, source_target_pairs={{0,8},{8,0},{16,24},{24,16},{1,9},{9,1},{17,25},{25,17},{2,10},{10... | collective-permute-start | bytes 12296 | tf_op jit(solution)/shard_map/ppermute | solution.py:862
  74.9 9.0 %collective-permute-start.9 = (f32[8,128]{1,0:T(8,128)}, f32[8,128]{1,0:T(8,128)}, u32[]{:S(2)}, u32[]{:S(2)}) collective-permute-start(f32[8,128]{1,0:T(8,128)} %add.11.refs_1_.refs_5_), channel_id=1, source_target_pairs={{0,16},{8,24},{16,0},{24,8},{1,17},{9,25},{17,1},{25,9},{2,18},{10... | collective-permute-start | bytes 12296 | tf_op jit(solution)/shard_map/ppermute | solution.py:862
  91.7 23.6 %collective-permute-start.13 = (f32[64,8,512]{2,1,0:T(8,128)}, f32[64,8,512]{2,1,0:T(8,128)}, u32[]{:S(2)}, u32[]{:S(2)}) collective-permute-start(f32[64,8,512]{2,1,0:T(8,128)} %get-tuple-element.42.refs_0_.refs_4_), channel_id=1, source_target_pairs={{0,8},{16,24},{8,0},{24,16},{1,9},{17,25},{9,1},{25,17},{2,10},{18... | collective-permute-start | bytes 3145736 | tf_op jit(solution)/shard_map/ppermute | solution.py:871
  93.0 22.3 %collective-permute-start.14 = (f32[64,8,512]{2,1,0:T(8,128)}, f32[64,8,512]{2,1,0:T(8,128)}, u32[]{:S(2)}, u32[]{:S(2)}) collective-permute-start(f32[64,8,512]{2,1,0:T(8,128)} %get-tuple-element.43.refs_5_), channel_id=1, source_target_pairs={{8,16},{16,8},{9,17},{17,9},{10,18},{18,10},{11,19},{19,11},{12,20... | collective-permute-start | bytes 3145736 | tf_op jit(solution)/shard_map/ppermute | solution.py:871
Sparse Core Ops, SparseCore 0:
  11.7 92.6 all-gather.2

commit v6 on v5

--- a/solution.py
+++ b/solution.py
@@ -15,7 +15,7 @@
 SMEM = pl.BlockSpec(memory_space=pltpu.SMEM)
 ANY = pl.BlockSpec(memory_space=pl.ANY)
 REACH = 3
-DEEP = 3
+DEEP = 4
 MICROSECOND = 3.0e6
 EXPECTED = dict(planes=4, gather=6, sweep=13, local_heads=5, solve=5, mix=4, update=4)
 SLOT = 8
@@ -115,7 +115,7 @@
 
 def planes_of(lp, head, cut, after=()):
     members, planes, depth, across = lp.shape
-    step = 16
+    step = 8
     lines = depth // 8
     spans = row_spans(depth, cut)
     sides = [
@@ -188,7 +188,7 @@
 
     ends = []
     at = zlo
-    for width in (4, 8, 12, 12, 12, 12, 12):
+    for width in (4, 4, 8, 8, 8, 8, 8, 8, 8):
         if at >= zhi + 1:
             break
         ends.append(min(at + width, zhi + 1))
@@ -468,7 +468,7 @@
     operands = list(lines)
     for spans in fields.values():
         operands += [ref for ref, _, _ in spans]
-    copies = sum(len(spans) for spans in fields.values()) * 8 + 8
+    copies = sum(len(spans) for spans in fields.values()) * 10 + 8
     field = pltpu.VMEM((4, depth, members, across), F32)
     line = pltpu.VMEM((2, members, across), F32)
     flat = pltpu.VMEM((2, depth, across), F32)

time: 131 us -> 132 us (level)
  transfers between devices with their start and end apart: 16 -> 16, of which waited for: 5 -> 5; matrix products, arithmetic and copies ran while one was open for 1% -> 1% of each run, Pallas kernels for 45% -> 46%
where the time goes in v6:
time: 132 us; the launch traced here: 130 us
  Pallas kernels  71.9 us (54%)
  starting transfers between devices  30.6 us (23%)
  between operations  14.9 us (11%)
  waiting for transfers between devices  11.7 us (9%)
    pallas_call x6, Pallas kernels, sweep_of(): call(functools.partial(sweep_kernel, cfg), 'sweep', out_shape, [ANY] * le...  47.7 us
    ppermute x6, starting transfers between devices, halo(): return lax.ppermute(x, 'space', pairs + [(b, a) for a, b in pairs])  17.4 us
    ppermute x9, starting transfers between devices, swap(): lax.ppermute(x, axis, [(i, i ^ bit) for i in range(lax.axis_size(axis))])  13.2 us
    pallas_call x1, Pallas kernels, update_of(): call(functools.partial(update_kernel, step, nobs), 'update', jax.ShapeDty...  10.9 us
    pallas_call x1, Pallas kernels, gather_of(): call(functools.partial(gather_kernel, slabs), 'gather', [jax.ShapeDtypeSt...  6.5 us
    ppermute x9, waiting for transfers between devices, swap(): lax.ppermute(x, axis, [(i, i ^ bit) for i in range(lax.axis_size(axis))])  5.71 us
    ppermute x6, waiting for transfers between devices, halo(): return lax.ppermute(x, 'space', pairs + [(b, a) for a, b in pairs])  4.67 us
    pallas_call x1, Pallas kernels, planes_of(): call(functools.partial(planes_kernel, step, cut), 'planes', sides * 2 + [...  4.25 us
  transfers between devices with their start and end apart: 16, of which 5 were waited for; matrix products, arithmetic and copies ran while one was open for 1% of the time, Pallas kernels for 46%

profile of v6, /device:TPU:0, one launch (start us, length us, event | category | flops | bytes accessed | tf_op | source)
XLA Modules:
  0.0 130.3 jit_solution(17550136352792705439)
XLA Ops:
  7.2 4.3 %planes.1 = (f32[72,8,512]{2,1,0:T(8,128)}, f32[72,8,512]{2,1,0:T(8,128)}, f32[2,64,8,512]{3,2,1,0:T(8,128)}) custom-call(f32[8,2,64,512]{3,2,1,0:T(8,128)} %refs_0_.2, f32[2,64,512]{2,1,0:T(8,128)} %refs_1_.8), custom_call_target="tpu_custom_call" | custom-call | bytes 12000000 | tf_op jit(solution)/shard_map/planes/pallas_call | solution.py:126
  11.5 3.1 %collective-permute-start = (f32[72,8,512]{2,1,0:T(8,128)}, f32[72,8,512]{2,1,0:T(8,128)}, u32[]{:S(2)}, u32[]{:S(2)}) collective-permute-start(f32[72,8,512]{2,1,0:T(8,128)} %get-tuple-element.25.refs_2_.refs_4_.refs_5_.refs_1_.refs_9_), channel_id=1, source_target_pairs={{0,8},{16,24},{8,0},{24,16},{1,9},{17,25},{9,1},{25,17},{2,10},{18... | collective-permute-start | bytes 3538952 | tf_op jit(solution)/shard_map/ppermute | solution.py:871
  14.6 1.7 %collective-permute-start.1 = (f32[72,8,512]{2,1,0:T(8,128)}, f32[72,8,512]{2,1,0:T(8,128)}, u32[]{:S(2)}, u32[]{:S(2)}) collective-permute-start(f32[72,8,512]{2,1,0:T(8,128)} %get-tuple-element.26.refs_3_.refs_5_.refs_6_.refs_2_), channel_id=1, source_target_pairs={{8,16},{16,8},{9,17},{17,9},{10,18},{18,10},{11,19},{19,11},{12,20... | collective-permute-start | bytes 3538952 | tf_op jit(solution)/shard_map/ppermute | solution.py:871
  16.3 6.5 %gather.1 = (f32[2,7,8,128]{3,2,1,0:T(8,128)}, f32[2,7,8,128]{3,2,1,0:T(8,128)}, f32[2,7,8,128]{3,2,1,0:T(8,128)}, f32[2,7,8,128]{3,2,1,0:T(8,128)}, f32[2,64,512]{2,1,0:T(8,128)}) custom-call(s32[16]{0:T(128)} %refs_0_.3, f32[16]{0:T(128)} %refs_1_.6, s32[32]{0:T(128)} %refs_1_.9, f32[2,64,512]{2,1,0:T(8,128)} %refs_1_.8, f32[2,64,512]{2,1,0:T(8,128)} %refs_3_.4, ...), custom_call_target="tpu_custom_call" | custom-call | bytes 18000000 | tf_op jit(solution)/shard_map/gather/pallas_call | solution.py:635
  22.8 3.4 %collective-permute-start.2 = (f32[2,7,8,128]{3,2,1,0:T(8,128)}, f32[2,7,8,128]{3,2,1,0:T(8,128)}, u32[]{:S(2)}, u32[]{:S(2)}) collective-permute-start(f32[2,7,8,128]{3,2,1,0:T(8,128)} %get-tuple-element.32), channel_id=1, source_target_pairs={{0,8},{8,0},{16,24},{24,16},{1,9},{9,1},{17,25},{25,17},{2,10},{10... | collective-permute-start | bytes 172040 | tf_op jit(solution)/shard_map/ppermute | solution.py:862
  26.2 2.4 %collective-permute-start.4 = (f32[2,7,8,128]{3,2,1,0:T(8,128)}, f32[2,7,8,128]{3,2,1,0:T(8,128)}, u32[]{:S(2)}, u32[]{:S(2)}) collective-permute-start(f32[2,7,8,128]{3,2,1,0:T(8,128)} %get-tuple-element.34), channel_id=1, source_target_pairs={{0,24},{8,16},{16,8},{24,0},{1,25},{9,17},{17,9},{25,1},{2,26},{10... | collective-permute-start | bytes 172040 | tf_op jit(solution)/shard_map/ppermute | solution.py:862
  28.6 8.2 %sweep.6 = (f32[2,64,8,512]{3,2,1,0:T(8,128)}, f32[2,64,8,512]{3,2,1,0:T(8,128)}) custom-call(f32[2,7,8,128]{3,2,1,0:T(8,128)} %get-tuple-element.35.refs_0_.refs_2_, f32[2,64,512]{2,1,0:T(8,128)} %refs_1_.8, f32[72,8,512]{2,1,0:T(8,128)} %get-tuple-element.25.refs_2_.refs_4_.refs_5_.refs_1_.refs_9_, ...), custom_call_target="tpu_custom_call" | custom-call | bytes 39000000 | tf_op jit(solution)/shard_map/sweep/pallas_call | solution.py:494
  36.8 4.7 %collective-permute-done.refs_6_.refs_7_.refs_3_ = f32[72,8,512]{2,1,0:T(8,128)} collective-permute-done((f32[72,8,512]{2,1,0:T(8,128)}, f32[72,8,512]{2,1,0:T(8,128)}, u32[]{:S(2)}, u32[]{:S(2)}) %collective-permute-start) | collective-permute-done | bytes 1179680 | tf_op jit(solution)/shard_map/ppermute | solution.py:871
  41.5 8.7 %sweep.7 = (f32[64,8,512]{2,1,0:T(8,128)}, f32[64,8,512]{2,1,0:T(8,128)}, f32[2,64,8,512]{3,2,1,0:T(8,128)}) custom-call(f32[2,64,8,512]{3,2,1,0:T(8,128)} %get-tuple-element.27.refs_0_.refs_8_, f32[2,64,512]{2,1,0:T(8,128)} %refs_1_.8, f32[2,64,512]{2,1,0:T(8,128)} %get-tuple-element.28.refs_2_.refs_1_, f32[2,64,512]{2,1,0:T(8,128)} %refs_3_.4, ...), custom_call_target="tpu_custom_call" | custom-call | bytes 39000000 | tf_op jit(solution)/shard_map/sweep/pallas_call | solution.py:494
  50.2 7.8 %collective-permute-start.11 = (f32[64,8,512]{2,1,0:T(8,128)}, f32[64,8,512]{2,1,0:T(8,128)}, u32[]{:S(2)}, u32[]{:S(2)}) collective-permute-start(f32[64,8,512]{2,1,0:T(8,128)} %get-tuple-element.40.refs_0_.refs_4_), channel_id=1, source_target_pairs={{0,8},{16,24},{8,0},{24,16},{1,9},{17,25},{9,1},{25,17},{2,10},{18... | collective-permute-start | bytes 3145736 | tf_op jit(solution)/shard_map/ppermute | solution.py:871
  58.0 1.6 %collective-permute-start.12 = (f32[64,8,512]{2,1,0:T(8,128)}, f32[64,8,512]{2,1,0:T(8,128)}, u32[]{:S(2)}, u32[]{:S(2)}) collective-permute-start(f32[64,8,512]{2,1,0:T(8,128)} %get-tuple-element.41.refs_5_), channel_id=1, source_target_pairs={{8,16},{16,8},{9,17},{17,9},{10,18},{18,10},{11,19},{19,11},{12,20... | collective-permute-start | bytes 3145736 | tf_op jit(solution)/shard_map/ppermute | solution.py:871
  59.7 2.6 %local_heads.1.refs_0_ = f32[8,128]{1,0:T(8,128)} custom-call(f32[64,8,512]{2,1,0:T(8,128)} %get-tuple-element.40.refs_0_.refs_4_, s32[32]{0:T(128)} %refs_1_.9, f32[2,7,8,128]{3,2,1,0:T(8,128)} %get-tuple-element.35.refs_0_.refs_2_, f32[2,7,8,128]{3,2,1,0:T(8,128)} %collective-permute-done.2.refs_3_, f32[2,7,8,128]{3,2,1,0:T(8,128)} %collective-permute-done.3.refs_4_, ...), custom_call_target="tpu_custom_call" | custom-call | bytes 15000000 | tf_op jit(solution)/shard_map/local_heads/pallas_call | solution.py:741
  64.3 1.5 %collective-permute-start.6 = (f32[8,128]{1,0:T(8,128)S(1)}, f32[8,128]{1,0:T(8,128)S(1)}, u32[]{:S(2)}, u32[]{:S(2)}) collective-permute-start(f32[8,128]{1,0:T(8,128)S(1)} %add.9), channel_id=1, source_target_pairs={{0,2},{1,3},{2,0},{3,1},{4,6},{5,7},{6,4},{7,5},{8,10},{9,11},{10,... | collective-permute-start | bytes 12296 | tf_op jit(solution)/shard_map/ppermute | solution.py:862
  65.8 2.2 %collective-permute-done.6 = f32[8,128]{1,0:T(8,128)S(1)} collective-permute-done((f32[8,128]{1,0:T(8,128)S(1)}, f32[8,128]{1,0:T(8,128)S(1)}, u32[]{:S(2)}, u32[]{:S(2)}) %collective-permute-start.6) | collective-permute-done | bytes 4128 | tf_op jit(solution)/shard_map/ppermute | solution.py:862
  68.0 1.5 %collective-permute-start.7 = (f32[8,128]{1,0:T(8,128)S(1)}, f32[8,128]{1,0:T(8,128)S(1)}, u32[]{:S(2)}, u32[]{:S(2)}) collective-permute-start(f32[8,128]{1,0:T(8,128)S(1)} %add.10), channel_id=1, source_target_pairs={{0,4},{1,5},{2,6},{3,7},{4,0},{5,1},{6,2},{7,3},{8,12},{9,13},{10,... | collective-permute-start | bytes 12296 | tf_op jit(solution)/shard_map/ppermute | solution.py:862
  69.5 2.1 %collective-permute-done.7 = f32[8,128]{1,0:T(8,128)S(1)} collective-permute-done((f32[8,128]{1,0:T(8,128)S(1)}, f32[8,128]{1,0:T(8,128)S(1)}, u32[]{:S(2)}, u32[]{:S(2)}) %collective-permute-start.7) | collective-permute-done | bytes 4128 | tf_op jit(solution)/shard_map/ppermute | solution.py:862
  72.2 2.7 %collective-permute-start.10 = (f32[8,128]{1,0:T(8,128)}, f32[8,128]{1,0:T(8,128)}, u32[]{:S(2)}, u32[]{:S(2)}) collective-permute-start(f32[8,128]{1,0:T(8,128)} %add.11.refs_1_.refs_5_), channel_id=1, source_target_pairs={{0,24},{8,16},{16,8},{24,0},{1,25},{9,17},{17,9},{25,1},{2,26},{10... | collective-permute-start | bytes 12296 | tf_op jit(solution)/shard_map/ppermute | solution.py:862
  74.9 1.7 %collective-permute-start.9 = (f32[8,128]{1,0:T(8,128)}, f32[8,128]{1,0:T(8,128)}, u32[]{:S(2)}, u32[]{:S(2)}) collective-permute-start(f32[8,128]{1,0:T(8,128)} %add.11.refs_1_.refs_5_), channel_id=1, source_target_pairs={{0,16},{8,24},{16,0},{24,8},{1,17},{9,25},{17,1},{25,9},{2,18},{10... | collective-permute-start | bytes 12296 | tf_op jit(solution)/shard_map/ppermute | solution.py:862
  76.6 7.4 %sweep.8.refs_0_.refs_12_ = f32[2,64,8,512]{3,2,1,0:T(8,128)} custom-call(f32[8,128]{1,0:T(8,128)} %local_heads.1.refs_0_, f32[2,64,512]{2,1,0:T(8,128)} %get-tuple-element.28.refs_2_.refs_1_, f32[72,8,512]{2,1,0:T(8,128)} %get-tuple-element.25.refs_2_.refs_4_.refs_5_.refs_1_.refs_9_, f32[72,8,512]{2,1,0:T(8,128)} %get-tuple-element.26.refs_3_.refs_5_.refs_6_.refs_2_, ...), custom_call_target="tpu_custom_call" | custom-call | bytes 39000000 | tf_op jit(solution)/shard_map/sweep/pallas_call | solution.py:494
  84.0 7.8 %sweep.9 = (f32[64,8,512]{2,1,0:T(8,128)}, f32[64,8,512]{2,1,0:T(8,128)}) custom-call(f32[2,64,8,512]{3,2,1,0:T(8,128)} %sweep.8.refs_0_.refs_12_, f32[8,128]{1,0:T(8,128)} %add.11.refs_1_.refs_5_, f32[8,128]{1,0:T(8,128)} %collective-permute-done.8.refs_2_.refs_6_, f32[8,128]{1,0:T(8,128)} %collective-permute-done.9.refs_3_.refs_7_, ...), custom_call_target="tpu_custom_call" | custom-call | bytes 39000000 | tf_op jit(solution)/shard_map/sweep/pallas_call | solution.py:494
  93.3 1.6 %collective-permute-start.14 = (f32[64,8,512]{2,1,0:T(8,128)}, f32[64,8,512]{2,1,0:T(8,128)}, u32[]{:S(2)}, u32[]{:S(2)}) collective-permute-start(f32[64,8,512]{2,1,0:T(8,128)} %get-tuple-element.43.refs_5_), channel_id=1, source_target_pairs={{8,16},{16,8},{9,17},{17,9},{10,18},{18,10},{11,19},{19,11},{12,20... | collective-permute-start | bytes 3145736 | tf_op jit(solution)/shard_map/ppermute | solution.py:871
  95.6 7.4 %sweep.10.refs_0_.refs_8_ = f32[2,64,8,512]{3,2,1,0:T(8,128)} custom-call(f32[64,8,512]{2,1,0:T(8,128)} %get-tuple-element.42.refs_0_.refs_4_, f32[2,64,512]{2,1,0:T(8,128)} %get-tuple-element.28.refs_2_.refs_1_, f32[72,8,512]{2,1,0:T(8,128)} %get-tuple-element.25.refs_2_.refs_4_.refs_5_.refs_1_.refs_9_, ...), custom_call_target="tpu_custom_call" | custom-call | bytes 39000000 | tf_op jit(solution)/shard_map/sweep/pallas_call | solution.py:494
  104.3 10.9 %update.1.refs_0_ = f32[8,2,64,512]{3,2,1,0:T(8,128)} custom-call(f32[2,64,8,512]{3,2,1,0:T(8,128)} %sweep.10.refs_0_.refs_8_, f32[1,32]{1,0:T(1,128)} %bitcast.4, f32[1,32]{1,0:T(1,128)} %bitcast.5, f32[1]{0:T(128)S(6)} %copy.12.refs_3_, f32[8,32]{1,0:T(8,128)} %refs_4_.3, f32[8,128]{1,0:T(8,128)} %add.11.refs_1_.refs_5_, ...), custom_call_target="tpu_custom_call" | custom-call | bytes 12000000 | tf_op jit(solution)/shard_map/update/pallas_call | solution.py:844
  115.2 8.3 %sweep.11 = f32[8,2,64,512]{3,2,1,0:T(8,128)} custom-call(f32[8,2,64,512]{3,2,1,0:T(8,128)} %update.1.refs_0_, f32[72,8,512]{2,1,0:T(8,128)} %get-tuple-element.25.refs_2_.refs_4_.refs_5_.refs_1_.refs_9_, f32[72,8,512]{2,1,0:T(8,128)} %get-tuple-element.26.refs_3_.refs_5_.refs_6_.refs_2_, f32[72,8,512]{2,1,0:T(8,128)} %collective-permute-done.refs_6_.refs_7_.refs_3_, ...), custom_call_target="tpu_custom_call" | custom-call | bytes 39000000 | tf_op jit(solution)/shard_map/sweep/pallas_call | solution.py:494
  (22 shorter events, 5.5 us)
Async XLA Ops:
  7.2 97.2 %all-gather.3.cloned.1.call-start = ((), (), s32[]{:S(2)}) async-start(), calls=%async_computation | async-start | bytes 18874368 | tf_op jit(solution)/shard_map/all_gather | solution.py:906
  11.5 30.0 %collective-permute-start = (f32[72,8,512]{2,1,0:T(8,128)}, f32[72,8,512]{2,1,0:T(8,128)}, u32[]{:S(2)}, u32[]{:S(2)}) collective-permute-start(f32[72,8,512]{2,1,0:T(8,128)} %get-tuple-element.25.refs_2_.refs_4_.refs_5_.refs_1_.refs_9_), channel_id=1, source_target_pairs={{0,8},{16,24},{8,0},{24,16},{1,9},{17,25},{9,1},{25,17},{2,10},{18... | collective-permute-start | bytes 3538952 | tf_op jit(solution)/shard_map/ppermute | solution.py:871
  14.6 26.9 %collective-permute-start.1 = (f32[72,8,512]{2,1,0:T(8,128)}, f32[72,8,512]{2,1,0:T(8,128)}, u32[]{:S(2)}, u32[]{:S(2)}) collective-permute-start(f32[72,8,512]{2,1,0:T(8,128)} %get-tuple-element.26.refs_3_.refs_5_.refs_6_.refs_2_), channel_id=1, source_target_pairs={{8,16},{16,8},{9,17},{17,9},{10,18},{18,10},{11,19},{19,11},{12,20... | collective-permute-start | bytes 3538952 | tf_op jit(solution)/shard_map/ppermute | solution.py:871
  22.8 27.4 %collective-permute-start.2 = (f32[2,7,8,128]{3,2,1,0:T(8,128)}, f32[2,7,8,128]{3,2,1,0:T(8,128)}, u32[]{:S(2)}, u32[]{:S(2)}) collective-permute-start(f32[2,7,8,128]{3,2,1,0:T(8,128)} %get-tuple-element.32), channel_id=1, source_target_pairs={{0,8},{8,0},{16,24},{24,16},{1,9},{9,1},{17,25},{25,17},{2,10},{10... | collective-permute-start | bytes 172040 | tf_op jit(solution)/shard_map/ppermute | solution.py:862
  26.2 24.0 %collective-permute-start.3 = (f32[2,7,8,128]{3,2,1,0:T(8,128)}, f32[2,7,8,128]{3,2,1,0:T(8,128)}, u32[]{:S(2)}, u32[]{:S(2)}) collective-permute-start(f32[2,7,8,128]{3,2,1,0:T(8,128)} %get-tuple-element.33), channel_id=1, source_target_pairs={{0,16},{8,24},{16,0},{24,8},{1,17},{9,25},{17,1},{25,9},{2,18},{10... | collective-permute-start | bytes 172040 | tf_op jit(solution)/shard_map/ppermute | solution.py:862
  26.2 24.0 %collective-permute-start.4 = (f32[2,7,8,128]{3,2,1,0:T(8,128)}, f32[2,7,8,128]{3,2,1,0:T(8,128)}, u32[]{:S(2)}, u32[]{:S(2)}) collective-permute-start(f32[2,7,8,128]{3,2,1,0:T(8,128)} %get-tuple-element.34), channel_id=1, source_target_pairs={{0,24},{8,16},{16,8},{24,0},{1,25},{9,17},{17,9},{25,1},{2,26},{10... | collective-permute-start | bytes 172040 | tf_op jit(solution)/shard_map/ppermute | solution.py:862
  50.2 33.8 %collective-permute-start.11 = (f32[64,8,512]{2,1,0:T(8,128)}, f32[64,8,512]{2,1,0:T(8,128)}, u32[]{:S(2)}, u32[]{:S(2)}) collective-permute-start(f32[64,8,512]{2,1,0:T(8,128)} %get-tuple-element.40.refs_0_.refs_4_), channel_id=1, source_target_pairs={{0,8},{16,24},{8,0},{24,16},{1,9},{17,25},{9,1},{25,17},{2,10},{18... | collective-permute-start | bytes 3145736 | tf_op jit(solution)/shard_map/ppermute | solution.py:871
  58.0 26.0 %collective-permute-start.12 = (f32[64,8,512]{2,1,0:T(8,128)}, f32[64,8,512]{2,1,0:T(8,128)}, u32[]{:S(2)}, u32[]{:S(2)}) collective-permute-start(f32[64,8,512]{2,1,0:T(8,128)} %get-tuple-element.41.refs_5_), channel_id=1, source_target_pairs={{8,16},{16,8},{9,17},{17,9},{10,18},{18,10},{11,19},{19,11},{12,20... | collective-permute-start | bytes 3145736 | tf_op jit(solution)/shard_map/ppermute | solution.py:871
  62.2 1.4 %collective-permute-start.5 = (f32[8,128]{1,0:T(8,128)}, f32[8,128]{1,0:T(8,128)S(1)}, u32[]{:S(2)}, u32[]{:S(2)}) collective-permute-start(f32[8,128]{1,0:T(8,128)} %local_heads.1.refs_0_), channel_id=1, source_target_pairs={{0,1},{1,0},{2,3},{3,2},{4,5},{5,4},{6,7},{7,6},{8,9},{9,8},{10,11... | collective-permute-start | bytes 12296 | tf_op jit(solution)/shard_map/ppermute | solution.py:862
  64.3 3.7 %collective-permute-start.6 = (f32[8,128]{1,0:T(8,128)S(1)}, f32[8,128]{1,0:T(8,128)S(1)}, u32[]{:S(2)}, u32[]{:S(2)}) collective-permute-start(f32[8,128]{1,0:T(8,128)S(1)} %add.9), channel_id=1, source_target_pairs={{0,2},{1,3},{2,0},{3,1},{4,6},{5,7},{6,4},{7,5},{8,10},{9,11},{10,... | collective-permute-start | bytes 12296 | tf_op jit(solution)/shard_map/ppermute | solution.py:862
  68.0 3.7 %collective-permute-start.7 = (f32[8,128]{1,0:T(8,128)S(1)}, f32[8,128]{1,0:T(8,128)S(1)}, u32[]{:S(2)}, u32[]{:S(2)}) collective-permute-start(f32[8,128]{1,0:T(8,128)S(1)} %add.10), channel_id=1, source_target_pairs={{0,4},{1,5},{2,6},{3,7},{4,0},{5,1},{6,2},{7,3},{8,12},{9,13},{10,... | collective-permute-start | bytes 12296 | tf_op jit(solution)/shard_map/ppermute | solution.py:862
  72.2 11.8 %collective-permute-start.10 = (f32[8,128]{1,0:T(8,128)}, f32[8,128]{1,0:T(8,128)}, u32[]{:S(2)}, u32[]{:S(2)}) collective-permute-start(f32[8,128]{1,0:T(8,128)} %add.11.refs_1_.refs_5_), channel_id=1, source_target_pairs={{0,24},{8,16},{16,8},{24,0},{1,25},{9,17},{17,9},{25,1},{2,26},{10... | collective-permute-start | bytes 12296 | tf_op jit(solution)/shard_map/ppermute | solution.py:862
  74.9 9.1 %collective-permute-start.8 = (f32[8,128]{1,0:T(8,128)}, f32[8,128]{1,0:T(8,128)}, u32[]{:S(2)}, u32[]{:S(2)}) collective-permute-start(f32[8,128]{1,0:T(8,128)} %add.11.refs_1_.refs_5_), channel_id=1, source_target_pairs={{0,8},{8,0},{16,24},{24,16},{1,9},{9,1},{17,25},{25,17},{2,10},{10... | collective-permute-start | bytes 12296 | tf_op jit(solution)/shard_map/ppermute | solution.py:862
  74.9 9.1 %collective-permute-start.9 = (f32[8,128]{1,0:T(8,128)}, f32[8,128]{1,0:T(8,128)}, u32[]{:S(2)}, u32[]{:S(2)}) collective-permute-start(f32[8,128]{1,0:T(8,128)} %add.11.refs_1_.refs_5_), channel_id=1, source_target_pairs={{0,16},{8,24},{16,0},{24,8},{1,17},{9,25},{17,1},{25,9},{2,18},{10... | collective-permute-start | bytes 12296 | tf_op jit(solution)/shard_map/ppermute | solution.py:862
  91.9 23.3 %collective-permute-start.13 = (f32[64,8,512]{2,1,0:T(8,128)}, f32[64,8,512]{2,1,0:T(8,128)}, u32[]{:S(2)}, u32[]{:S(2)}) collective-permute-start(f32[64,8,512]{2,1,0:T(8,128)} %get-tuple-element.42.refs_0_.refs_4_), channel_id=1, source_target_pairs={{0,8},{16,24},{8,0},{24,16},{1,9},{17,25},{9,1},{25,17},{2,10},{18... | collective-permute-start | bytes 3145736 | tf_op jit(solution)/shard_map/ppermute | solution.py:871
  93.3 21.9 %collective-permute-start.14 = (f32[64,8,512]{2,1,0:T(8,128)}, f32[64,8,512]{2,1,0:T(8,128)}, u32[]{:S(2)}, u32[]{:S(2)}) collective-permute-start(f32[64,8,512]{2,1,0:T(8,128)} %get-tuple-element.43.refs_5_), channel_id=1, source_target_pairs={{8,16},{16,8},{9,17},{17,9},{10,18},{18,10},{11,19},{19,11},{12,20... | collective-permute-start | bytes 3145736 | tf_op jit(solution)/shard_map/ppermute | solution.py:871
Sparse Core Ops, SparseCore 0:
  11.6 92.6 all-gather.2
